TPU v7x, 32 devices: a whole 2x2x4 slice. The times are simulated.
32 devices in a mesh: sect: 4 (over x, core), slab: 8 (over z, y).
Axes of the slice: x: 2, y: 2, z: 4, core: 2. Of those that a mesh axis runs over, the one named last changes fastest.
Arguments:
- density: float32 [64, 128, 128], P('slab', 'sect'), may hold values from 0.3 to 3
- velocity: float32 [3, 64, 128, 128], P(None, 'slab', 'sect'), may hold values from -4.8 to 4.8, as said below
- pressure: float32 [64, 128, 128], P('slab', 'sect'), may hold values from 0.3 to 3
- owners: int32 [128, 4, 1], P('sect'), may hold values from 0 to 7; in each aligned block of 128 rows (0 to 127, 128 to 255, ..., all dimensions but the last counted through in order) at most 32 rows name the same one
Outputs:
- new_state: float32 [5, 64, 128, 128], P(None, 'slab', 'sect')
- optical_depth: float32 [4, 8, 32, 64], P('sect', 'slab')
Inputs may be any that keep to these rules, and one draw needn't show every extreme that they name: velocity components are real values within the range. `owners`: among the sightlines of one section (the aligned block of 128 rows) no index is named more than 32 times, a bound that some block reaches.
All inputs are finite; a program needn't handle non-finite values. Where the computation divides by a largest or mean magnitude, that divisor is 1e-20 or more.
Results may differ from a plain program's by a relative error of at most 0.0001.
Values sent between devices are 32-bit elements; how exact they have to be, the bound alone decides.
No kernel may reach another device: no remote copies, remote signals or barrier semaphores. Data moves between devices by JAX's collectives and lax.ppermute only.
A program may use at most 128 MiB of HBM per device.

v0:
```python
import jax
import jax.numpy as jnp
from jax import lax
from jax.sharding import PartitionSpec as P

STRIDE = 32
BAND = 512


GAMMA = 5.0 / 3.0
COURANT = 0.15
TURBULENT = 0.25
NORMALISE = 0.5641895835477563


def extended(block, sides, width):
    for axis, dim in sides:
        count = lax.axis_size(axis)
        forward = [(i, i + 1) for i in range(count - 1)]
        forward.append((count - 1, 0))
        backward = [(target, source) for source, target in forward]
        low = lax.ppermute(
            lax.slice_in_dim(block, block.shape[dim] - width, None, axis=dim), axis, forward
        )
        high = lax.ppermute(lax.slice_in_dim(block, 0, width, axis=dim), axis, backward)
        block = jnp.concatenate([low, block, high], axis=dim)
    return block


def primitives(current):
    density = current[0]
    velocity = current[1:4] / density
    pressure = (GAMMA - 1.0) * (current[4] - 0.5 * jnp.sum(current[1:4] * velocity, axis=0))
    return (density, velocity, pressure)


def conserved(density, velocity, pressure):
    momentum = density[None] * velocity
    energy = pressure / (GAMMA - 1.0) + 0.5 * jnp.sum(momentum * velocity, axis=0)
    return jnp.concatenate([density[None], momentum, energy[None]], axis=0)


def physical_flux(current, velocity, pressure, axis_dim):
    moving = velocity[axis_dim]
    pieces = [current[axis_dim + 1]]
    for component in range(3):
        summand = current[component + 1] * moving
        if component == axis_dim:
            summand = summand + pressure
        pieces.append(summand)
    pieces.append((current[4] + pressure) * moving)
    return jnp.stack(pieces, axis=0)


def face_flux(left_state, right_state, axis_dim):
    left_density, left_velocity, left_pressure = primitives(left_state)
    right_density, right_velocity, right_pressure = primitives(right_state)
    left_speed = jnp.abs(left_velocity[axis_dim]) + jnp.sqrt(GAMMA * left_pressure / left_density)
    right_speed = jnp.abs(right_velocity[axis_dim]) + jnp.sqrt(
        GAMMA * right_pressure / right_density
    )
    signal_speed = jnp.maximum(left_speed, right_speed)
    average = 0.5 * (
        physical_flux(left_state, left_velocity, left_pressure, axis_dim)
        + physical_flux(right_state, right_velocity, right_pressure, axis_dim)
    )
    return average - 0.5 * signal_speed[None] * (right_state - left_state)


def line_inputs(current):
    density, velocity, pressure = primitives(current)
    broadening = TURBULENT + pressure / density
    return jnp.stack([density, broadening, velocity[0]], axis=0)


def line_params(fields):
    width = BAND / 64.0 * jnp.sqrt(fields[1])
    amplitude = NORMALISE * jnp.square(fields[0]) * jnp.power(fields[1], -0.7) / width
    return jnp.stack([amplitude, 1.0 / width, BAND / 8.0 * fields[2]], axis=0)


def skewer_depth(params):
    length = params.shape[2]
    half_band = BAND // 2
    offsets = (jnp.arange(BAND, dtype=jnp.int32) - half_band).astype(jnp.float32)[:, None]
    repeats = (length + BAND) // length + 2
    first_col = -half_band % length

    def one_line(line_parts):
        amplitude, inverse, line_shift = line_parts
        summands = amplitude[None, :] * jnp.exp(
            -jnp.square((offsets - line_shift[None, :]) * inverse[None, :])
        )
        tiled = jnp.tile(summands, (1, repeats))[:, first_col : first_col + length + BAND]
        flattened = tiled.reshape(-1)[BAND : BAND + BAND * (length + BAND - 1)]
        return jnp.sum(flattened.reshape(BAND, length + BAND - 1)[:, :length], axis=0)

    return lax.map(one_line, (params[0], params[1], params[2]))


def depth_lines(arrived):
    return skewer_depth(arrived)


def body(density, velocity, pressure, owners):
    current = conserved(density, velocity, pressure)
    sound_speed = jnp.sqrt(GAMMA * pressure / density)
    fastest = lax.pmax(jnp.max(jnp.abs(velocity) + sound_speed[None]), ("sect", "slab"))
    time_step = COURANT / fastest
    padded = extended(current, (("sect", 2), ("slab", 1)), 1)
    inner_rows = padded[:, :, 1:-1, :]
    first_flux = face_flux(inner_rows[:, :-1], inner_rows[:, 1:], 0)
    change = first_flux[:, 1:] - first_flux[:, :-1]
    middle = padded[:, 1:-1]
    second_flux = face_flux(middle[:, :, :-1], middle[:, :, 1:], 1)
    change = change + (second_flux[:, :, 1:] - second_flux[:, :, :-1])
    third_flux = face_flux(current, jnp.roll(current, -1, axis=3), 2)
    change = change + (third_flux - jnp.roll(third_flux, 1, axis=3))
    new_state = current - time_step * change
    sampled = line_inputs(new_state[:, :, :, ::STRIDE])
    fields = line_params(sampled)
    width_x = fields.shape[1]
    columns = fields.shape[2] * fields.shape[3]
    by_column = jnp.transpose(fields.reshape(3, width_x, columns), (0, 2, 1))
    group_size = lax.axis_size("slab")
    most_slots = 2 * columns // group_size
    owner_flat = owners.reshape(columns)
    choose = (owner_flat[:, None] == jnp.arange(group_size, dtype=jnp.int32)[None, :]).astype(
        jnp.int32
    )
    ranking = jnp.sum((jnp.cumsum(choose, axis=0) - choose) * choose, axis=1)
    per_device = columns // group_size
    arrived = lax.all_to_all(by_column, "slab", split_axis=1, concat_axis=2, tiled=True)
    local_depth = depth_lines(arrived)
    my_index = lax.axis_index("slab")
    block_owner = lax.dynamic_slice_in_dim(owner_flat, my_index * per_device, per_device)
    keep_mask = block_owner[None, :] == jnp.arange(group_size, dtype=jnp.int32)[:, None]
    outgoing = jnp.where(keep_mask[:, :, None], local_depth[None], 0.0).reshape(
        group_size * per_device, local_depth.shape[1]
    )
    returned = lax.all_to_all(outgoing, "slab", split_axis=0, concat_axis=0, tiled=True)
    target = jnp.where(owner_flat == my_index, ranking, most_slots)
    source_rows = jnp.full((most_slots,), columns, jnp.int32)
    source_rows = source_rows.at[target].set(jnp.arange(columns, dtype=jnp.int32), mode="drop")
    padded_back = jnp.concatenate(
        [returned, jnp.zeros((1, returned.shape[1]), jnp.float32)], axis=0
    )
    depth_rows = jnp.take(padded_back, source_rows, axis=0)
    return (new_state, depth_rows.reshape(1, 1, most_slots, depth_rows.shape[1]))


def solution(mesh):
    in_specs = (
        P("slab", "sect", None),
        P(None, "slab", "sect", None),
        P("slab", "sect", None),
        P("sect", None, None),
    )
    out_specs = (P(None, "slab", "sect", None), P("sect", "slab", None, None))
    return jax.shard_map(body, mesh=mesh, in_specs=in_specs, out_specs=out_specs, check_vma=False)
```

profile of v0, /device:TPU:0, one launch (start us, length us, event | category | flops | bytes accessed | tf_op | source)
XLA Modules:
  0.0 226.0 jit_solution(13633930070821447088)
XLA Ops:
  1.7 1.8 multiply_reduce_fusion.5
  4.6 2.4 %collective-permute-start.1 = (f32[5,8,1,128]{3,1,2,0:T(8,128)}, f32[5,8,1,128]{3,1,2,0:T(8,128)}, u32[]{:S(2)}, u32[]{:S(2)}) collective-permute-start(f32[5,8,1,128]{3,1,2,0:T(8,128)} %bitcast.44), channel_id=1, source_target_pairs={{8,0},{16,8},{24,16},{0,24},{9,1},{17,9},{25,17},{1,25},{10,2},{18... | collective-permute-start | bytes 61448 | tf_op jit(solution)/shard_map/ppermute | solution.py:25
  10.7 3.0 %copy.162 = f32[5,8,32,128]{2,1,3,0:T(8,128)} copy(f32[5,8,32,128]{3,2,1,0:T(8,128)} %pad_maximum_fusion.2) | data formatting | bytes 1310720 | tf_op jit(solution)/shard_map/jit(_roll_static)/concatenate | solution.py:117
  13.7 1.6 bitcast_dynamic-update-slice_fusion
  15.4 3.0 %copy.159 = f32[5,8,32,128]{2,1,3,0:T(8,128)} copy(f32[5,8,32,128]{3,2,1,0:T(8,128)} %bitcast_dynamic-update-slice_fusion) | data formatting | bytes 1310720 | tf_op jit(solution)/shard_map/stack | solution.py:52
  19.9 1.7 fusion.39
  22.4 1.7 fusion.53
  25.7 3.0 %copy.160 = f32[5,8,32,128]{2,1,3,0:T(8,128)} copy(f32[5,8,32,128]{3,2,1,0:T(8,128)} %multiply_dynamic-update-slice_fusion.4) | data formatting | bytes 1310720 | tf_op jit(solution)/shard_map/stack | solution.py:52
  31.0 5.4 %multiply_subtract_fusion.1 = f32[5,8,32,128]{2,1,3,0:T(8,128)} fusion(f32[5,8,32,128]{2,1,3,0:T(8,128)} %copy.162, f32[5,8,32,128]{2,1,3,0:T(8,128)S(1)} %copy.164, f32[5,8,32,128]{2,1,3,0:T(8,128)} %copy.159, f32[5,8,32,128]{2,1,3,0:T(8,128)} %copy.160, f32[8,32,128]{1,0,2:T(8,128)S(1)} %copy.161), kind=kLoop, calls=%fused_computation.23 | loop fusion | flops 819200 | bytes 3407872 | tf_op jit(solution)/shard_map/sub | solution.py:67
  36.3 40.3 %pmax.7 = f32[]{:T(128)} all-reduce(f32[]{:T(128)} %get-tuple-element.94), channel_id=1, replica_groups=mesh['sect'=4,'slab'=8] {'sect','slab'}, use_global_device_ids=true, to_apply=%region_2.0 | all-reduce | flops 1 | bytes 8 | tf_op jit(solution)/shard_map/pmax | solution.py:108
  76.6 3.4 %slice.384 = f32[5,8,32,127]{2,1,3,0:T(8,128)} slice(f32[5,8,32,128]{2,1,3,0:T(8,128)} %multiply_subtract_fusion.1), slice={[0:5], [0:8], [0:32], [0:127]} | slice | bytes 1300480 | tf_op jit(solution)/shard_map/jit(_roll_static)/slice | solution.py:118
  80.7 3.0 %copy.158 = f32[5,8,1,128]{2,1,3,0:T(8,128)} copy(f32[5,8,1,128]{3,1,2,0:T(8,128)} %collective-permute-done.1) | data formatting | bytes 40960 | tf_op jit(solution)/shard_map/ppermute | solution.py:25
  83.7 3.0 %copy.155 = f32[5,8,1,128]{2,1,3,0:T(8,128)} copy(f32[5,8,1,128]{3,1,2,0:T(8,128)} %collective-permute-done) | data formatting | bytes 40960 | tf_op jit(solution)/shard_map/ppermute | solution.py:22
  86.7 2.3 %constant_dynamic-update-slice_fusion.1 = (f32[5,8,33,128]{2,1,3,0:T(8,128)S(1)}, f32[8,33,128]{1,0,2:T(8,128)S(1)}, f32[5,8,33,128]{2,1,3,0:T(8,128)S(1)}, f32[8,33,128]{1,0,2:T(8,128)S(1)}) fusion(f32[5,8,1,128]{2,1,3,0:T(8,128)} %copy.158, f32[5,8,32,128]{2,1,3,0:T(8,128)S(1)} %copy.164, f32[5,8,1,128]{2,1,3,0:T(8,128)} %copy.155), kind=kLoop, calls=%fused_computation.172 | loop fusion | flops 135166 | bytes 2793472
  89.9 1.9 multiply_reduce_fusion
  94.7 2.5 %collective-permute-start.2 = (f32[5,1,34,128]{3,2,1,0:T(8,128)S(1)}, f32[5,1,34,128]{3,2,1,0:T(8,128)S(1)}, u32[]{:S(2)}, u32[]{:S(2)}) collective-permute-start(f32[5,1,34,128]{3,2,1,0:T(8,128)S(1)} %get-tuple-element.143), channel_id=1, source_target_pairs={{0,1},{1,2},{2,3},{3,4},{4,5},{5,6},{6,7},{7,0},{8,9},{9,10},{10,1... | collective-permute-start | bytes 261128 | tf_op jit(solution)/shard_map/ppermute | solution.py:22
  97.3 2.3 collective-permute-start.3
  100.6 1.5 copy-done.13
  102.1 5.0 %fusion.10 = f32[5,8,33,128]{2,1,3,0:T(8,128)} fusion(f32[5,8,33,128]{2,1,3,0:T(8,128)S(1)} %get-tuple-element.120, f32[5,8,33,128]{2,1,3,0:T(8,128)} %copy-done.13, f32[5,8,32,128]{2,1,3,0:T(8,128)S(1)} %copy.164, f32[5,8,1,128]{2,1,3,0:T(8,128)S(1)} %copy-done.1, f32[5,8,1,128]{2,1,3,0:T(8,128)S(1)} %copy-done, f32[8,33,128]{1,0,2:T(8,128)S(1)} %get-tuple-element.119), kind=kLoop, calls=%fused_computation.21 | loop fusion | flops 1182720 | bytes 2859008 | tf_op jit(solution)/shard_map/sub | solution.py:67
  111.9 4.7 %copy.153 = f32[5,9,32,128]{2,1,3,0:T(8,128)} copy(f32[5,9,32,128]{3,2,1,0:T(8,128)} %slice.332) | data formatting | bytes 1474560 | tf_op jit(solution)/shard_map/slice | solution.py:112
  116.6 4.7 %copy.154 = f32[5,9,32,128]{2,1,3,0:T(8,128)} copy(f32[5,9,32,128]{3,2,1,0:T(8,128)} %slice.333) | data formatting | bytes 1474560 | tf_op jit(solution)/shard_map/slice | solution.py:112
  126.8 4.8 %copy.150 = f32[5,9,32,128]{2,1,3,0:T(8,128)} copy(f32[5,9,32,128]{3,2,1,0:T(8,128)} %get-tuple-element.133) | data formatting | bytes 1474560 | tf_op jit(solution)/shard_map/stack | solution.py:52
  131.7 3.9 %copy.151 = f32[5,9,32,128]{2,1,3,0:T(8,128)} copy(f32[5,9,32,128]{3,2,1,0:T(8,128)S(1)} %copy-done.20) | data formatting | bytes 1474560 | tf_op jit(solution)/shard_map/stack | solution.py:52
  137.0 11.0 %multiply_subtract_fusion = f32[5,9,32,128]{2,1,3,0:T(8,128)} fusion(f32[5,9,32,128]{2,1,3,0:T(8,128)} %copy.153, f32[5,9,32,128]{2,1,3,0:T(8,128)} %copy.154, f32[5,9,32,128]{2,1,3,0:T(8,128)} %copy.150, f32[5,9,32,128]{2,1,3,0:T(8,128)} %copy.151, f32[9,32,128]{1,0,2:T(8,128)} %copy.152), kind=kLoop, calls=%fused_computation.12 | loop fusion | flops 921600 | bytes 3833856 | tf_op jit(solution)/shard_map/sub | solution.py:67
  148.0 7.1 %fusion.8 = f32[5,8,32,128]{2,1,3,0:T(8,128)S(1)} fusion(f32[5,8,32,128]{2,1,3,0:T(8,128)S(1)} %copy.164, f32[5,8,33,128]{2,1,3,0:T(8,128)} %fusion.10, f32[5,9,32,128]{2,1,3,0:T(8,128)} %multiply_subtract_fusion, f32[5,8,32,128]{2,1,3,0:T(8,128)} %multiply_subtract_fusion.1, f32[5,8,32,127]{2,1,3,0:T(8,128)} %slice.384, f32[5,8,32,1]{2,1,3,0:T(8,128)S(1)} %slice-done, ...), kind=kLoop, calls=%fused_computation.17 | loop fusion | flops 1310720 | bytes 5242884 | tf_op jit(solution)/shard_map/sub | solution.py:119
  155.1 1.5 copy-done.8
  158.0 3.6 %all-to-all-start = ((f32[8,1,384]{2,1,0:T(1,128)}), f32[8,1,384]{2,1,0:T(1,128)S(1)}, u32[]{:S(2)}, u32[]{:S(2)}) async-start(f32[8,1,384]{2,1,0:T(1,128)} %reshape.278), calls=%async_computation | async-start | bytes 24576 | tf_op jit(solution)/shard_map/all_to_all | solution.py:133
  161.5 6.2 %all-to-all-done = f32[8,1,384]{2,1,0:T(1,128)S(1)} async-done(((f32[8,1,384]{2,1,0:T(1,128)}), f32[8,1,384]{2,1,0:T(1,128)S(1)}, u32[]{:S(2)}, u32[]{:S(2)}) %all-to-all-start) | async-done | bytes 12320 | tf_op jit(solution)/shard_map/all_to_all | solution.py:133
  169.5 43.7 %while.11 = (s32[]{:T(128)}, f32[16,64]{1,0:T(8,128)S(1)}, f32[16,64]{1,0:T(8,128)S(1)}, f32[16,64]{1,0:T(8,128)S(1)}, f32[16,64]{1,0:T(8,128)S(1)}, /*index=5*/s32[]{:T(128)}, s32[]{:T(128)}) while((s32[]{:T(128)}, f32[16,64]{1,0:T(8,128)S(1)}, f32[16,64]{1,0:T(8,128)S(1)}, f32[16,64]{1,0:T(8,128)S(1)}, ...), condition=%wide.region_15.16_spmd.clone, body=%wide.region_13.15_spmd.clone.sunk | while | flops 197570 | bytes 13630561 | solution.py:98
  214.0 3.3 %all-to-all-start.1 = ((f32[8,1,1024]{2,1,0:T(1,128)}), f32[8,1,1024]{2,1,0:T(1,128)S(1)}, u32[]{:S(2)}, u32[]{:S(2)}) async-start(f32[8,1,1024]{2,1,0:T(1,128)} %reshape.280), calls=%async_computation.1 | async-start | bytes 65536 | tf_op jit(solution)/shard_map/all_to_all | solution.py:141
  217.3 3.0 %copy.175 = f32[5,8,32,128]{3,2,1,0:T(8,128)} copy(f32[5,8,32,128]{2,1,3,0:T(8,128)} %copy-done.8) | data formatting | bytes 1310720
  220.3 3.6 %all-to-all-done.1 = f32[8,1,1024]{2,1,0:T(1,128)S(1)} async-done(((f32[8,1,1024]{2,1,0:T(1,128)}), f32[8,1,1024]{2,1,0:T(1,128)S(1)}, u32[]{:S(2)}, u32[]{:S(2)}) %all-to-all-start.1) | async-done | bytes 32800 | tf_op jit(solution)/shard_map/all_to_all | solution.py:141
  (328 shorter events, 76.4 us)
Async XLA Ops:
  0.6 3.1 %copy-start.9 = (f32[8,32,128]{2,1,0:T(8,128)S(1)}, f32[8,32,128]{2,1,0:T(8,128)}, u32[]{:S(2)}) copy-start(f32[8,32,128]{2,1,0:T(8,128)} %param.6) | copy-start | bytes 393220
  0.6 3.0 %copy-start.23 = (f32[8,32,128]{2,1,0:T(8,128)S(1)}, f32[8,32,128]{2,1,0:T(8,128)}, u32[]{:S(2)}) copy-start(f32[8,32,128]{2,1,0:T(8,128)} %param.8) | copy-start | bytes 393220
  3.5 3.5 %copy-start.6 = (f32[3,8,32,128]{3,2,1,0:T(8,128)}, f32[3,8,32,128]{3,2,1,0:T(8,128)S(1)}, u32[]{:S(2)}) copy-start(f32[3,8,32,128]{3,2,1,0:T(8,128)S(1)} %get-tuple-element.147) | copy-start | bytes 1179652
  3.5 3.5 %copy-start.14 = (f32[3,8,32,128]{3,2,1,0:T(8,128)}, f32[3,8,32,128]{3,2,1,0:T(8,128)S(1)}, u32[]{:S(2)}) copy-start(f32[3,8,32,128]{3,2,1,0:T(8,128)S(1)} %get-tuple-element.148) | copy-start | bytes 1179652
  3.5 3.5 %copy-start.15 = (f32[8,32,128]{2,1,0:T(8,128)}, f32[8,32,128]{2,1,0:T(8,128)S(1)}, u32[]{:S(2)}) copy-start(f32[8,32,128]{2,1,0:T(8,128)S(1)} %get-tuple-element.92) | copy-start | bytes 393220
  3.7 3.4 %copy-start.21 = (f32[5,8,32,128]{3,2,1,0:T(8,128)}, f32[5,8,32,128]{3,2,1,0:T(8,128)S(1)}, u32[]{:S(2)}) copy-start(f32[5,8,32,128]{3,2,1,0:T(8,128)S(1)} %get-tuple-element.109) | copy-start | bytes 1966084
  3.7 89.6 %copy-start.11 = (f32[8,32,128]{2,1,0:T(8,128)}, f32[8,32,128]{2,1,0:T(8,128)S(1)}, u32[]{:S(2)}) copy-start(f32[8,32,128]{2,1,0:T(8,128)S(1)} %get-tuple-element.110) | copy-start | bytes 393220
  4.6 76.0 %collective-permute-start.1 = (f32[5,8,1,128]{3,1,2,0:T(8,128)}, f32[5,8,1,128]{3,1,2,0:T(8,128)}, u32[]{:S(2)}, u32[]{:S(2)}) collective-permute-start(f32[5,8,1,128]{3,1,2,0:T(8,128)} %bitcast.44), channel_id=1, source_target_pairs={{8,0},{16,8},{24,16},{0,24},{9,1},{17,9},{25,17},{1,25},{10,2},{18... | collective-permute-start | bytes 61448 | tf_op jit(solution)/shard_map/ppermute | solution.py:25
  7.0 76.7 %collective-permute-start = (f32[5,8,1,128]{3,1,2,0:T(8,128)}, f32[5,8,1,128]{3,1,2,0:T(8,128)}, u32[]{:S(2)}, u32[]{:S(2)}) collective-permute-start(f32[5,8,1,128]{3,1,2,0:T(8,128)} %bitcast.43), channel_id=1, source_target_pairs={{0,8},{8,16},{16,24},{24,0},{1,9},{9,17},{17,25},{25,1},{2,10},{10... | collective-permute-start | bytes 61448 | tf_op jit(solution)/shard_map/ppermute | solution.py:22
  8.8 1.1 copy-start.2
  18.4 3.2 %copy-start.3 = (f32[5,8,32,127]{3,2,1,0:T(8,128)S(1)}, f32[5,8,32,127]{3,2,1,0:T(8,128)}, u32[]{:S(2)}) copy-start(f32[5,8,32,127]{3,2,1,0:T(8,128)} %copy-done.2) | copy-start | bytes 1950724
  18.4 4.0 %copy-start.16 = (f32[8,32,128]{2,1,0:T(8,128)S(1)}, f32[8,32,128]{2,1,0:T(8,128)}, u32[]{:S(2)}) copy-start(f32[8,32,128]{2,1,0:T(8,128)} %copy-done.15) | copy-start | bytes 393220
  18.4 4.0 %copy-start.17 = (f32[8,32,128]{2,1,0:T(8,128)S(1)}, f32[8,32,128]{2,1,0:T(8,128)}, u32[]{:S(2)}) copy-start(f32[8,32,128]{2,1,0:T(8,128)} %get-tuple-element.135) | copy-start | bytes 393220
  24.9 4.1 %copy-start.25 = (s32[32,4,1]{0,2,1:T(1,128)S(1)}, s32[32,4,1]{0,2,1:T(1,128)}, u32[]{:S(2)}) copy-start(s32[32,4,1]{0,2,1:T(1,128)} %param.9) | copy-start | bytes 1540
  25.7 3.0 %copy-start.24 = (f32[8,32,128]{2,1,0:T(8,128)S(1)}, f32[8,32,128]{2,1,0:T(8,128)}, u32[]{:S(2)}) copy-start(f32[8,32,128]{2,1,0:T(8,128)} %fusion.53) | copy-start | bytes 393220
  86.7 2.4 %copy-start = (f32[5,8,1,128]{2,1,3,0:T(8,128)S(1)}, f32[5,8,1,128]{2,1,3,0:T(8,128)}, u32[]{:S(2)}) copy-start(f32[5,8,1,128]{2,1,3,0:T(8,128)} %copy.158) | copy-start | bytes 61444
  86.7 3.2 %copy-start.1 = (f32[5,8,1,128]{2,1,3,0:T(8,128)S(1)}, f32[5,8,1,128]{2,1,3,0:T(8,128)}, u32[]{:S(2)}) copy-start(f32[5,8,1,128]{2,1,3,0:T(8,128)} %copy.155) | copy-start | bytes 61444
  93.0 1.0 copy-start.7
  94.7 12.4 %collective-permute-start.2 = (f32[5,1,34,128]{3,2,1,0:T(8,128)S(1)}, f32[5,1,34,128]{3,2,1,0:T(8,128)S(1)}, u32[]{:S(2)}, u32[]{:S(2)}) collective-permute-start(f32[5,1,34,128]{3,2,1,0:T(8,128)S(1)} %get-tuple-element.143), channel_id=1, source_target_pairs={{0,1},{1,2},{2,3},{3,4},{4,5},{5,6},{6,7},{7,0},{8,9},{9,10},{10,1... | collective-permute-start | bytes 261128 | tf_op jit(solution)/shard_map/ppermute | solution.py:22
  97.3 9.8 %collective-permute-start.3 = (f32[5,1,34,128]{3,2,1,0:T(8,128)S(1)}, f32[5,1,34,128]{3,2,1,0:T(8,128)S(1)}, u32[]{:S(2)}, u32[]{:S(2)}) collective-permute-start(f32[5,1,34,128]{3,2,1,0:T(8,128)S(1)} %get-tuple-element.144), channel_id=1, source_target_pairs={{1,0},{2,1},{3,2},{4,3},{5,4},{6,5},{7,6},{0,7},{9,8},{10,9},{11,1... | collective-permute-start | bytes 261128 | tf_op jit(solution)/shard_map/ppermute | solution.py:25
  100.6 1.5 copy-start.13
  102.1 5.0 %copy-start.10 = (f32[8,32,128]{2,1,0:T(8,128)S(1)}, f32[8,32,128]{2,1,0:T(8,128)}, u32[]{:S(2)}) copy-start(f32[8,32,128]{2,1,0:T(8,128)} %param.6) | copy-start | bytes 393220
  102.1 5.0 %copy-start.12 = (f32[8,32,128]{2,1,0:T(8,128)S(1)}, f32[8,32,128]{2,1,0:T(8,128)}, u32[]{:S(2)}) copy-start(f32[8,32,128]{2,1,0:T(8,128)} %copy-done.11) | copy-start | bytes 393220
  108.1 1.2 copy-start.4
  121.3 3.6 %copy-start.5 = (f32[5,9,34,128]{3,2,1,0:T(8,128)S(1)}, f32[5,9,34,128]{3,2,1,0:T(8,128)}, u32[]{:S(2)}) copy-start(f32[5,9,34,128]{3,2,1,0:T(8,128)} %copy-done.4) | copy-start | bytes 2350084
  121.3 3.6 %copy-start.18 = (f32[5,9,32,128]{3,2,1,0:T(8,128)S(1)}, f32[5,9,32,128]{3,2,1,0:T(8,128)}, u32[]{:S(2)}) copy-start(f32[5,9,32,128]{3,2,1,0:T(8,128)} %get-tuple-element.138) | copy-start | bytes 2211844
  126.8 4.8 %copy-start.20 = (f32[5,9,32,128]{3,2,1,0:T(8,128)S(1)}, f32[5,9,32,128]{3,2,1,0:T(8,128)}, u32[]{:S(2)}) copy-start(f32[5,9,32,128]{3,2,1,0:T(8,128)} %copy-done.19) | copy-start | bytes 2211844
  131.6 3.9 %copy-start.22 = (f32[9,32,128]{2,1,0:T(8,128)S(1)}, f32[9,32,128]{2,1,0:T(8,128)}, u32[]{:S(2)}) copy-start(f32[9,32,128]{2,1,0:T(8,128)} %get-tuple-element.132) | copy-start | bytes 442372
  137.0 11.0 %slice-start = ((f32[5,8,32,128]{2,1,3,0:T(8,128)}), f32[5,8,32,1]{2,1,3,0:T(8,128)S(1)}, s32[]{:S(2)}) async-start(f32[5,8,32,128]{2,1,3,0:T(8,128)} %multiply_subtract_fusion.1), calls=%async_computation.2 | async-start | bytes 40960 | tf_op jit(solution)/shard_map/jit(_roll_static)/slice | solution.py:118
  155.1 1.5 copy-start.8
  158.0 9.8 %all-to-all-start = ((f32[8,1,384]{2,1,0:T(1,128)}), f32[8,1,384]{2,1,0:T(1,128)S(1)}, u32[]{:S(2)}, u32[]{:S(2)}) async-start(f32[8,1,384]{2,1,0:T(1,128)} %reshape.278), calls=%async_computation | async-start | bytes 24576 | tf_op jit(solution)/shard_map/all_to_all | solution.py:133
  214.0 10.0 %all-to-all-start.1 = ((f32[8,1,1024]{2,1,0:T(1,128)}), f32[8,1,1024]{2,1,0:T(1,128)S(1)}, u32[]{:S(2)}, u32[]{:S(2)}) async-start(f32[8,1,1024]{2,1,0:T(1,128)} %reshape.280), calls=%async_computation.1 | async-start | bytes 65536 | tf_op jit(solution)/shard_map/all_to_all | solution.py:141
  (1 other events, 0.9 us)
where the time goes:
time: 227 us; the launch traced here: 226 us
  local copies, waits for them, and re-layouts  97.4 us (43%)
  other arithmetic  61.1 us (27%)
  blocking collectives  40.3 us (18%)
  starting transfers between devices  14.1 us (6%)
  waiting for transfers between devices  9.84 us (4%)
    pmax x1, blocking collectives, body(): lax.pmax(jnp.max(jnp.abs(velocity) + sound_speed[None]), ('sect', 'slab'))  40.3 us
    sub x3, other arithmetic, face_flux(): return average - 0.5 * signal_speed[None] * (right_state - left_state)  21.3 us
    reshape x16, local copies, waits for them, and re-layouts, one_line(): flattened.reshape(BAND, length + BAND - 1)[:, :length]  17.9 us
    another operation x4, local copies, waits for them, and re-layouts, physical_flux(): return jnp.stack(pieces, axis=0)  14.8 us
    slice x4, local copies, waits for them, and re-layouts, body(): first_flux = face_flux(inner_rows[:, :-1], inner_rows[:, 1:], 0)  11.6 us
    unnamed x62, local copies, waits for them, and re-layouts  10.8 us
    unnamed x17, other arithmetic  9.27 us
    reshape x16, local copies, waits for them, and re-layouts, one_line(): flattened = tiled.reshape(-1)[BAND:BAND + BAND * (length + BAND - 1)]  8.85 us
  transfers between devices with their start and end apart: 6, of which 2 were waited for; matrix products, arithmetic and copies ran while one was open for 20% of the time, Pallas kernels for 0%

commit v1 on v0

v1 whole, which is shorter than its diff:
```python
import functools
import math

import jax
import jax.numpy as jnp
from jax import lax
from jax.experimental import pallas as pl
from jax.experimental.pallas import tpu as pltpu
from jax.sharding import PartitionSpec as P

STRIDE = 32
BAND = 512

GAMMA = 5.0 / 3.0
COURANT = 0.15
TURBULENT = 0.25
NORMALISE = 0.5641895835477563

LANES = 128
ROWS = 8
FIELDS = 5

VMEM = pl.BlockSpec(memory_space=pltpu.VMEM)


def call(kernel, out_shapes, name, flops, scratch=()):
    return pl.pallas_call(
        kernel,
        out_shape=[jax.ShapeDtypeStruct(s, jnp.float32) for s in out_shapes],
        out_specs=[VMEM] * len(out_shapes),
        scratch_shapes=list(scratch),
        compiler_params=pltpu.CompilerParams(vmem_limit_bytes=24 * 1024 * 1024),
        cost_estimate=pl.CostEstimate(flops=flops, bytes_accessed=1 << 20, transcendentals=0),
        name=name,
    )


def shift(array, amount, axis):
    size = array.shape[axis]
    amount = amount % size
    return array if amount == 0 else pltpu.roll(array, amount, axis)


def derived(cell):
    r, u, v, w, p = cell
    m = (r * u, r * v, r * w)
    energy = p * (1.0 / (GAMMA - 1.0)) + 0.5 * (m[0] * u + m[1] * v + m[2] * w)
    sound = jnp.sqrt(GAMMA * p / r)
    return (r, *m, energy), sound


def flux_parts(cell, state, sound, d):
    moving = cell[1 + d]
    flux = [state[1 + d]]
    for k in range(3):
        term = state[1 + k] * moving
        flux.append(term + cell[4] if k == d else term)
    flux.append((state[4] + cell[4]) * moving)
    return (*state, *flux, jnp.abs(moving) + sound)


def face(left, right):
    speed = jnp.maximum(left[10], right[10])
    return [
        (left[5 + k] + right[5 + k]) - speed * (right[k] - left[k]) for k in range(FIELDS)
    ]


def fields_of(r_ref, v_ref, p_ref, index):
    total = r_ref.shape[0]
    first = index.start if isinstance(index, pl.Slice) else index
    out = [r_ref[index]]
    for k in range(3):
        if isinstance(index, pl.Slice):
            out.append(v_ref[pl.ds(k * total + first, index.size, index.stride)])
        else:
            out.append(v_ref[k * total + index])
    out.append(p_ref[index])
    return out


def edges_kernel(sizes, r_ref, v_ref, p_ref, x_first, x_last, y_first, y_last, top_ref):
    nx, ny, nz = sizes
    for out, x in ((x_first, 0), (x_last, nx - 1)):
        for f, value in enumerate(fields_of(r_ref, v_ref, p_ref, pl.ds(x * ny, ny))):
            out[f] = value
    for out, y in ((y_first, 0), (y_last, ny - 1)):
        for f, value in enumerate(fields_of(r_ref, v_ref, p_ref, pl.ds(y, nx, ny))):
            out[f] = value
    top = jnp.zeros((ROWS, nz), jnp.float32)
    for row in range(0, nx * ny, ROWS):
        r, u, v, w, p = fields_of(r_ref, v_ref, p_ref, pl.ds(row, ROWS))
        speed = jnp.maximum(jnp.maximum(jnp.abs(u), jnp.abs(v)), jnp.abs(w)) + jnp.sqrt(GAMMA * p / r)
        top = jnp.maximum(top, speed)
    y_first[FIELDS] = top
    y_last[FIELDS] = top
    top_ref[...] = top


def pack_kernel(sizes, geometry, n_far, r_ref, v_ref, p_ref, y_low, y_high, top_ref, owner_ref, *rest):
    nx, ny, nz = sizes
    n_owner, slots, group, width = geometry
    far, (out_ref, spread) = rest[:n_far], rest[n_far:]
    lines = nz // STRIDE
    columns = ny * lines
    step = STRIDE // ROWS
    per_owner = slots // group
    lane = lax.broadcasted_iota(jnp.int32, (nx, nz), 1)
    n_tiles = ny // ROWS
    tiles = []
    for t in range(n_tiles):
        cell = None
        for s in range(ROWS):
            rows = fields_of(r_ref, v_ref, p_ref, pl.ds(t * ROWS + s, nx, ny))
            rows = [shift(a, step * s, 1) for a in rows]
            if cell is None:
                cell = rows
            else:
                mine = (lane - step * s + 1) % STRIDE < 3
                cell = [jnp.where(mine, a, b) for a, b in zip(rows, cell)]
        tiles.append(cell)
    first = lane % STRIDE < step
    last = lane % STRIDE >= step * (ROWS - 1)
    span = step * (ROWS - 1)
    below = [shift(y_low[f], span, 1) for f in range(FIELDS)]
    above = [y_high[f] for f in range(FIELDS)]
    dense = None
    for t in range(n_tiles):
        cell = tiles[t]
        before = tiles[t - 1] if t > 0 else below
        after = tiles[t + 1] if t + 1 < n_tiles else above
        y_minus = [jnp.where(first, shift(b, -span, 1), shift(c, step, 1)) for b, c in zip(before, cell)]
        y_plus = [jnp.where(last, shift(a, span, 1), shift(c, -step, 1)) for a, c in zip(after, cell)]
        z_minus = [shift(c, 1, 1) for c in cell]
        z_plus = [shift(c, -1, 1) for c in cell]
        state, sound = derived(cell)
        total = None
        for d, minus, plus in ((1, y_minus, y_plus), (2, z_minus, z_plus)):
            here = flux_parts(cell, state, sound, d)
            low = flux_parts(minus, *derived(minus), d)
            high = flux_parts(plus, *derived(plus), d)
            change = [a - b for a, b in zip(face(here, high), face(low, here))]
            total = change if total is None else [a + b for a, b in zip(total, change)]
        values = [shift(a, t, 1) for a in [*cell, *total]]
        dense = values if dense is None else [jnp.where(lane % step == t, a, b) for a, b in zip(values, dense)]
    spread[...] = jnp.zeros_like(spread)
    for f, value in enumerate(dense):
        for h in range(group):
            spread[pl.ds(h * width + f * nx * group + h, nx, group), :] = value
    own = jnp.broadcast_to(owner_ref[...], (columns, columns))
    own_t = own.T

    def place(dim):
        at = lax.broadcasted_iota(jnp.int32, (columns, columns), dim)
        return ((at % step) * ROWS + (at // step) % ROWS) * lines + at // STRIDE

    ahead = (own == own_t) & (place(0) < place(1))
    rank = jnp.sum(jnp.where(ahead, 1.0, 0.0), axis=0, keepdims=True)
    target = owner_ref[...] * slots + rank
    row = lax.broadcasted_iota(jnp.int32, (n_owner * per_owner, columns), 0)
    chosen = []
    for h in range(group):
        slot = ((row // per_owner) * slots + h * per_owner + row % per_owner).astype(jnp.float32)
        chosen.append(jnp.where(slot == target, 1.0, 0.0))
    picked = lax.dot_general(
        jnp.concatenate(chosen, axis=1),
        jnp.concatenate([spread[pl.ds(h * width, width), :] for h in range(group)], axis=1),
        (((1,), (1,)), ((), ())),
        precision=lax.Precision.HIGHEST,
        preferred_element_type=jnp.float32,
    )
    top = jnp.maximum(jnp.maximum(top_ref[...], y_low[FIELDS]), y_high[FIELDS])
    for ref in far:
        top = jnp.maximum(top, ref[...])
    top = jnp.max(top, keepdims=True)
    out_lane = lax.broadcasted_iota(jnp.int32, picked.shape, 1)
    out_ref[...] = jnp.where(out_lane < 2 * FIELDS * nx * group, picked, top)


def change_kernel(sizes, r_ref, v_ref, p_ref, x_low, x_high, y_low, y_high, out_ref):
    nx, ny, nz = sizes
    row = lax.broadcasted_iota(jnp.int32, (ny, nz), 0)
    half = 0.5

    def layer(x):
        if x < 0:
            return [x_low[f] for f in range(FIELDS)]
        if x >= nx:
            return [x_high[f] for f in range(FIELDS)]
        return fields_of(r_ref, v_ref, p_ref, pl.ds(x * ny, ny))

    def prepared(x):
        cell = layer(x)
        state, sound = derived(cell)
        return cell, state, sound, flux_parts(cell, state, sound, 0)

    previous = prepared(-1)
    here = prepared(0)
    x_face = face(previous[3], here[3])
    for x in range(nx):
        following = prepared(x + 1)
        cell, state, sound, parts = here
        next_face = face(parts, following[3])
        total = [a - b for a, b in zip(next_face, x_face)]
        x_face = next_face
        low_cell = [y_low[f, pl.ds(x, 1), :] for f in range(FIELDS)]
        high_cell = [y_high[f, pl.ds(x, 1), :] for f in range(FIELDS)]
        low = flux_parts(low_cell, *derived(low_cell), 1)
        high = flux_parts(high_cell, *derived(high_cell), 1)
        parts = flux_parts(cell, state, sound, 1)
        plus = [jnp.where(row == ny - 1, h, shift(a, -1, 0)) for a, h in zip(parts, high)]
        after = face(parts, plus)
        edge = face(low, [a[0:1] for a in parts])
        before = [jnp.where(row == 0, e, shift(a, 1, 0)) for a, e in zip(after, edge)]
        total = [t + (a - b) for t, a, b in zip(total, after, before)]
        parts = flux_parts(cell, state, sound, 2)
        after = face(parts, [shift(a, -1, 1) for a in parts])
        total = [t + (a - shift(a, 1, 1)) for t, a in zip(total, after)]
        for f in range(FIELDS):
            out_ref[f, pl.ds(x * ny, ny), :] = half * total[f]
        here = following


def final_kernel(sizes, geometry, r_ref, v_ref, p_ref, change_ref, packed_ref, new_ref, depth_ref):
    nx, ny, nz = sizes
    n_owner, slots, group, width = geometry
    per_owner = slots // group
    part = nx * group
    length = nx * n_owner
    everything = packed_ref[...]
    lane = lax.broadcasted_iota(jnp.int32, everything.shape, 1)
    fastest = jnp.max(jnp.where(lane >= 2 * FIELDS * part, everything, 0.0), keepdims=True)
    step = COURANT / fastest
    for x in range(nx):
        state, _ = derived(fields_of(r_ref, v_ref, p_ref, pl.ds(x * ny, ny)))
        for f in range(FIELDS):
            new_ref[f, pl.ds(x * ny, ny), :] = state[f] - step * change_ref[f, pl.ds(x * ny, ny), :]
    line = []
    for f in range(2 * FIELDS):
        pieces = [
            packed_ref[pl.ds(q * per_owner, per_owner), pl.ds(f * part, part)] for q in range(n_owner)
        ]
        line.append(jnp.concatenate(pieces, axis=1))
    cell, change = line[:FIELDS], line[FIELDS:]
    taken = cell[0] > 0.0
    cell[0] = jnp.where(taken, cell[0], 1.0)
    state, sound = derived(cell)
    parts = flux_parts(cell, state, sound, 0)
    after = face(parts, [shift(a, -group, 1) for a in parts])
    change = [c + (a - shift(a, group, 1)) for c, a in zip(change, after)]
    new = [s - (0.5 * step) * c for s, c in zip(state, change)]
    density = new[0]
    pressure = (GAMMA - 1.0) * (new[4] - 0.5 * (new[1] * new[1] + new[2] * new[2] + new[3] * new[3]) / density)
    broadening = TURBULENT + pressure / density
    inverse = 1.0 / (BAND / 64.0 * jnp.sqrt(broadening))
    amplitude = NORMALISE * (density * density) * jnp.exp(-0.7 * jnp.log(broadening)) * inverse
    amplitude = jnp.where(taken, amplitude, 0.0)
    scaled = inverse * math.sqrt(math.log2(math.e))
    centre = (BAND / 8.0) * (new[1] / density)
    turns = BAND // length
    strides = [scaled * float(length * m) for m in range(turns)]

    def offset(count, running):
        e = (length - 1 - count).astype(jnp.float32) - float(BAND // 2)
        start = (e - centre) * scaled
        total = None
        for m in range(turns):
            t = start + strides[m] if m else start
            value = jnp.exp2(-(t * t))
            total = value if total is None else total + value
        return shift(running, group, 1) + amplitude * total

    running = lax.fori_loop(0, length, offset, jnp.zeros_like(amplitude), unroll=8)
    running = shift(running, -(BAND // 2) * group, 1)
    if group == 1:
        depth_ref[...] = running
    else:
        at = lax.broadcasted_iota(jnp.int32, (group * length, length), 0)
        cell_of = lax.broadcasted_iota(jnp.int32, (group * length, length), 1)
        for h in range(group):
            pick = jnp.where(at == cell_of * group + h, 1.0, 0.0)
            depth_ref[pl.ds(h * per_owner, per_owner), :] = jnp.dot(
                running, pick, precision=lax.Precision.HIGHEST, preferred_element_type=jnp.float32
            )


def around(value, axis, amount):
    count = lax.axis_size(axis)
    return lax.ppermute(value, axis, [(i, (i + amount) % count) for i in range(count)])


def body(density, velocity, pressure, owners):
    sizes = nx, ny, nz = density.shape
    n_sect, n_slab = lax.axis_size("sect"), lax.axis_size("slab")
    lines = nz // STRIDE
    columns = ny * lines
    slots = 2 * columns // n_slab
    length = nx * n_slab
    group = max(1, LANES // length)
    width = -(-(2 * FIELDS * nx * group + 1) // LANES) * LANES
    geometry = (n_slab, slots, group, width)
    gas = (
        density.reshape(nx * ny, nz),
        velocity.reshape(3 * nx * ny, nz),
        pressure.reshape(nx * ny, nz),
    )
    cells = nx * ny * nz
    x_edge, y_edge = (FIELDS, ny, nz), (FIELDS + 1, nx, nz)
    x_first, x_last, y_first, y_last, top = call(
        functools.partial(edges_kernel, sizes),
        [x_edge, x_edge, y_edge, y_edge, (ROWS, nz)],
        "edges",
        20 * cells,
    )(*gas)
    y_low = around(y_last, "sect", 1)
    y_high = around(y_first, "sect", -1)
    far = [around(top, "sect", d) for d in range(2, n_sect - 1)]
    x_low = around(x_last, "slab", 1)
    x_high = around(x_first, "slab", -1)
    order = jnp.transpose(owners.reshape(ny // ROWS, ROWS, lines), (2, 1, 0))
    owner_row = order.reshape(1, columns).astype(jnp.float32)
    (packed,) = call(
        functools.partial(pack_kernel, sizes, geometry, len(far)),
        [(n_slab * slots // group, width)],
        "pack",
        20 * cells,
        [pltpu.VMEM((group * width, columns), jnp.float32)],
    )(*gas, y_low, y_high, top, owner_row, *far)
    arrived = lax.all_to_all(packed, "slab", split_axis=0, concat_axis=0, tiled=True)
    (change,) = call(
        functools.partial(change_kernel, sizes),
        [(FIELDS, nx * ny, nz)],
        "change",
        300 * cells,
    )(*gas, x_low, x_high, y_low, y_high)
    new_state, depth = call(
        functools.partial(final_kernel, sizes, geometry),
        [(FIELDS, nx * ny, nz), (slots, length)],
        "final",
        100 * cells,
    )(*gas, change, arrived)
    return (new_state.reshape(FIELDS, nx, ny, nz), depth.reshape(1, 1, slots, length))


def solution(mesh):
    in_specs = (
        P("slab", "sect", None),
        P(None, "slab", "sect", None),
        P("slab", "sect", None),
        P("sect", None, None),
    )
    out_specs = (P(None, "slab", "sect", None), P("sect", "slab", None, None))
    return jax.shard_map(body, mesh=mesh, in_specs=in_specs, out_specs=out_specs, check_vma=False)
```

time: 227 us -> 34.1 us (0.15)
  local copies, waits for them, and re-layouts: 97.4 us -> 3.11 us
  other arithmetic: 61.1 us -> 0.02 us
  blocking collectives: 40.3 us -> 0 us
  Pallas kernels: 0 us -> 8.48 us
  waiting for transfers between devices: 9.84 us -> 6.16 us
    pmax x1 -> x0, blocking collectives: 40.3 us -> none  [body(): lax.pmax(jnp.max(jnp.abs(velocity) + sound_speed[None]), ('sect', 'slab'))]
    sub x4 -> x0, other arithmetic: 28.5 us -> none  [the longest x3 21.3 us: face_flux(): return average - 0.5 * signal_speed[None] * (right_state - left_state)]
    reshape x32 -> x0, local copies, waits for them, and re-layouts: 26.7 us -> none  [the longest x16 17.9 us: one_line(): flattened.reshape(BAND, length + BAND - 1)[:, :length]]
    slice x58 -> x0, local copies, waits for them, and re-layouts: 25.1 us -> none  [the longest x4 11.6 us: body(): first_flux = face_flux(inner_rows[:, :-1], inner_rows[:, 1:], 0)]
    another operation x20 -> x0, local copies, waits for them, and re-layouts: 17.4 us -> none  [the longest x4 14.8 us: physical_flux(): return jnp.stack(pieces, axis=0)]
    all_to_all x2 -> x1, waiting for transfers between devices: 9.83 us -> 0.01 us  [body(): lax.all_to_all(packed, 'slab', split_axis=0, concat_axis=0, tiled=True)]
    unnamed x17 -> x0, other arithmetic: 9.27 us -> none
    pallas_call x0 -> x4, Pallas kernels: none -> 8.48 us  [the longest x1 5.63 us: body(): call(functools.partial(final_kernel, sizes, geometry), [(FIELDS, nx * ny,...]
  transfers between devices with their start and end apart: 6 -> 6, of which waited for: 2 -> 2; matrix products, arithmetic and copies ran while one was open for 20% -> 1% of each run, Pallas kernels for 0% -> 3%
where the time goes in v1:
time: 34.1 us; the launch traced here: 33.8 us
  starting transfers between devices  15.3 us (45%)
  Pallas kernels  8.48 us (25%)
  waiting for transfers between devices  6.16 us (18%)
  local copies, waits for them, and re-layouts  3.11 us (9%)
  between operations  0.69 us (2%)
    ppermute x5, starting transfers between devices, around(): lax.ppermute(value, axis, [(i, (i + amount) % count) for i in range(count)])  9.5 us
    ppermute x5, waiting for transfers between devices, around(): lax.ppermute(value, axis, [(i, (i + amount) % count) for i in range(count)])  6.16 us
    all_to_all x1, starting transfers between devices, body(): lax.all_to_all(packed, 'slab', split_axis=0, concat_axis=0, tiled=True)  5.84 us
    pallas_call x1, Pallas kernels, body(): call(functools.partial(final_kernel, sizes, geometry), [(FIELDS, nx * ny,...  5.63 us
    unnamed x14, local copies, waits for them, and re-layouts  2.81 us
    pallas_call x1, Pallas kernels, body(): call(functools.partial(pack_kernel, sizes, geometry, len(far)), [(n_slab...  1.65 us
    pallas_call x1, Pallas kernels, body(): call(functools.partial(change_kernel, sizes), [(FIELDS, nx * ny, nz)], 'c...  1.11 us
  transfers between devices with their start and end apart: 6, of which 2 were waited for; matrix products, arithmetic and copies ran while one was open for 1% of the time, Pallas kernels for 3%

profile of v1, /device:TPU:0, one launch (start us, length us, event | category | flops | bytes accessed | tf_op | source)
XLA Modules:
  0.0 33.8 jit_solution(17481081655319939535)
XLA Ops:
  0.6 0.0 copy-start
  0.6 1.0 %copy-done = f32[3,8,32,128]{3,2,1,0:T(8,128)S(1)} copy-done((f32[3,8,32,128]{3,2,1,0:T(8,128)S(1)}, f32[3,8,32,128]{3,2,1,0:T(8,128)}, u32[]{:S(2)}) %copy-start) | copy-done | bytes 393240
  1.6 0.0 copy-start.2
  1.6 0.9 %copy-done.2 = f32[8,32,128]{2,1,0:T(8,128)S(1)} copy-done((f32[8,32,128]{2,1,0:T(8,128)S(1)}, f32[8,32,128]{2,1,0:T(8,128)}, u32[]{:S(2)}) %copy-start.2) | copy-done | bytes 131096
  2.5 0.0 copy-start.4
  2.5 0.9 %copy-done.4 = f32[8,32,128]{2,1,0:T(8,128)S(1)} copy-done((f32[8,32,128]{2,1,0:T(8,128)S(1)}, f32[8,32,128]{2,1,0:T(8,128)}, u32[]{:S(2)}) %copy-start.4) | copy-done | bytes 131096
  3.4 0.0 copy-start.1
  3.4 0.0 copy-start.3
  3.4 0.1 edges.1
  3.5 0.0 copy-start.6
  3.6 3.0 %collective-permute-start.4 = (f32[8,128]{1,0:T(8,128)S(1)}, f32[8,128]{1,0:T(8,128)S(1)}, u32[]{:S(2)}, u32[]{:S(2)}) collective-permute-start(f32[8,128]{1,0:T(8,128)S(1)} %get-tuple-element.13.top_ref), channel_id=1, source_target_pairs={{0,16},{8,24},{16,0},{24,8},{1,17},{9,25},{17,1},{25,9},{2,18},{10... | collective-permute-start | bytes 12296 | tf_op jit(solution)/shard_map/ppermute | solution.py:289
  6.6 0.0 collective-permute-start.2
  6.6 1.7 %collective-permute-start.3 = (f32[6,8,128]{2,1,0:T(8,128)S(1)}, f32[6,8,128]{2,1,0:T(8,128)S(1)}, u32[]{:S(2)}, u32[]{:S(2)}) collective-permute-start(f32[6,8,128]{2,1,0:T(8,128)S(1)} %get-tuple-element.12), channel_id=1, source_target_pairs={{0,24},{8,0},{16,8},{24,16},{1,25},{9,1},{17,9},{25,17},{2,26},{10... | collective-permute-start | bytes 73736 | tf_op jit(solution)/shard_map/ppermute | solution.py:289
  8.3 0.0 copy-done.6
  8.3 0.1 convert_element_type.10
  8.4 0.1 copy.7
  8.5 0.1 convert_element_type.12.owner_ref
  8.6 0.0 collective-permute-done.4.rest_0_
  8.6 1.2 %collective-permute-done.2.y_low = f32[6,8,128]{2,1,0:T(8,128)S(1)} collective-permute-done((f32[6,8,128]{2,1,0:T(8,128)S(1)}, f32[6,8,128]{2,1,0:T(8,128)S(1)}, u32[]{:S(2)}, u32[]{:S(2)}) %collective-permute-start.2) | collective-permute-done | bytes 24608 | tf_op jit(solution)/shard_map/ppermute | solution.py:289
  9.8 0.0 collective-permute-done.3.y_high
  9.8 0.0 copy-done.1
  9.8 0.0 copy-done.3
  9.8 0.0 copy-done.5
  9.8 1.7 %pack.1 = f32[128,256]{1,0:T(8,128)} custom-call(f32[256,128]{1,0:T(8,128)S(1)} %bitcast.15, f32[768,128]{1,0:T(8,128)S(1)} %bitcast.11, f32[256,128]{1,0:T(8,128)S(1)} %bitcast.19, f32[6,8,128]{2,1,0:T(8,128)S(1)} %collective-permute-done.2.y_low, f32[6,8,128]{2,1,0:T(8,128)S(1)} %collective-permute-done.3.y_high, f32[8,128]{1,0:T(8,128)S(1)} %get-tuple-element.13.top_ref, ...), custom_call_target="tpu_custom_call" | custom-call | flops 655360 | bytes 1048576 | tf_op jit(solution)/shard_map/pack/pallas_call | solution.py:322
  11.5 5.8 %all-to-all-start = ((f32[8,16,256]{2,1,0:T(8,128)}), f32[8,16,256]{2,1,0:T(8,128)S(1)}, u32[]{:S(2)}, u32[]{:S(2)}) async-start(f32[8,16,256]{2,1,0:T(8,128)} %bitcast.4), calls=%async_computation | async-start | bytes 262144 | tf_op jit(solution)/shard_map/all_to_all | solution.py:329
  17.3 2.0 %collective-permute-start = (f32[5,32,128]{2,1,0:T(8,128)S(1)}, f32[5,32,128]{2,1,0:T(8,128)S(1)}, u32[]{:S(2)}, u32[]{:S(2)}) collective-permute-start(f32[5,32,128]{2,1,0:T(8,128)S(1)} %get-tuple-element.9), channel_id=1, source_target_pairs={{0,1},{1,2},{2,3},{3,4},{4,5},{5,6},{6,7},{7,0},{8,9},{9,10},{10,1... | collective-permute-start | bytes 245768 | tf_op jit(solution)/shard_map/ppermute | solution.py:289
  19.4 2.7 %collective-permute-start.1 = (f32[5,32,128]{2,1,0:T(8,128)S(1)}, f32[5,32,128]{2,1,0:T(8,128)S(1)}, u32[]{:S(2)}, u32[]{:S(2)}) collective-permute-start(f32[5,32,128]{2,1,0:T(8,128)S(1)} %get-tuple-element.10), channel_id=1, source_target_pairs={{0,7},{1,0},{2,1},{3,2},{4,3},{5,4},{6,5},{7,6},{8,15},{9,8},{10,9... | collective-permute-start | bytes 245768 | tf_op jit(solution)/shard_map/ppermute | solution.py:289
  22.1 5.0 %collective-permute-done.x_low = f32[5,32,128]{2,1,0:T(8,128)S(1)} collective-permute-done((f32[5,32,128]{2,1,0:T(8,128)S(1)}, f32[5,32,128]{2,1,0:T(8,128)S(1)}, u32[]{:S(2)}, u32[]{:S(2)}) %collective-permute-start) | collective-permute-done | bytes 81952 | tf_op jit(solution)/shard_map/ppermute | solution.py:289
  27.0 0.0 collective-permute-done.1.x_high
  27.0 1.1 %change.1.change_ref = f32[5,256,128]{2,1,0:T(8,128)S(1)} custom-call(f32[256,128]{1,0:T(8,128)S(1)} %bitcast.16, f32[768,128]{1,0:T(8,128)S(1)} %bitcast.12, f32[256,128]{1,0:T(8,128)S(1)} %bitcast.20, f32[5,32,128]{2,1,0:T(8,128)S(1)} %collective-permute-done.x_low, f32[5,32,128]{2,1,0:T(8,128)S(1)} %collective-permute-done.1.x_high, ...), custom_call_target="tpu_custom_call" | custom-call | flops 9830400 | bytes 1048576 | tf_op jit(solution)/shard_map/change/pallas_call | solution.py:330
  28.2 0.0 all-to-all-done
  28.2 5.6 %final.1 = (f32[5,256,128]{2,1,0:T(8,128)}, f32[32,64]{1,0:T(8,128)}) custom-call(f32[256,128]{1,0:T(8,128)S(1)} %bitcast.17, f32[768,128]{1,0:T(8,128)S(1)} %bitcast.13, f32[256,128]{1,0:T(8,128)S(1)} %bitcast.21, f32[5,256,128]{2,1,0:T(8,128)S(1)} %change.1.change_ref, f32[128,256]{1,0:T(8,128)S(1)} %bitcast.22), custom_call_target="tpu_custom_call" | custom-call | flops 3276800 | bytes 1048576 | tf_op jit(solution)/shard_map/final/pallas_call | solution.py:336
  (2 shorter events, 0.0 us)
Async XLA Ops:
  0.6 1.0 %copy-start = (f32[3,8,32,128]{3,2,1,0:T(8,128)S(1)}, f32[3,8,32,128]{3,2,1,0:T(8,128)}, u32[]{:S(2)}) copy-start(f32[3,8,32,128]{3,2,1,0:T(8,128)} %param.5) | copy-start | bytes 1179652
  1.6 0.9 %copy-start.2 = (f32[8,32,128]{2,1,0:T(8,128)S(1)}, f32[8,32,128]{2,1,0:T(8,128)}, u32[]{:S(2)}) copy-start(f32[8,32,128]{2,1,0:T(8,128)} %param.4) | copy-start | bytes 393220
  2.5 0.9 %copy-start.4 = (f32[8,32,128]{2,1,0:T(8,128)S(1)}, f32[8,32,128]{2,1,0:T(8,128)}, u32[]{:S(2)}) copy-start(f32[8,32,128]{2,1,0:T(8,128)} %param.6) | copy-start | bytes 393220
  3.4 6.4 %copy-start.1 = (f32[3,8,32,128]{3,2,1,0:T(8,128)S(1)}, f32[3,8,32,128]{3,2,1,0:T(8,128)}, u32[]{:S(2)}) copy-start(f32[3,8,32,128]{3,2,1,0:T(8,128)} %param.5) | copy-start | bytes 1179652
  3.4 6.4 %copy-start.3 = (f32[8,32,128]{2,1,0:T(8,128)S(1)}, f32[8,32,128]{2,1,0:T(8,128)}, u32[]{:S(2)}) copy-start(f32[8,32,128]{2,1,0:T(8,128)} %param.4) | copy-start | bytes 393220
  3.4 6.4 %copy-start.5 = (f32[8,32,128]{2,1,0:T(8,128)S(1)}, f32[8,32,128]{2,1,0:T(8,128)}, u32[]{:S(2)}) copy-start(f32[8,32,128]{2,1,0:T(8,128)} %param.6) | copy-start | bytes 393220
  3.5 4.8 %copy-start.6 = (s32[32,4,1]{0,2,1:T(1,128)S(1)}, s32[32,4,1]{0,2,1:T(1,128)}, u32[]{:S(2)}) copy-start(s32[32,4,1]{0,2,1:T(1,128)} %param.7) | copy-start | bytes 1540
  3.6 5.1 %collective-permute-start.4 = (f32[8,128]{1,0:T(8,128)S(1)}, f32[8,128]{1,0:T(8,128)S(1)}, u32[]{:S(2)}, u32[]{:S(2)}) collective-permute-start(f32[8,128]{1,0:T(8,128)S(1)} %get-tuple-element.13.top_ref), channel_id=1, source_target_pairs={{0,16},{8,24},{16,0},{24,8},{1,17},{9,25},{17,1},{25,9},{2,18},{10... | collective-permute-start | bytes 12296 | tf_op jit(solution)/shard_map/ppermute | solution.py:289
  6.6 3.3 %collective-permute-start.2 = (f32[6,8,128]{2,1,0:T(8,128)S(1)}, f32[6,8,128]{2,1,0:T(8,128)S(1)}, u32[]{:S(2)}, u32[]{:S(2)}) collective-permute-start(f32[6,8,128]{2,1,0:T(8,128)S(1)} %get-tuple-element.11), channel_id=1, source_target_pairs={{0,8},{8,16},{16,24},{24,0},{1,9},{9,17},{17,25},{25,1},{2,10},{10... | collective-permute-start | bytes 73736 | tf_op jit(solution)/shard_map/ppermute | solution.py:289
  6.6 3.3 %collective-permute-start.3 = (f32[6,8,128]{2,1,0:T(8,128)S(1)}, f32[6,8,128]{2,1,0:T(8,128)S(1)}, u32[]{:S(2)}, u32[]{:S(2)}) collective-permute-start(f32[6,8,128]{2,1,0:T(8,128)S(1)} %get-tuple-element.12), channel_id=1, source_target_pairs={{0,24},{8,0},{16,8},{24,16},{1,25},{9,1},{17,9},{25,17},{2,26},{10... | collective-permute-start | bytes 73736 | tf_op jit(solution)/shard_map/ppermute | solution.py:289
  11.5 16.7 %all-to-all-start = ((f32[8,16,256]{2,1,0:T(8,128)}), f32[8,16,256]{2,1,0:T(8,128)S(1)}, u32[]{:S(2)}, u32[]{:S(2)}) async-start(f32[8,16,256]{2,1,0:T(8,128)} %bitcast.4), calls=%async_computation | async-start | bytes 262144 | tf_op jit(solution)/shard_map/all_to_all | solution.py:329
  17.3 9.7 %collective-permute-start = (f32[5,32,128]{2,1,0:T(8,128)S(1)}, f32[5,32,128]{2,1,0:T(8,128)S(1)}, u32[]{:S(2)}, u32[]{:S(2)}) collective-permute-start(f32[5,32,128]{2,1,0:T(8,128)S(1)} %get-tuple-element.9), channel_id=1, source_target_pairs={{0,1},{1,2},{2,3},{3,4},{4,5},{5,6},{6,7},{7,0},{8,9},{9,10},{10,1... | collective-permute-start | bytes 245768 | tf_op jit(solution)/shard_map/ppermute | solution.py:289
  19.4 7.7 %collective-permute-start.1 = (f32[5,32,128]{2,1,0:T(8,128)S(1)}, f32[5,32,128]{2,1,0:T(8,128)S(1)}, u32[]{:S(2)}, u32[]{:S(2)}) collective-permute-start(f32[5,32,128]{2,1,0:T(8,128)S(1)} %get-tuple-element.10), channel_id=1, source_target_pairs={{0,7},{1,0},{2,1},{3,2},{4,3},{5,4},{6,5},{7,6},{8,15},{9,8},{10,9... | collective-permute-start | bytes 245768 | tf_op jit(solution)/shard_map/ppermute | solution.py:289

commit v2 on v1

--- a/solution.py
+++ b/solution.py
@@ -19,15 +19,21 @@
 LANES = 128
 ROWS = 8
 FIELDS = 5
+UNROLL = 64
 
 VMEM = pl.BlockSpec(memory_space=pltpu.VMEM)
 
 
-def call(kernel, out_shapes, name, flops, scratch=()):
+HBM = pl.BlockSpec(memory_space=pltpu.HBM)
+
+
+def call(kernel, out_shapes, name, flops, scratch=(), in_specs=None, out_specs=None):
+    more = {} if in_specs is None else {"in_specs": in_specs}
     return pl.pallas_call(
         kernel,
         out_shape=[jax.ShapeDtypeStruct(s, jnp.float32) for s in out_shapes],
-        out_specs=[VMEM] * len(out_shapes),
+        out_specs=out_specs or [VMEM] * len(out_shapes),
+        **more,
         scratch_shapes=list(scratch),
         compiler_params=pltpu.CompilerParams(vmem_limit_bytes=24 * 1024 * 1024),
         cost_estimate=pl.CostEstimate(flops=flops, bytes_accessed=1 << 20, transcendentals=0),
@@ -79,8 +85,16 @@
     return out
 
 
-def edges_kernel(sizes, r_ref, v_ref, p_ref, x_first, x_last, y_first, y_last, top_ref):
+def edges_kernel(sizes, r_hbm, v_hbm, p_hbm, x_first, x_last, y_first, y_last, top_ref, r_ref, v_ref, p_ref, sems):
     nx, ny, nz = sizes
+    loads = [
+        pltpu.make_async_copy(source, target, sems.at[i])
+        for i, (source, target) in enumerate(((r_hbm, r_ref), (v_hbm, v_ref), (p_hbm, p_ref)))
+    ]
+    for load in loads:
+        load.start()
+    for load in loads:
+        load.wait()
     for out, x in ((x_first, 0), (x_last, nx - 1)):
         for f, value in enumerate(fields_of(r_ref, v_ref, p_ref, pl.ds(x * ny, ny))):
             out[f] = value
@@ -221,7 +235,7 @@
         here = following
 
 
-def final_kernel(sizes, geometry, r_ref, v_ref, p_ref, change_ref, packed_ref, new_ref, depth_ref):
+def final_kernel(sizes, geometry, r_ref, v_ref, p_ref, change_ref, packed_ref, new_hbm, depth_ref, new_ref, sem):
     nx, ny, nz = sizes
     n_owner, slots, group, width = geometry
     per_owner = slots // group
@@ -235,6 +249,8 @@
         state, _ = derived(fields_of(r_ref, v_ref, p_ref, pl.ds(x * ny, ny)))
         for f in range(FIELDS):
             new_ref[f, pl.ds(x * ny, ny), :] = state[f] - step * change_ref[f, pl.ds(x * ny, ny), :]
+    writing = pltpu.make_async_copy(new_ref, new_hbm, sem)
+    writing.start()
     line = []
     for f in range(2 * FIELDS):
         pieces = [
@@ -260,17 +276,30 @@
     turns = BAND // length
     strides = [scaled * float(length * m) for m in range(turns)]
 
-    def offset(count, running):
-        e = (length - 1 - count).astype(jnp.float32) - float(BAND // 2)
-        start = (e - centre) * scaled
-        total = None
-        for m in range(turns):
-            t = start + strides[m] if m else start
-            value = jnp.exp2(-(t * t))
-            total = value if total is None else total + value
-        return shift(running, group, 1) + amplitude * total
-
-    running = lax.fori_loop(0, length, offset, jnp.zeros_like(amplitude), unroll=8)
+    block = min(length, UNROLL)
+
+    def offsets(count, running):
+        e = (length - block - block * count) * 1.0 - float(BAND // 2)
+        for b in range(block):
+            start = (e + float(b) - centre) * scaled
+            total = None
+            for m in range(turns):
+                t = start + strides[m] if m else start
+                value = jnp.exp2(-(t * t))
+                total = value if total is None else total + value
+            part = shift(amplitude * total, b * group, 1)
+            block_sum = part if b == 0 else block_sum + part
+        return block_sum if running is None else shift(running, block * group, 1) + block_sum
+
+    if length == block:
+        running = offsets(0, None)
+    else:
+        running = lax.fori_loop(
+            0,
+            length // block,
+            lambda i, c: offsets(i.astype(jnp.float32), c),
+            jnp.zeros_like(amplitude),
+        )
     running = shift(running, -(BAND // 2) * group, 1)
     if group == 1:
         depth_ref[...] = running
@@ -282,6 +311,7 @@
             depth_ref[pl.ds(h * per_owner, per_owner), :] = jnp.dot(
                 running, pick, precision=lax.Precision.HIGHEST, preferred_element_type=jnp.float32
             )
+    writing.wait()
 
 
 def around(value, axis, amount):
@@ -306,12 +336,14 @@
     )
     cells = nx * ny * nz
     x_edge, y_edge = (FIELDS, ny, nz), (FIELDS + 1, nx, nz)
-    x_first, x_last, y_first, y_last, top = call(
+    x_first, x_last, y_first, y_last, top, *gas = call(
         functools.partial(edges_kernel, sizes),
-        [x_edge, x_edge, y_edge, y_edge, (ROWS, nz)],
+        [x_edge, x_edge, y_edge, y_edge, (ROWS, nz), *(a.shape for a in gas)],
         "edges",
         20 * cells,
-    )(*gas)
+        [pltpu.SemaphoreType.DMA((3,))],
+        in_specs=[HBM] * 3,
+    )(*(pltpu.with_memory_space_constraint(a, pltpu.HBM) for a in gas))
     y_low = around(y_last, "sect", 1)
     y_high = around(y_first, "sect", -1)
     far = [around(top, "sect", d) for d in range(2, n_sect - 1)]
@@ -331,13 +363,15 @@
         functools.partial(change_kernel, sizes),
         [(FIELDS, nx * ny, nz)],
         "change",
-        300 * cells,
+        300_000 * cells,
     )(*gas, x_low, x_high, y_low, y_high)
     new_state, depth = call(
         functools.partial(final_kernel, sizes, geometry),
         [(FIELDS, nx * ny, nz), (slots, length)],
         "final",
         100 * cells,
+        [pltpu.VMEM((FIELDS, nx * ny, nz), jnp.float32), pltpu.SemaphoreType.DMA],
+        out_specs=[HBM, VMEM],
     )(*gas, change, arrived)
     return (new_state.reshape(FIELDS, nx, ny, nz), depth.reshape(1, 1, slots, length))
 

time: 34.1 us -> 27 us (0.79)
  local copies, waits for them, and re-layouts: 3.11 us -> 0.3 us
  starting transfers between devices: 15.3 us -> 12.8 us
  Pallas kernels: 8.48 us -> 6.69 us
    ppermute x5, waiting for transfers between devices: 6.16 us -> 0.01 us  [around(): lax.ppermute(value, axis, [(i, (i + amount) % count) for i in range(count)])]
    all_to_all x1, waiting for transfers between devices: 0.01 us -> 6.14 us  [body(): lax.all_to_all(packed, 'slab', split_axis=0, concat_axis=0, tiled=True)]
    pallas_call x1, Pallas kernels: 5.63 us -> 2.7 us  [body(): call(functools.partial(final_kernel, sizes, geometry), [(FIELDS, nx * ny,...]
    unnamed x14 -> x2, local copies, waits for them, and re-layouts: 2.81 us -> 0.01 us
    all_to_all x1, starting transfers between devices: 5.84 us -> 3.37 us  [body(): lax.all_to_all(packed, 'slab', split_axis=0, concat_axis=0, tiled=True)]
    pallas_call x1, Pallas kernels: 0.1 us -> 1.22 us  [body(): call(functools.partial(edges_kernel, sizes), [x_edge, x_edge, y_edge, y_e...]
  transfers between devices with their start and end apart: 6 -> 6, of which waited for: 2 -> 1; matrix products, arithmetic and copies ran while one was open for 1% -> 1% of each run, Pallas kernels for 3% -> 10%
where the time goes in v2:
time: 27 us; the launch traced here: 26.7 us
  starting transfers between devices  12.8 us (47%)
  Pallas kernels  6.69 us (25%)
  waiting for transfers between devices  6.15 us (23%)
  between operations  0.7 us (3%)
  local copies, waits for them, and re-layouts  0.3 us (1%)
    ppermute x5, starting transfers between devices, around(): lax.ppermute(value, axis, [(i, (i + amount) % count) for i in range(count)])  9.47 us
    all_to_all x1, waiting for transfers between devices, body(): lax.all_to_all(packed, 'slab', split_axis=0, concat_axis=0, tiled=True)  6.14 us
    all_to_all x1, starting transfers between devices, body(): lax.all_to_all(packed, 'slab', split_axis=0, concat_axis=0, tiled=True)  3.37 us
    pallas_call x1, Pallas kernels, body(): call(functools.partial(final_kernel, sizes, geometry), [(FIELDS, nx * ny,...  2.7 us
    pallas_call x1, Pallas kernels, body(): call(functools.partial(pack_kernel, sizes, geometry, len(far)), [(n_slab...  1.65 us
    pallas_call x1, Pallas kernels, body(): call(functools.partial(edges_kernel, sizes), [x_edge, x_edge, y_edge, y_e...  1.22 us
    pallas_call x1, Pallas kernels, body(): call(functools.partial(change_kernel, sizes), [(FIELDS, nx * ny, nz)], 'c...  1.11 us
  transfers between devices with their start and end apart: 6, of which 1 were waited for; matrix products, arithmetic and copies ran while one was open for 1% of the time, Pallas kernels for 10%

profile of v2, /device:TPU:0, one launch (start us, length us, event | category | flops | bytes accessed | tf_op | source)
XLA Modules:
  0.0 26.7 jit_solution(13191415338577832119)
XLA Ops:
  0.6 1.2 %edges.1 = (f32[5,32,128]{2,1,0:T(8,128)S(1)}, f32[5,32,128]{2,1,0:T(8,128)S(1)}, f32[6,8,128]{2,1,0:T(8,128)S(1)}, f32[6,8,128]{2,1,0:T(8,128)S(1)}, f32[8,128]...) custom-call(f32[256,128]{1,0:T(8,128)} %bitcast.12, ...), custom_call_target="tpu_custom_call" | custom-call | flops 655360 | bytes 1048576 | tf_op jit(solution)/shard_map/edges/pallas_call | solution.py:339
  1.9 3.0 %collective-permute-start.4 = (f32[8,128]{1,0:T(8,128)S(1)}, f32[8,128]{1,0:T(8,128)S(1)}, u32[]{:S(2)}, u32[]{:S(2)}) collective-permute-start(f32[8,128]{1,0:T(8,128)S(1)} %get-tuple-element.19.top_ref), channel_id=1, source_target_pairs={{0,16},{8,24},{16,0},{24,8},{1,17},{9,25},{17,1},{25,9},{2,18},{10... | collective-permute-start | bytes 12296 | tf_op jit(solution)/shard_map/ppermute | solution.py:319
  4.9 0.0 collective-permute-start.2
  4.9 0.0 copy-start
  4.9 1.7 %collective-permute-start.3 = (f32[6,8,128]{2,1,0:T(8,128)S(1)}, f32[6,8,128]{2,1,0:T(8,128)S(1)}, u32[]{:S(2)}, u32[]{:S(2)}) collective-permute-start(f32[6,8,128]{2,1,0:T(8,128)S(1)} %get-tuple-element.18), channel_id=1, source_target_pairs={{0,24},{8,0},{16,8},{24,16},{1,25},{9,1},{17,9},{25,17},{2,26},{10... | collective-permute-start | bytes 73736 | tf_op jit(solution)/shard_map/ppermute | solution.py:319
  6.6 1.5 %collective-permute-start = (f32[5,32,128]{2,1,0:T(8,128)S(1)}, f32[5,32,128]{2,1,0:T(8,128)S(1)}, u32[]{:S(2)}, u32[]{:S(2)}) collective-permute-start(f32[5,32,128]{2,1,0:T(8,128)S(1)} %get-tuple-element.15), channel_id=1, source_target_pairs={{0,1},{1,2},{2,3},{3,4},{4,5},{5,6},{6,7},{7,0},{8,9},{9,10},{10,1... | collective-permute-start | bytes 245768 | tf_op jit(solution)/shard_map/ppermute | solution.py:319
  8.1 3.2 %collective-permute-start.1 = (f32[5,32,128]{2,1,0:T(8,128)S(1)}, f32[5,32,128]{2,1,0:T(8,128)S(1)}, u32[]{:S(2)}, u32[]{:S(2)}) collective-permute-start(f32[5,32,128]{2,1,0:T(8,128)S(1)} %get-tuple-element.16), channel_id=1, source_target_pairs={{0,7},{1,0},{2,1},{3,2},{4,3},{5,4},{6,5},{7,6},{8,15},{9,8},{10,9... | collective-permute-start | bytes 245768 | tf_op jit(solution)/shard_map/ppermute | solution.py:319
  11.3 0.0 copy-done
  11.4 0.1 convert_element_type.10
  11.4 0.1 copy.7
  11.5 0.1 convert_element_type.12.owner_ref
  11.7 0.0 collective-permute-done.4.rest_0_
  11.7 0.0 collective-permute-done.2.y_low
  11.7 0.0 collective-permute-done.3.y_high
  11.7 1.7 %pack.1 = f32[128,256]{1,0:T(8,128)} custom-call(f32[256,128]{1,0:T(8,128)S(1)} %get-tuple-element.12.r_ref, f32[768,128]{1,0:T(8,128)S(1)} %get-tuple-element.13.v_ref, f32[256,128]{1,0:T(8,128)S(1)} %get-tuple-element.14.p_ref, f32[6,8,128]{2,1,0:T(8,128)S(1)} %collective-permute-done.2.y_low, f32[6,8,128]{2,1,0:T(8,128)S(1)} %collective-permute-done.3.y_high, ...), custom_call_target="tpu_custom_call" | custom-call | flops 655360 | bytes 1048576 | tf_op jit(solution)/shard_map/pack/pallas_call | solution.py:354
  13.3 3.4 %all-to-all-start = ((f32[8,16,256]{2,1,0:T(8,128)}), f32[8,16,256]{2,1,0:T(8,128)S(1)}, u32[]{:S(2)}, u32[]{:S(2)}) async-start(f32[8,16,256]{2,1,0:T(8,128)} %bitcast.4), calls=%async_computation | async-start | bytes 262144 | tf_op jit(solution)/shard_map/all_to_all | solution.py:361
  16.7 0.0 collective-permute-done.x_low
  16.7 0.0 collective-permute-done.1.x_high
  16.7 1.1 %change.1.change_ref = f32[5,256,128]{2,1,0:T(8,128)S(1)} custom-call(f32[256,128]{1,0:T(8,128)S(1)} %get-tuple-element.12.r_ref, f32[768,128]{1,0:T(8,128)S(1)} %get-tuple-element.13.v_ref, f32[256,128]{1,0:T(8,128)S(1)} %get-tuple-element.14.p_ref, f32[5,32,128]{2,1,0:T(8,128)S(1)} %collective-permute-done.x_low, ...), custom_call_target="tpu_custom_call" | custom-call | flops 9830400000 | bytes 1048576 | tf_op jit(solution)/shard_map/change/pallas_call | solution.py:362
  17.9 6.1 %all-to-all-done = f32[8,16,256]{2,1,0:T(8,128)S(1)} async-done(((f32[8,16,256]{2,1,0:T(8,128)}), f32[8,16,256]{2,1,0:T(8,128)S(1)}, u32[]{:S(2)}, u32[]{:S(2)}) %all-to-all-start) | async-done | bytes 131104 | tf_op jit(solution)/shard_map/all_to_all | solution.py:361
  24.0 2.7 %final.1 = (f32[5,256,128]{2,1,0:T(8,128)}, f32[32,64]{1,0:T(8,128)}) custom-call(f32[256,128]{1,0:T(8,128)S(1)} %get-tuple-element.12.r_ref, f32[768,128]{1,0:T(8,128)S(1)} %get-tuple-element.13.v_ref, f32[256,128]{1,0:T(8,128)S(1)} %get-tuple-element.14.p_ref, f32[5,256,128]{2,1,0:T(8,128)S(1)} %change.1.change_ref, f32[128,256]{1,0:T(8,128)S(1)} %bitcast.10), custom_call_target="tpu_custom_call" | custom-call | flops 3276800 | bytes 1048576 | tf_op jit(solution)/shard_map/final/pallas_call | solution.py:368
  (1 shorter events, 0.0 us)
Async XLA Ops:
  1.9 9.8 %collective-permute-start.4 = (f32[8,128]{1,0:T(8,128)S(1)}, f32[8,128]{1,0:T(8,128)S(1)}, u32[]{:S(2)}, u32[]{:S(2)}) collective-permute-start(f32[8,128]{1,0:T(8,128)S(1)} %get-tuple-element.19.top_ref), channel_id=1, source_target_pairs={{0,16},{8,24},{16,0},{24,8},{1,17},{9,25},{17,1},{25,9},{2,18},{10... | collective-permute-start | bytes 12296 | tf_op jit(solution)/shard_map/ppermute | solution.py:319
  4.9 6.8 %collective-permute-start.2 = (f32[6,8,128]{2,1,0:T(8,128)S(1)}, f32[6,8,128]{2,1,0:T(8,128)S(1)}, u32[]{:S(2)}, u32[]{:S(2)}) collective-permute-start(f32[6,8,128]{2,1,0:T(8,128)S(1)} %get-tuple-element.17), channel_id=1, source_target_pairs={{0,8},{8,16},{16,24},{24,0},{1,9},{9,17},{17,25},{25,1},{2,10},{10... | collective-permute-start | bytes 73736 | tf_op jit(solution)/shard_map/ppermute | solution.py:319
  4.9 6.5 %copy-start = (s32[32,4,1]{0,2,1:T(1,128)S(1)}, s32[32,4,1]{0,2,1:T(1,128)}, u32[]{:S(2)}) copy-start(s32[32,4,1]{0,2,1:T(1,128)} %param.7) | copy-start | bytes 1540
  4.9 6.8 %collective-permute-start.3 = (f32[6,8,128]{2,1,0:T(8,128)S(1)}, f32[6,8,128]{2,1,0:T(8,128)S(1)}, u32[]{:S(2)}, u32[]{:S(2)}) collective-permute-start(f32[6,8,128]{2,1,0:T(8,128)S(1)} %get-tuple-element.18), channel_id=1, source_target_pairs={{0,24},{8,0},{16,8},{24,16},{1,25},{9,1},{17,9},{25,17},{2,26},{10... | collective-permute-start | bytes 73736 | tf_op jit(solution)/shard_map/ppermute | solution.py:319
  6.6 10.1 %collective-permute-start = (f32[5,32,128]{2,1,0:T(8,128)S(1)}, f32[5,32,128]{2,1,0:T(8,128)S(1)}, u32[]{:S(2)}, u32[]{:S(2)}) collective-permute-start(f32[5,32,128]{2,1,0:T(8,128)S(1)} %get-tuple-element.15), channel_id=1, source_target_pairs={{0,1},{1,2},{2,3},{3,4},{4,5},{5,6},{6,7},{7,0},{8,9},{9,10},{10,1... | collective-permute-start | bytes 245768 | tf_op jit(solution)/shard_map/ppermute | solution.py:319
  8.1 8.6 %collective-permute-start.1 = (f32[5,32,128]{2,1,0:T(8,128)S(1)}, f32[5,32,128]{2,1,0:T(8,128)S(1)}, u32[]{:S(2)}, u32[]{:S(2)}) collective-permute-start(f32[5,32,128]{2,1,0:T(8,128)S(1)} %get-tuple-element.16), channel_id=1, source_target_pairs={{0,7},{1,0},{2,1},{3,2},{4,3},{5,4},{6,5},{7,6},{8,15},{9,8},{10,9... | collective-permute-start | bytes 245768 | tf_op jit(solution)/shard_map/ppermute | solution.py:319
  13.3 10.7 %all-to-all-start = ((f32[8,16,256]{2,1,0:T(8,128)}), f32[8,16,256]{2,1,0:T(8,128)S(1)}, u32[]{:S(2)}, u32[]{:S(2)}) async-start(f32[8,16,256]{2,1,0:T(8,128)} %bitcast.4), calls=%async_computation | async-start | bytes 262144 | tf_op jit(solution)/shard_map/all_to_all | solution.py:361

commit v3 on v2

--- a/solution.py
+++ b/solution.py
@@ -20,6 +20,7 @@
 ROWS = 8
 FIELDS = 5
 UNROLL = 64
+PACK_COST = 30_000
 
 VMEM = pl.BlockSpec(memory_space=pltpu.VMEM)
 
@@ -31,7 +32,10 @@
     more = {} if in_specs is None else {"in_specs": in_specs}
     return pl.pallas_call(
         kernel,
-        out_shape=[jax.ShapeDtypeStruct(s, jnp.float32) for s in out_shapes],
+        out_shape=[
+            jax.ShapeDtypeStruct(*s) if isinstance(s[0], tuple) else jax.ShapeDtypeStruct(s, jnp.float32)
+            for s in out_shapes
+        ],
         out_specs=out_specs or [VMEM] * len(out_shapes),
         **more,
         scratch_shapes=list(scratch),
@@ -85,47 +89,80 @@
     return out
 
 
-def edges_kernel(sizes, r_hbm, v_hbm, p_hbm, x_first, x_last, y_first, y_last, top_ref, r_ref, v_ref, p_ref, sems):
+def place_of(direct):
+    me = lax.axis_index("slab")
+    return (me // 2 if direct else 0), me % 2
+
+
+def layer_of(r_ref, v_ref, p_ref, at, rows):
+    total = r_ref.shape[0]
+    velocity = [v_ref[pl.ds(pl.multiple_of(k * total + at, ROWS), rows)] for k in range(3)]
+    return [r_ref[pl.ds(at, rows)], *velocity, p_ref[pl.ds(at, rows)]]
+
+
+def is_odd(axis, shape):
+    return jnp.full(shape, lax.axis_index(axis) % 2) == 1
+
+
+def sides(near, far, axis):
+    odd = is_odd(axis, near[0].shape)
+    low = [jnp.where(odd, n, f) for n, f in zip(near, far)]
+    high = [jnp.where(odd, f, n) for n, f in zip(near, far)]
+    return low, high
+
+
+def edges_kernel(
+    sizes, r_hbm, v_hbm, p_hbm, o_hbm, x_near, x_far, y_near, y_far, top_ref, r_ref, v_ref, p_ref, o_ref, sems
+):
     nx, ny, nz = sizes
     loads = [
         pltpu.make_async_copy(source, target, sems.at[i])
-        for i, (source, target) in enumerate(((r_hbm, r_ref), (v_hbm, v_ref), (p_hbm, p_ref)))
+        for i, (source, target) in enumerate(((r_hbm, r_ref), (v_hbm, v_ref), (p_hbm, p_ref), (o_hbm, o_ref)))
     ]
     for load in loads:
         load.start()
     for load in loads:
         load.wait()
-    for out, x in ((x_first, 0), (x_last, nx - 1)):
-        for f, value in enumerate(fields_of(r_ref, v_ref, p_ref, pl.ds(x * ny, ny))):
+    odd = lax.axis_index("slab") % 2
+    for out, end in ((x_near, 1 - odd), (x_far, odd)):
+        at = pl.multiple_of(end * ((nx - 1) * ny), ROWS)
+        for f, value in enumerate(layer_of(r_ref, v_ref, p_ref, at, ny)):
             out[f] = value
-    for out, y in ((y_first, 0), (y_last, ny - 1)):
-        for f, value in enumerate(fields_of(r_ref, v_ref, p_ref, pl.ds(y, nx, ny))):
-            out[f] = value
+    first, last = (fields_of(r_ref, v_ref, p_ref, pl.ds(y, nx, ny)) for y in (0, ny - 1))
+    far, near = sides(last, first, "sect")
+    for f in range(FIELDS):
+        y_near[f] = near[f]
+        y_far[f] = far[f]
     top = jnp.zeros((ROWS, nz), jnp.float32)
     for row in range(0, nx * ny, ROWS):
         r, u, v, w, p = fields_of(r_ref, v_ref, p_ref, pl.ds(row, ROWS))
         speed = jnp.maximum(jnp.maximum(jnp.abs(u), jnp.abs(v)), jnp.abs(w)) + jnp.sqrt(GAMMA * p / r)
         top = jnp.maximum(top, speed)
-    y_first[FIELDS] = top
-    y_last[FIELDS] = top
+    y_near[FIELDS] = top
     top_ref[...] = top
 
 
-def pack_kernel(sizes, geometry, n_far, r_ref, v_ref, p_ref, y_low, y_high, top_ref, owner_ref, *rest):
+def join_kernel(y_far, top_ref, near_ref, out_ref):
+    for f in range(FIELDS):
+        out_ref[f] = y_far[f]
+    out_ref[FIELDS] = jnp.maximum(top_ref[...], near_ref[FIELDS])
+
+
+def pack_kernel(sizes, geometry, n_far, direct, r_ref, v_ref, p_ref, y_near, y_far, top_ref, owner_ref, *rest):
     nx, ny, nz = sizes
     n_owner, slots, group, width = geometry
-    far, (out_ref, spread) = rest[:n_far], rest[n_far:]
+    far, outs, spread = rest[:n_far], rest[n_far:-1], rest[-1]
+    y_low, y_high = sides([y_near[f] for f in range(FIELDS)], [y_far[f] for f in range(FIELDS)], "sect")
     lines = nz // STRIDE
     columns = ny * lines
     step = STRIDE // ROWS
     per_owner = slots // group
     lane = lax.broadcasted_iota(jnp.int32, (nx, nz), 1)
-    n_tiles = ny // ROWS
     tiles = []
-    for t in range(n_tiles):
+    for t in range(step):
         cell = None
-        for s in range(ROWS):
-            rows = fields_of(r_ref, v_ref, p_ref, pl.ds(t * ROWS + s, nx, ny))
+        for s in range(ny // step):
+            rows = fields_of(r_ref, v_ref, p_ref, pl.ds(step * s + t, nx, ny))
             rows = [shift(a, step * s, 1) for a in rows]
             if cell is None:
                 cell = rows
@@ -134,65 +171,80 @@
                 cell = [jnp.where(mine, a, b) for a, b in zip(rows, cell)]
         tiles.append(cell)
     first = lane % STRIDE < step
-    last = lane % STRIDE >= step * (ROWS - 1)
-    span = step * (ROWS - 1)
-    below = [shift(y_low[f], span, 1) for f in range(FIELDS)]
-    above = [y_high[f] for f in range(FIELDS)]
+    last = lane % STRIDE >= ny - step
+    below = [jnp.where(first, y_low[f], shift(a, step, 1)) for f, a in enumerate(tiles[-1])]
+    above = [jnp.where(last, shift(y_high[f], ny - step, 1), shift(a, -step, 1)) for f, a in enumerate(tiles[0])]
+    full = [(cell, *derived(cell)) for cell in (below, *tiles, above)]
+    y_parts = [flux_parts(*c, 1) for c in full]
+    y_faces = [face(a, b) for a, b in zip(y_parts, y_parts[1:])]
     dense = None
-    for t in range(n_tiles):
-        cell = tiles[t]
-        before = tiles[t - 1] if t > 0 else below
-        after = tiles[t + 1] if t + 1 < n_tiles else above
-        y_minus = [jnp.where(first, shift(b, -span, 1), shift(c, step, 1)) for b, c in zip(before, cell)]
-        y_plus = [jnp.where(last, shift(a, span, 1), shift(c, -step, 1)) for a, c in zip(after, cell)]
-        z_minus = [shift(c, 1, 1) for c in cell]
-        z_plus = [shift(c, -1, 1) for c in cell]
-        state, sound = derived(cell)
-        total = None
-        for d, minus, plus in ((1, y_minus, y_plus), (2, z_minus, z_plus)):
-            here = flux_parts(cell, state, sound, d)
-            low = flux_parts(minus, *derived(minus), d)
-            high = flux_parts(plus, *derived(plus), d)
-            change = [a - b for a, b in zip(face(here, high), face(low, here))]
-            total = change if total is None else [a + b for a, b in zip(total, change)]
+    for t in range(step):
+        cell, state, sound = full[t + 1]
+        here = flux_parts(cell, state, sound, 2)
+        after = face(here, [shift(a, -1, 1) for a in here])
+        total = [
+            (high - low) + (a - shift(a, 1, 1))
+            for low, high, a in zip(y_faces[t], y_faces[t + 1], after)
+        ]
         values = [shift(a, t, 1) for a in [*cell, *total]]
         dense = values if dense is None else [jnp.where(lane % step == t, a, b) for a, b in zip(values, dense)]
     spread[...] = jnp.zeros_like(spread)
     for f, value in enumerate(dense):
         for h in range(group):
             spread[pl.ds(h * width + f * nx * group + h, nx, group), :] = value
-    own = jnp.broadcast_to(owner_ref[...], (columns, columns))
+    owner = jnp.concatenate([owner_ref[k] for k in range(lines)], axis=1).astype(jnp.float32)
+    own = jnp.broadcast_to(owner, (columns, columns))
     own_t = own.T
 
     def place(dim):
         at = lax.broadcasted_iota(jnp.int32, (columns, columns), dim)
-        return ((at % step) * ROWS + (at // step) % ROWS) * lines + at // STRIDE
+        return (at % ny) * lines + at // ny
 
     ahead = (own == own_t) & (place(0) < place(1))
     rank = jnp.sum(jnp.where(ahead, 1.0, 0.0), axis=0, keepdims=True)
-    target = owner_ref[...] * slots + rank
+    target = owner * slots + rank
     row = lax.broadcasted_iota(jnp.int32, (n_owner * per_owner, columns), 0)
+    block = row // per_owner
+    z_me, y_me = place_of(direct)
+    own_of = 2 * ((block // 2) ^ z_me) + ((block % 2) ^ y_me)
     chosen = []
     for h in range(group):
-        slot = ((row // per_owner) * slots + h * per_owner + row % per_owner).astype(jnp.float32)
+        slot = (own_of * slots + h * per_owner + row % per_owner).astype(jnp.float32)
         chosen.append(jnp.where(slot == target, 1.0, 0.0))
-    picked = lax.dot_general(
-        jnp.concatenate(chosen, axis=1),
-        jnp.concatenate([spread[pl.ds(h * width, width), :] for h in range(group)], axis=1),
-        (((1,), (1,)), ((), ())),
-        precision=lax.Precision.HIGHEST,
-        preferred_element_type=jnp.float32,
-    )
-    top = jnp.maximum(jnp.maximum(top_ref[...], y_low[FIELDS]), y_high[FIELDS])
+    chosen = jnp.concatenate(chosen, axis=1).astype(jnp.bfloat16)
+    value = jnp.concatenate([spread[pl.ds(h * width, width), :] for h in range(group)], axis=1)
+    picked = None
+    for _ in range(3):
+        piece = value.astype(jnp.bfloat16)
+        value = value - piece.astype(jnp.float32)
+        part = lax.dot_general(chosen, piece, (((1,), (1,)), ((), ())), preferred_element_type=jnp.float32)
+        picked = part if picked is None else picked + part
+    top = jnp.maximum(jnp.maximum(top_ref[...], y_near[FIELDS]), y_far[FIELDS])
     for ref in far:
         top = jnp.maximum(top, ref[...])
     top = jnp.max(top, keepdims=True)
     out_lane = lax.broadcasted_iota(jnp.int32, picked.shape, 1)
-    out_ref[...] = jnp.where(out_lane < 2 * FIELDS * nx * group, picked, top)
-
-
-def change_kernel(sizes, r_ref, v_ref, p_ref, x_low, x_high, y_low, y_high, out_ref):
+    picked = jnp.where(out_lane < 2 * FIELDS * nx * group, picked, top)
+    parts = width // LANES
+    each = n_owner // len(outs)
+    for b in range(n_owner):
+        for w in range(parts):
+            outs[b // each][pl.ds(((b % each) * parts + w) * per_owner, per_owner), :] = picked[
+                b * per_owner : (b + 1) * per_owner, w * LANES : (w + 1) * LANES
+            ]
+
+
+def merge_kernel(rows, firsts, *refs):
+    for first, ref in zip(firsts, refs[:-1]):
+        for d in range(ref.shape[0] // (2 * rows)):
+            refs[-1][pl.ds((first + d) * rows, rows), :] = ref[pl.ds((2 * d + 1) * rows, rows), :]
+
+
+def change_kernel(sizes, r_ref, v_ref, p_ref, x_near, x_far, y_near, y_far, out_ref):
     nx, ny, nz = sizes
+    every = range(FIELDS)
+    x_low, x_high = sides([x_near[f] for f in every], [x_far[f] for f in every], "slab")
+    y_low, y_high = sides([y_near[f] for f in every], [y_far[f] for f in every], "sect")
     row = lax.broadcasted_iota(jnp.int32, (ny, nz), 0)
     half = 0.5
 
@@ -217,8 +269,8 @@
         next_face = face(parts, following[3])
         total = [a - b for a, b in zip(next_face, x_face)]
         x_face = next_face
-        low_cell = [y_low[f, pl.ds(x, 1), :] for f in range(FIELDS)]
-        high_cell = [y_high[f, pl.ds(x, 1), :] for f in range(FIELDS)]
+        low_cell = [y_low[f][x : x + 1] for f in range(FIELDS)]
+        high_cell = [y_high[f][x : x + 1] for f in range(FIELDS)]
         low = flux_parts(low_cell, *derived(low_cell), 1)
         high = flux_parts(high_cell, *derived(high_cell), 1)
         parts = flux_parts(cell, state, sound, 1)
@@ -235,12 +287,33 @@
         here = following
 
 
-def final_kernel(sizes, geometry, r_ref, v_ref, p_ref, change_ref, packed_ref, new_hbm, depth_ref, new_ref, sem):
+def final_kernel(sizes, geometry, firsts, direct, r_ref, v_ref, p_ref, change_ref, got_ref, *rest):
+    blocks, (new_hbm, depth_ref, new_ref, packed_ref, sem) = rest[: len(firsts)], rest[len(firsts) :]
     nx, ny, nz = sizes
     n_owner, slots, group, width = geometry
     per_owner = slots // group
     part = nx * group
     length = nx * n_owner
+    parts = width // LANES
+    rows = parts * per_owner
+
+    z_me, y_me = place_of(direct)
+
+    def settle(source, at, d, odd):
+        owner = 2 * (d ^ z_me) + (odd ^ y_me)
+        for w in range(parts):
+            to = owner * per_owner
+            if per_owner % ROWS == 0:
+                to = pl.multiple_of(to, ROWS)
+            packed_ref[pl.ds(to, per_owner), pl.ds(w * LANES, LANES)] = source[
+                pl.ds(at + w * per_owner, per_owner), :
+            ]
+
+    for first, ref in zip(firsts, blocks):
+        for d in range(ref.shape[0] // (2 * rows)):
+            settle(ref, 2 * d * rows, first + d, 0)
+    for d in range(got_ref.shape[0] // rows):
+        settle(got_ref, d * rows, d, 1)
     everything = packed_ref[...]
     lane = lax.broadcasted_iota(jnp.int32, everything.shape, 1)
     fastest = jnp.max(jnp.where(lane >= 2 * FIELDS * part, everything, 0.0), keepdims=True)
@@ -319,6 +392,15 @@
     return lax.ppermute(value, axis, [(i, (i + amount) % count) for i in range(count)])
 
 
+def to_partner(value, axis, bits):
+    return lax.ppermute(value, axis, [(i, i ^ bits) for i in range(lax.axis_size(axis))])
+
+
+def to_other(value, axis):
+    count = lax.axis_size(axis)
+    return lax.ppermute(value, axis, [(i, (i + 2 * (i % 2) - 1) % count) for i in range(count)])
+
+
 def body(density, velocity, pressure, owners):
     sizes = nx, ny, nz = density.shape
     n_sect, n_slab = lax.axis_size("sect"), lax.axis_size("slab")
@@ -335,44 +417,66 @@
         pressure.reshape(nx * ny, nz),
     )
     cells = nx * ny * nz
-    x_edge, y_edge = (FIELDS, ny, nz), (FIELDS + 1, nx, nz)
-    x_first, x_last, y_first, y_last, top, *gas = call(
+    half = n_slab // 2
+    direct = half <= 4
+    x_edge, y_edge, row = (FIELDS, ny, nz), (FIELDS + 1, nx, nz), (ROWS, nz)
+    owners = jnp.transpose(owners, (1, 2, 0))
+    shapes = [(a.shape, a.dtype) for a in (*gas, owners)]
+    x_near, x_far, y_near, y_far, top, *gas, owners = call(
         functools.partial(edges_kernel, sizes),
-        [x_edge, x_edge, y_edge, y_edge, (ROWS, nz), *(a.shape for a in gas)],
+        [x_edge, x_edge, y_edge, (FIELDS, nx, nz), row, *shapes],
         "edges",
         20 * cells,
-        [pltpu.SemaphoreType.DMA((3,))],
-        in_specs=[HBM] * 3,
-    )(*(pltpu.with_memory_space_constraint(a, pltpu.HBM) for a in gas))
-    y_low = around(y_last, "sect", 1)
-    y_high = around(y_first, "sect", -1)
-    far = [around(top, "sect", d) for d in range(2, n_sect - 1)]
-    x_low = around(x_last, "slab", 1)
-    x_high = around(x_first, "slab", -1)
-    order = jnp.transpose(owners.reshape(ny // ROWS, ROWS, lines), (2, 1, 0))
-    owner_row = order.reshape(1, columns).astype(jnp.float32)
-    (packed,) = call(
-        functools.partial(pack_kernel, sizes, geometry, len(far)),
-        [(n_slab * slots // group, width)],
+        [pltpu.SemaphoreType.DMA((4,))],
+        in_specs=[HBM] * 4,
+    )(*(pltpu.with_memory_space_constraint(a, pltpu.HBM) for a in (*gas, owners)))
+    y_near = to_partner(y_near, "sect", 1)
+    (y_far,) = call(join_kernel, [y_edge], "join", cells)(y_far, top, y_near)
+    y_far = to_other(y_far, "sect")
+    far = [around(top, "sect", d) for d in range(2, n_sect - 1)] if n_sect > 4 else []
+    x_near = to_partner(x_near, "slab", 1)
+    x_far = to_other(x_far, "slab")
+    rows = width // LANES * slots // group
+    firsts = range(half) if direct else range(1)
+    packed = call(
+        functools.partial(pack_kernel, sizes, geometry, len(far), direct),
+        [(n_slab // len(firsts) * rows, LANES)] * len(firsts),
         "pack",
-        20 * cells,
+        PACK_COST * cells,
         [pltpu.VMEM((group * width, columns), jnp.float32)],
-    )(*gas, y_low, y_high, top, owner_row, *far)
-    arrived = lax.all_to_all(packed, "slab", split_axis=0, concat_axis=0, tiled=True)
+    )(*gas, y_near, y_far, top, owners, *far)
+    if direct:
+        arrived = [to_partner(m, "slab", 2 * d) if d else m for d, m in zip(firsts, packed)]
+    else:
+        alike = [[2 * i + odd for i in range(half)] for odd in range(2)]
+        arrived = [
+            lax.all_to_all(m, "slab", split_axis=0, concat_axis=0, axis_index_groups=alike, tiled=True) for m in packed
+        ]
+    (merged,) = call(
+        functools.partial(merge_kernel, rows, firsts[::-1]),
+        [(half * rows, LANES)],
+        "merge",
+        cells,
+    )(*arrived[::-1])
+    got = to_partner(merged, "slab", 1)
     (change,) = call(
         functools.partial(change_kernel, sizes),
         [(FIELDS, nx * ny, nz)],
         "change",
         300_000 * cells,
-    )(*gas, x_low, x_high, y_low, y_high)
+    )(*gas, x_near, x_far, y_near, y_far)
     new_state, depth = call(
-        functools.partial(final_kernel, sizes, geometry),
+        functools.partial(final_kernel, sizes, geometry, firsts, direct),
         [(FIELDS, nx * ny, nz), (slots, length)],
         "final",
         100 * cells,
-        [pltpu.VMEM((FIELDS, nx * ny, nz), jnp.float32), pltpu.SemaphoreType.DMA],
+        [
+            pltpu.VMEM((FIELDS, nx * ny, nz), jnp.float32),
+            pltpu.VMEM((n_slab * slots // group, width), jnp.float32),
+            pltpu.SemaphoreType.DMA,
+        ],
         out_specs=[HBM, VMEM],
-    )(*gas, change, arrived)
+    )(*gas, change, got, *arrived)
     return (new_state.reshape(FIELDS, nx, ny, nz), depth.reshape(1, 1, slots, length))
 
 

time: 27 us -> 25.3 us (0.937)
  waiting for transfers between devices: 6.15 us -> 4.88 us
  starting transfers between devices: 12.8 us -> 13.6 us
  Pallas kernels: 6.69 us -> 5.99 us
  local copies, waits for them, and re-layouts: 0.3 us -> 0 us
    all_to_all x1 -> x0, waiting for transfers between devices: 6.14 us -> none  [body(): lax.all_to_all(packed, 'slab', split_axis=0, concat_axis=0, tiled=True)]
    ppermute x5 -> x8, waiting for transfers between devices: 0.01 us -> 4.88 us  [the longest x6 4.88 us: to_partner(): lax.ppermute(value, axis, [(i, i ^ bits) for i in range(lax.axis_size(axi...]
    ppermute x5 -> x8, starting transfers between devices: 9.47 us -> 13.6 us  [the longest x6 7.49 us: to_partner(): lax.ppermute(value, axis, [(i, i ^ bits) for i in range(lax.axis_size(axi...]
    all_to_all x1 -> x0, starting transfers between devices: 3.37 us -> none  [body(): lax.all_to_all(packed, 'slab', split_axis=0, concat_axis=0, tiled=True)]
    pallas_call x3 -> x5, Pallas kernels: 5.57 us -> 4.87 us  [the longest x1 2.73 us: body(): call(functools.partial(final_kernel, sizes, geometry, firsts, direct), [(...]
    convert_element_type x3 -> x0, local copies, waits for them, and re-layouts: 0.29 us -> none  [body(): owner_row = order.reshape(1, columns).astype(jnp.float32)]
  transfers between devices with their start and end apart: 6 -> 8, of which waited for: 1 -> 4; matrix products, arithmetic and copies ran while one was open for 1% -> 0% of each run, Pallas kernels for 10% -> 8%
where the time goes in v3:
time: 25.3 us; the launch traced here: 25.2 us
  starting transfers between devices  13.6 us (54%)
  Pallas kernels  5.99 us (24%)
  waiting for transfers between devices  4.88 us (19%)
  between operations  0.66 us (3%)
    ppermute x6, starting transfers between devices, to_partner(): lax.ppermute(value, axis, [(i, i ^ bits) for i in range(lax.axis_size(axi...  7.49 us
    ppermute x2, starting transfers between devices, to_other(): lax.ppermute(value, axis, [(i, (i + 2 * (i % 2) - 1) % count) for i in ra...  6.14 us
    ppermute x6, waiting for transfers between devices, to_partner(): lax.ppermute(value, axis, [(i, i ^ bits) for i in range(lax.axis_size(axi...  4.88 us
    pallas_call x1, Pallas kernels, body(): call(functools.partial(final_kernel, sizes, geometry, firsts, direct), [(...  2.73 us
    pallas_call x1, Pallas kernels, body(): call(functools.partial(edges_kernel, sizes), [x_edge, x_edge, y_edge, (FI...  1.25 us
    pallas_call x1, Pallas kernels, body(): call(functools.partial(change_kernel, sizes), [(FIELDS, nx * ny, nz)], 'c...  1.12 us
    pallas_call x1, Pallas kernels, body(): call(functools.partial(pack_kernel, sizes, geometry, len(far), direct), [...  0.89 us
  transfers between devices with their start and end apart: 8, of which 4 were waited for; matrix products, arithmetic and copies ran while one was open for 0% of the time, Pallas kernels for 8%

profile of v3, /device:TPU:0, one launch (start us, length us, event | category | flops | bytes accessed | tf_op | source)
XLA Modules:
  0.0 25.2 jit_solution(2818132833291302119)
XLA Ops:
  0.6 1.2 %edges.1 = (f32[5,32,128]{2,1,0:T(8,128)S(1)}, f32[5,32,128]{2,1,0:T(8,128)S(1)}, f32[6,8,128]{2,1,0:T(8,128)S(1)}, f32[5,8,128]{2,1,0:T(8,128)S(1)}, f32[8,128]...) custom-call(f32[256,128]{1,0:T(8,128)} %bitcast.7, ...), custom_call_target="tpu_custom_call" | custom-call | flops 655360 | bytes 1048576 | tf_op jit(solution)/shard_map/edges/pallas_call | solution.py:425
  1.9 0.5 %collective-permute-start.2 = (f32[6,8,128]{2,1,0:T(8,128)S(1)}, f32[6,8,128]{2,1,0:T(8,128)S(1)}, u32[]{:S(2)}, u32[]{:S(2)}) collective-permute-start(f32[6,8,128]{2,1,0:T(8,128)S(1)} %get-tuple-element.22), channel_id=1, source_target_pairs={{0,8},{8,0},{16,24},{24,16},{1,9},{9,1},{17,25},{25,17},{2,10},{10... | collective-permute-start | bytes 73736 | tf_op jit(solution)/shard_map/ppermute | solution.py:396
  2.4 0.8 %collective-permute-done.2.near_ref.y_near = f32[6,8,128]{2,1,0:T(8,128)S(1)} collective-permute-done((f32[6,8,128]{2,1,0:T(8,128)S(1)}, f32[6,8,128]{2,1,0:T(8,128)S(1)}, u32[]{:S(2)}, u32[]{:S(2)}) %collective-permute-start.2) | collective-permute-done | bytes 24608 | tf_op jit(solution)/shard_map/ppermute | solution.py:396
  3.3 2.6 %collective-permute-start.3 = (f32[6,8,128]{2,1,0:T(8,128)S(1)}, f32[6,8,128]{2,1,0:T(8,128)S(1)}, u32[]{:S(2)}, u32[]{:S(2)}) collective-permute-start(f32[6,8,128]{2,1,0:T(8,128)S(1)} %join.1), channel_id=1, source_target_pairs={{0,24},{8,16},{16,8},{24,0},{1,25},{9,17},{17,9},{25,1},{2,26},{10... | collective-permute-start | bytes 73736 | tf_op jit(solution)/shard_map/ppermute | solution.py:401
  5.9 1.5 %collective-permute-start = (f32[5,32,128]{2,1,0:T(8,128)S(1)}, f32[5,32,128]{2,1,0:T(8,128)S(1)}, u32[]{:S(2)}, u32[]{:S(2)}) collective-permute-start(f32[5,32,128]{2,1,0:T(8,128)S(1)} %get-tuple-element.20), channel_id=1, source_target_pairs={{0,1},{1,0},{2,3},{3,2},{4,5},{5,4},{6,7},{7,6},{8,9},{9,8},{10,11... | collective-permute-start | bytes 245768 | tf_op jit(solution)/shard_map/ppermute | solution.py:396
  7.4 3.5 %collective-permute-start.1 = (f32[5,32,128]{2,1,0:T(8,128)S(1)}, f32[5,32,128]{2,1,0:T(8,128)S(1)}, u32[]{:S(2)}, u32[]{:S(2)}) collective-permute-start(f32[5,32,128]{2,1,0:T(8,128)S(1)} %get-tuple-element.21), channel_id=1, source_target_pairs={{0,7},{1,2},{2,1},{3,4},{4,3},{5,6},{6,5},{7,0},{8,15},{9,10},{10,... | collective-permute-start | bytes 245768 | tf_op jit(solution)/shard_map/ppermute | solution.py:401
  10.9 0.0 collective-permute-done.3.y_far
  10.9 0.9 %pack.1 = (f32[64,128]{1,0:T(8,128)S(1)}, f32[64,128]{1,0:T(8,128)S(1)}, f32[64,128]{1,0:T(8,128)S(1)}, f32[64,128]{1,0:T(8,128)S(1)}) custom-call(f32[256,128]{1,0:T(8,128)S(1)} %get-tuple-element.17.r_ref, f32[768,128]{1,0:T(8,128)S(1)} %get-tuple-element.18.v_ref, f32[256,128]{1,0:T(8,128)S(1)} %get-tuple-element.19.p_ref, ...), custom_call_target="tpu_custom_call" | custom-call | flops 983040000 | bytes 1048576 | tf_op jit(solution)/shard_map/pack/pallas_call | solution.py:441
  11.8 0.6 %collective-permute-start.4 = (f32[64,128]{1,0:T(8,128)S(1)}, f32[64,128]{1,0:T(8,128)S(1)}, u32[]{:S(2)}, u32[]{:S(2)}) collective-permute-start(f32[64,128]{1,0:T(8,128)S(1)} %get-tuple-element.26), channel_id=1, source_target_pairs={{0,6},{1,7},{2,4},{3,5},{4,2},{5,3},{6,0},{7,1},{8,14},{9,15},{10,... | collective-permute-start | bytes 98312 | tf_op jit(solution)/shard_map/ppermute | solution.py:396
  12.4 0.0 collective-permute-start.5
  12.4 3.9 %collective-permute-start.6 = (f32[64,128]{1,0:T(8,128)S(1)}, f32[64,128]{1,0:T(8,128)S(1)}, u32[]{:S(2)}, u32[]{:S(2)}) collective-permute-start(f32[64,128]{1,0:T(8,128)S(1)} %get-tuple-element.28), channel_id=1, source_target_pairs={{0,2},{1,3},{2,0},{3,1},{4,6},{5,7},{6,4},{7,5},{8,10},{9,11},{10,... | collective-permute-start | bytes 98312 | tf_op jit(solution)/shard_map/ppermute | solution.py:396
  16.3 1.4 %collective-permute-done.4.refs_0_.rest_3_ = f32[64,128]{1,0:T(8,128)S(1)} collective-permute-done((f32[64,128]{1,0:T(8,128)S(1)}, f32[64,128]{1,0:T(8,128)S(1)}, u32[]{:S(2)}, u32[]{:S(2)}) %collective-permute-start.4) | collective-permute-done | bytes 32800 | tf_op jit(solution)/shard_map/ppermute | solution.py:396
  17.7 0.0 collective-permute-done.5.refs_1_.rest_2_
  17.7 0.5 %collective-permute-done.6.refs_2_.rest_1_ = f32[64,128]{1,0:T(8,128)S(1)} collective-permute-done((f32[64,128]{1,0:T(8,128)S(1)}, f32[64,128]{1,0:T(8,128)S(1)}, u32[]{:S(2)}, u32[]{:S(2)}) %collective-permute-start.6) | collective-permute-done | bytes 32800 | tf_op jit(solution)/shard_map/ppermute | solution.py:396
  18.2 1.0 %collective-permute-start.7 = (f32[128,128]{1,0:T(8,128)S(1)}, f32[128,128]{1,0:T(8,128)S(1)}, u32[]{:S(2)}, u32[]{:S(2)}) collective-permute-start(f32[128,128]{1,0:T(8,128)S(1)} %merge.1), channel_id=1, source_target_pairs={{0,1},{1,0},{2,3},{3,2},{4,5},{5,4},{6,7},{7,6},{8,9},{9,8},{10,11... | collective-permute-start | bytes 196616 | tf_op jit(solution)/shard_map/ppermute | solution.py:396
  19.2 0.0 collective-permute-done.x_near
  19.2 0.0 collective-permute-done.1.x_far
  19.2 1.1 %change.1.change_ref = f32[5,256,128]{2,1,0:T(8,128)S(1)} custom-call(f32[256,128]{1,0:T(8,128)S(1)} %get-tuple-element.17.r_ref, f32[768,128]{1,0:T(8,128)S(1)} %get-tuple-element.18.v_ref, f32[256,128]{1,0:T(8,128)S(1)} %get-tuple-element.19.p_ref, f32[5,32,128]{2,1,0:T(8,128)S(1)} %collective-permute-done.x_near, ...), custom_call_target="tpu_custom_call" | custom-call | flops 9830400000 | bytes 1048576 | tf_op jit(solution)/shard_map/change/pallas_call | solution.py:462
  20.3 2.1 %collective-permute-done.7.got_ref = f32[128,128]{1,0:T(8,128)S(1)} collective-permute-done((f32[128,128]{1,0:T(8,128)S(1)}, f32[128,128]{1,0:T(8,128)S(1)}, u32[]{:S(2)}, u32[]{:S(2)}) %collective-permute-start.7) | collective-permute-done | bytes 65568 | tf_op jit(solution)/shard_map/ppermute | solution.py:396
  22.4 2.7 %final.1 = (f32[5,256,128]{2,1,0:T(8,128)}, f32[32,64]{1,0:T(8,128)}) custom-call(f32[256,128]{1,0:T(8,128)S(1)} %get-tuple-element.17.r_ref, f32[768,128]{1,0:T(8,128)S(1)} %get-tuple-element.18.v_ref, f32[256,128]{1,0:T(8,128)S(1)} %get-tuple-element.19.p_ref, f32[5,256,128]{2,1,0:T(8,128)S(1)} %change.1.change_ref, ...), custom_call_target="tpu_custom_call" | custom-call | flops 3276800 | bytes 1048576 | tf_op jit(solution)/shard_map/final/pallas_call | solution.py:468
  (2 shorter events, 0.0 us)
Async XLA Ops:
  1.9 1.4 %collective-permute-start.2 = (f32[6,8,128]{2,1,0:T(8,128)S(1)}, f32[6,8,128]{2,1,0:T(8,128)S(1)}, u32[]{:S(2)}, u32[]{:S(2)}) collective-permute-start(f32[6,8,128]{2,1,0:T(8,128)S(1)} %get-tuple-element.22), channel_id=1, source_target_pairs={{0,8},{8,0},{16,24},{24,16},{1,9},{9,1},{17,25},{25,17},{2,10},{10... | collective-permute-start | bytes 73736 | tf_op jit(solution)/shard_map/ppermute | solution.py:396
  3.3 7.7 %collective-permute-start.3 = (f32[6,8,128]{2,1,0:T(8,128)S(1)}, f32[6,8,128]{2,1,0:T(8,128)S(1)}, u32[]{:S(2)}, u32[]{:S(2)}) collective-permute-start(f32[6,8,128]{2,1,0:T(8,128)S(1)} %join.1), channel_id=1, source_target_pairs={{0,24},{8,16},{16,8},{24,0},{1,25},{9,17},{17,9},{25,1},{2,26},{10... | collective-permute-start | bytes 73736 | tf_op jit(solution)/shard_map/ppermute | solution.py:401
  5.9 13.3 %collective-permute-start = (f32[5,32,128]{2,1,0:T(8,128)S(1)}, f32[5,32,128]{2,1,0:T(8,128)S(1)}, u32[]{:S(2)}, u32[]{:S(2)}) collective-permute-start(f32[5,32,128]{2,1,0:T(8,128)S(1)} %get-tuple-element.20), channel_id=1, source_target_pairs={{0,1},{1,0},{2,3},{3,2},{4,5},{5,4},{6,7},{7,6},{8,9},{9,8},{10,11... | collective-permute-start | bytes 245768 | tf_op jit(solution)/shard_map/ppermute | solution.py:396
  7.4 11.8 %collective-permute-start.1 = (f32[5,32,128]{2,1,0:T(8,128)S(1)}, f32[5,32,128]{2,1,0:T(8,128)S(1)}, u32[]{:S(2)}, u32[]{:S(2)}) collective-permute-start(f32[5,32,128]{2,1,0:T(8,128)S(1)} %get-tuple-element.21), channel_id=1, source_target_pairs={{0,7},{1,2},{2,1},{3,4},{4,3},{5,6},{6,5},{7,0},{8,15},{9,10},{10,... | collective-permute-start | bytes 245768 | tf_op jit(solution)/shard_map/ppermute | solution.py:401
  11.8 5.8 %collective-permute-start.4 = (f32[64,128]{1,0:T(8,128)S(1)}, f32[64,128]{1,0:T(8,128)S(1)}, u32[]{:S(2)}, u32[]{:S(2)}) collective-permute-start(f32[64,128]{1,0:T(8,128)S(1)} %get-tuple-element.26), channel_id=1, source_target_pairs={{0,6},{1,7},{2,4},{3,5},{4,2},{5,3},{6,0},{7,1},{8,14},{9,15},{10,... | collective-permute-start | bytes 98312 | tf_op jit(solution)/shard_map/ppermute | solution.py:396
  12.4 5.3 %collective-permute-start.5 = (f32[64,128]{1,0:T(8,128)S(1)}, f32[64,128]{1,0:T(8,128)S(1)}, u32[]{:S(2)}, u32[]{:S(2)}) collective-permute-start(f32[64,128]{1,0:T(8,128)S(1)} %get-tuple-element.27), channel_id=1, source_target_pairs={{0,4},{1,5},{2,6},{3,7},{4,0},{5,1},{6,2},{7,3},{8,12},{9,13},{10,... | collective-permute-start | bytes 98312 | tf_op jit(solution)/shard_map/ppermute | solution.py:396
  12.4 5.8 %collective-permute-start.6 = (f32[64,128]{1,0:T(8,128)S(1)}, f32[64,128]{1,0:T(8,128)S(1)}, u32[]{:S(2)}, u32[]{:S(2)}) collective-permute-start(f32[64,128]{1,0:T(8,128)S(1)} %get-tuple-element.28), channel_id=1, source_target_pairs={{0,2},{1,3},{2,0},{3,1},{4,6},{5,7},{6,4},{7,5},{8,10},{9,11},{10,... | collective-permute-start | bytes 98312 | tf_op jit(solution)/shard_map/ppermute | solution.py:396
  18.2 4.3 %collective-permute-start.7 = (f32[128,128]{1,0:T(8,128)S(1)}, f32[128,128]{1,0:T(8,128)S(1)}, u32[]{:S(2)}, u32[]{:S(2)}) collective-permute-start(f32[128,128]{1,0:T(8,128)S(1)} %merge.1), channel_id=1, source_target_pairs={{0,1},{1,0},{2,3},{3,2},{4,5},{5,4},{6,7},{7,6},{8,9},{9,8},{10,11... | collective-permute-start | bytes 196616 | tf_op jit(solution)/shard_map/ppermute | solution.py:396

commit v4 on v3

--- a/solution.py
+++ b/solution.py
@@ -1,5 +1,6 @@
 import functools
 import math
+from typing import NamedTuple
 
 import jax
 import jax.numpy as jnp
@@ -21,11 +22,35 @@
 FIELDS = 5
 UNROLL = 64
 PACK_COST = 30_000
+PREPARE_COST = 300
 
 VMEM = pl.BlockSpec(memory_space=pltpu.VMEM)
 
 
 HBM = pl.BlockSpec(memory_space=pltpu.HBM)
+
+
+class Message(NamedTuple):
+    owners: int
+    slots: int
+    group: int
+    rows: int
+    part: int
+    main: int
+    extra: int
+    fold: int
+    extra_rows: int
+    count: int
+
+
+def shape_of_message(nx, owners, slots, group):
+    rows, part = slots // group, nx * group
+    main = min(2 * FIELDS, LANES // part)
+    extra = 2 * FIELDS - main
+    fold = min(rows, LANES // (extra * part)) if extra else 1
+    extra_rows = rows // fold if extra else 0
+    count = 2 * rows + 2 * extra_rows + ROWS
+    return Message(owners, slots, group, rows, part, main, extra, fold, extra_rows, count)
 
 
 def call(kernel, out_shapes, name, flops, scratch=(), in_specs=None, out_specs=None):
@@ -115,10 +140,11 @@
     sizes, r_hbm, v_hbm, p_hbm, o_hbm, x_near, x_far, y_near, y_far, top_ref, r_ref, v_ref, p_ref, o_ref, sems
 ):
     nx, ny, nz = sizes
-    loads = [
-        pltpu.make_async_copy(source, target, sems.at[i])
-        for i, (source, target) in enumerate(((r_hbm, r_ref), (v_hbm, v_ref), (p_hbm, p_ref), (o_hbm, o_ref)))
-    ]
+    pairs = [(r_hbm, r_ref), (p_hbm, p_ref), (o_hbm, o_ref)]
+    for k in range(3):
+        component = pl.ds(k * nx * ny, nx * ny)
+        pairs.append((v_hbm.at[component], v_ref.at[component]))
+    loads = [pltpu.make_async_copy(source, target, sems.at[i]) for i, (source, target) in enumerate(pairs)]
     for load in loads:
         load.start()
     for load in loads:
@@ -142,23 +168,23 @@
     top_ref[...] = top
 
 
-def join_kernel(y_far, top_ref, near_ref, out_ref):
+def join_kernel(y_far, top_ref, near_ref, target_ref, out_ref, target_out):
     for f in range(FIELDS):
         out_ref[f] = y_far[f]
     out_ref[FIELDS] = jnp.maximum(top_ref[...], near_ref[FIELDS])
-
-
-def pack_kernel(sizes, geometry, n_far, direct, r_ref, v_ref, p_ref, y_near, y_far, top_ref, owner_ref, *rest):
+    target_out[...] = target_ref[...]
+
+
+def spread_rows(msg):
+    return LANES + msg.extra * msg.part
+
+
+def prepare_kernel(sizes, msg, r_ref, v_ref, p_ref, owner_ref, cell_ref, change_ref, target_ref):
     nx, ny, nz = sizes
-    n_owner, slots, group, width = geometry
-    far, outs, spread = rest[:n_far], rest[n_far:-1], rest[-1]
-    y_low, y_high = sides([y_near[f] for f in range(FIELDS)], [y_far[f] for f in range(FIELDS)], "sect")
     lines = nz // STRIDE
     columns = ny * lines
     step = STRIDE // ROWS
-    per_owner = slots // group
     lane = lax.broadcasted_iota(jnp.int32, (nx, nz), 1)
-    tiles = []
     for t in range(step):
         cell = None
         for s in range(ny // step):
@@ -169,78 +195,112 @@
             else:
                 mine = (lane - step * s + 1) % STRIDE < 3
                 cell = [jnp.where(mine, a, b) for a, b in zip(rows, cell)]
-        tiles.append(cell)
+        here = flux_parts(cell, *derived(cell), 2)
+        after = face(here, [shift(a, -1, 1) for a in here])
+        for f in range(FIELDS):
+            cell_ref[t, f] = cell[f]
+            change_ref[t, f] = after[f] - shift(after[f], 1, 1)
+    owner = jnp.concatenate([owner_ref[k] for k in range(lines)], axis=1).astype(jnp.float32)
+    own = jnp.broadcast_to(owner, (columns, columns))
+    own_t = own.T
+
+    def place(dim):
+        at = lax.broadcasted_iota(jnp.int32, (columns, columns), dim)
+        return (at % ny) * lines + at // ny
+
+    ahead = (own == own_t) & (place(0) < place(1))
+    rank = jnp.sum(jnp.where(ahead, 1.0, 0.0), axis=0, keepdims=True)
+    target_ref[...] = jnp.broadcast_to(owner * msg.slots + rank, target_ref.shape)
+
+
+def pack_kernel(sizes, msg, n_far, direct, cell_ref, change_ref, target_ref, y_near, y_far, top_ref, *rest):
+    nx, ny, nz = sizes
+    slots, group, width = msg.slots, msg.group, spread_rows(msg)
+    far, outs, spread = rest[:n_far], rest[n_far:-1], rest[-1]
+    y_low, y_high = sides([y_near[f] for f in range(FIELDS)], [y_far[f] for f in range(FIELDS)], "sect")
+    columns = ny * (nz // STRIDE)
+    step = STRIDE // ROWS
+    lane = lax.broadcasted_iota(jnp.int32, (nx, nz), 1)
+    target = target_ref[0:1]
+    tiles = [[cell_ref[t, f] for f in range(FIELDS)] for t in range(step)]
     first = lane % STRIDE < step
     last = lane % STRIDE >= ny - step
     below = [jnp.where(first, y_low[f], shift(a, step, 1)) for f, a in enumerate(tiles[-1])]
     above = [jnp.where(last, shift(y_high[f], ny - step, 1), shift(a, -step, 1)) for f, a in enumerate(tiles[0])]
-    full = [(cell, *derived(cell)) for cell in (below, *tiles, above)]
-    y_parts = [flux_parts(*c, 1) for c in full]
-    y_faces = [face(a, b) for a, b in zip(y_parts, y_parts[1:])]
+    parts = [flux_parts(cell, *derived(cell), 1) for cell in (below, *tiles, above)]
+    faces = [face(a, b) for a, b in zip(parts, parts[1:])]
     dense = None
     for t in range(step):
-        cell, state, sound = full[t + 1]
-        here = flux_parts(cell, state, sound, 2)
-        after = face(here, [shift(a, -1, 1) for a in here])
-        total = [
-            (high - low) + (a - shift(a, 1, 1))
-            for low, high, a in zip(y_faces[t], y_faces[t + 1], after)
-        ]
-        values = [shift(a, t, 1) for a in [*cell, *total]]
+        total = [(high - low) + change_ref[t, f] for f, (low, high) in enumerate(zip(faces[t], faces[t + 1]))]
+        values = [shift(a, t, 1) for a in [*tiles[t], *total]]
         dense = values if dense is None else [jnp.where(lane % step == t, a, b) for a, b in zip(values, dense)]
     spread[...] = jnp.zeros_like(spread)
     for f, value in enumerate(dense):
         for h in range(group):
             spread[pl.ds(h * width + f * nx * group + h, nx, group), :] = value
-    owner = jnp.concatenate([owner_ref[k] for k in range(lines)], axis=1).astype(jnp.float32)
-    own = jnp.broadcast_to(owner, (columns, columns))
-    own_t = own.T
-
-    def place(dim):
-        at = lax.broadcasted_iota(jnp.int32, (columns, columns), dim)
-        return (at % ny) * lines + at // ny
-
-    ahead = (own == own_t) & (place(0) < place(1))
-    rank = jnp.sum(jnp.where(ahead, 1.0, 0.0), axis=0, keepdims=True)
-    target = owner * slots + rank
-    row = lax.broadcasted_iota(jnp.int32, (n_owner * per_owner, columns), 0)
-    block = row // per_owner
     z_me, y_me = place_of(direct)
-    own_of = 2 * ((block // 2) ^ z_me) + ((block % 2) ^ y_me)
-    chosen = []
-    for h in range(group):
-        slot = (own_of * slots + h * per_owner + row % per_owner).astype(jnp.float32)
-        chosen.append(jnp.where(slot == target, 1.0, 0.0))
-    chosen = jnp.concatenate(chosen, axis=1).astype(jnp.bfloat16)
-    value = jnp.concatenate([spread[pl.ds(h * width, width), :] for h in range(group)], axis=1)
-    picked = None
-    for _ in range(3):
-        piece = value.astype(jnp.bfloat16)
-        value = value - piece.astype(jnp.float32)
-        part = lax.dot_general(chosen, piece, (((1,), (1,)), ((), ())), preferred_element_type=jnp.float32)
-        picked = part if picked is None else picked + part
+
+    def chosen(rows, first):
+        row = lax.broadcasted_iota(jnp.int32, (msg.owners * rows, columns), 0)
+        block = row // rows
+        own_of = 2 * ((block // 2) ^ z_me) + ((block % 2) ^ y_me)
+        out = []
+        for h in range(group):
+            slot = (own_of * slots + h * msg.rows + first + row % rows).astype(jnp.float32)
+            out.append(jnp.where(slot == target, 1.0, 0.0))
+        return jnp.concatenate(out, axis=1).astype(jnp.bfloat16)
+
+    def pieces(first, count):
+        value = jnp.concatenate([spread[pl.ds(h * width + first, count), :] for h in range(group)], axis=1)
+        out = []
+        for _ in range(3):
+            out.append(value.astype(jnp.bfloat16))
+            value = value - out[-1].astype(jnp.float32)
+        return out
+
+    def pick(selection, values):
+        parts = [
+            lax.dot_general(selection, v, (((1,), (1,)), ((), ())), preferred_element_type=jnp.float32) for v in values
+        ]
+        return (parts[0] + parts[1]) + parts[2]
+
+    per = msg.count
+    each = msg.owners // len(outs)
+    picked = pick(chosen(msg.rows, 0), pieces(0, LANES))
+    for b in range(msg.owners):
+        at = (b % each) // 2 * per + b % 2 * msg.rows
+        outs[b // each][pl.ds(at, msg.rows), :] = picked[b * msg.rows : (b + 1) * msg.rows]
+    if msg.extra:
+        values = pieces(LANES, msg.extra * msg.part)
+        rows = msg.extra_rows
+        picked = jnp.concatenate([pick(chosen(rows, a * rows), values) for a in range(msg.fold)], axis=1)
+        for b in range(msg.owners):
+            at = (b % each) // 2 * per + 2 * msg.rows + b % 2 * rows
+            outs[b // each][pl.ds(at, rows), :] = picked[b * rows : (b + 1) * rows]
     top = jnp.maximum(jnp.maximum(top_ref[...], y_near[FIELDS]), y_far[FIELDS])
     for ref in far:
         top = jnp.maximum(top, ref[...])
-    top = jnp.max(top, keepdims=True)
-    out_lane = lax.broadcasted_iota(jnp.int32, picked.shape, 1)
-    picked = jnp.where(out_lane < 2 * FIELDS * nx * group, picked, top)
-    parts = width // LANES
-    each = n_owner // len(outs)
-    for b in range(n_owner):
-        for w in range(parts):
-            outs[b // each][pl.ds(((b % each) * parts + w) * per_owner, per_owner), :] = picked[
-                b * per_owner : (b + 1) * per_owner, w * LANES : (w + 1) * LANES
-            ]
-
-
-def merge_kernel(rows, firsts, *refs):
+    for out in outs:
+        for d in range(each // 2):
+            out[pl.ds((d + 1) * per - ROWS, ROWS), :] = top
+
+
+def merge_kernel(msg, firsts, *refs):
+    out = refs[-1]
+    half, top = msg.owners // 2, None
     for first, ref in zip(firsts, refs[:-1]):
-        for d in range(ref.shape[0] // (2 * rows)):
-            refs[-1][pl.ds((first + d) * rows, rows), :] = ref[pl.ds((2 * d + 1) * rows, rows), :]
-
-
-def change_kernel(sizes, r_ref, v_ref, p_ref, x_near, x_far, y_near, y_far, out_ref):
+        for d in range(ref.shape[0] // msg.count):
+            at, to = d * msg.count, first + d
+            out[pl.ds(to * msg.rows, msg.rows), :] = ref[pl.ds(at + msg.rows, msg.rows), :]
+            if msg.extra:
+                rows = msg.extra_rows
+                out[pl.ds(half * msg.rows + to * rows, rows), :] = ref[pl.ds(at + 2 * msg.rows + rows, rows), :]
+            new = ref[pl.ds(at + msg.count - ROWS, ROWS), :]
+            top = new if top is None else jnp.maximum(top, new)
+    out[pl.ds(half * (msg.rows + msg.extra_rows), ROWS), :] = top
+
+
+def change_kernel(sizes, r_ref, v_ref, p_ref, x_far, x_near, y_near, y_far, out_ref):
     nx, ny, nz = sizes
     every = range(FIELDS)
     x_low, x_high = sides([x_near[f] for f in every], [x_far[f] for f in every], "slab")
@@ -287,49 +347,47 @@
         here = following
 
 
-def final_kernel(sizes, geometry, firsts, direct, r_ref, v_ref, p_ref, change_ref, got_ref, *rest):
-    blocks, (new_hbm, depth_ref, new_ref, packed_ref, sem) = rest[: len(firsts)], rest[len(firsts) :]
+def final_kernel(sizes, msg, firsts, direct, r_ref, v_ref, p_ref, change_ref, got_ref, *rest):
+    blocks = rest[: len(firsts)]
+    new_hbm, depth_hbm, new_ref, depth_ref, main_ref, extra_ref, sems = rest[len(firsts) :]
     nx, ny, nz = sizes
-    n_owner, slots, group, width = geometry
-    per_owner = slots // group
-    part = nx * group
-    length = nx * n_owner
-    parts = width // LANES
-    rows = parts * per_owner
-
+    n_owner, group, part = msg.owners, msg.group, msg.part
+    half, length = n_owner // 2, nx * n_owner
+    top = got_ref[pl.ds(half * (msg.rows + msg.extra_rows), ROWS), :]
+    for ref in blocks:
+        for d in range(ref.shape[0] // msg.count):
+            top = jnp.maximum(top, ref[pl.ds((d + 1) * msg.count - ROWS, ROWS), :])
+    step = COURANT / jnp.max(top, keepdims=True)
+    writes = []
+    for x in range(nx):
+        rows = pl.ds(x * ny, ny)
+        state, _ = derived(fields_of(r_ref, v_ref, p_ref, rows))
+        for f in range(FIELDS):
+            new_ref[f, rows, :] = state[f] - step * change_ref[f, rows, :]
+        writes.append(pltpu.make_async_copy(new_ref.at[:, rows], new_hbm.at[:, rows], sems.at[x]))
+        writes[-1].start()
     z_me, y_me = place_of(direct)
 
-    def settle(source, at, d, odd):
+    def settle(source, at, extra_at, d, odd):
         owner = 2 * (d ^ z_me) + (odd ^ y_me)
-        for w in range(parts):
-            to = owner * per_owner
-            if per_owner % ROWS == 0:
-                to = pl.multiple_of(to, ROWS)
-            packed_ref[pl.ds(to, per_owner), pl.ds(w * LANES, LANES)] = source[
-                pl.ds(at + w * per_owner, per_owner), :
-            ]
+        main_ref[owner] = source[pl.ds(at, msg.rows), :]
+        if msg.extra:
+            extra_ref[owner] = source[pl.ds(extra_at, msg.extra_rows), :]
 
     for first, ref in zip(firsts, blocks):
-        for d in range(ref.shape[0] // (2 * rows)):
-            settle(ref, 2 * d * rows, first + d, 0)
-    for d in range(got_ref.shape[0] // rows):
-        settle(got_ref, d * rows, d, 1)
-    everything = packed_ref[...]
-    lane = lax.broadcasted_iota(jnp.int32, everything.shape, 1)
-    fastest = jnp.max(jnp.where(lane >= 2 * FIELDS * part, everything, 0.0), keepdims=True)
-    step = COURANT / fastest
-    for x in range(nx):
-        state, _ = derived(fields_of(r_ref, v_ref, p_ref, pl.ds(x * ny, ny)))
-        for f in range(FIELDS):
-            new_ref[f, pl.ds(x * ny, ny), :] = state[f] - step * change_ref[f, pl.ds(x * ny, ny), :]
-    writing = pltpu.make_async_copy(new_ref, new_hbm, sem)
-    writing.start()
+        for d in range(ref.shape[0] // msg.count):
+            settle(ref, d * msg.count, d * msg.count + 2 * msg.rows, first + d, 0)
+    for d in range(half):
+        settle(got_ref, d * msg.rows, half * msg.rows + d * msg.extra_rows, d, 1)
     line = []
-    for f in range(2 * FIELDS):
-        pieces = [
-            packed_ref[pl.ds(q * per_owner, per_owner), pl.ds(f * part, part)] for q in range(n_owner)
-        ]
-        line.append(jnp.concatenate(pieces, axis=1))
+    for f in range(msg.main):
+        line.append(jnp.concatenate([main_ref[q, :, pl.ds(f * part, part)] for q in range(n_owner)], axis=1))
+    for f in range(msg.extra):
+        folds = []
+        for a in range(msg.fold):
+            at = pl.ds((a * msg.extra + f) * part, part)
+            folds.append(jnp.concatenate([extra_ref[q, :, at] for q in range(n_owner)], axis=1))
+        line.append(jnp.concatenate(folds, axis=0))
     cell, change = line[:FIELDS], line[FIELDS:]
     taken = cell[0] > 0.0
     cell[0] = jnp.where(taken, cell[0], 1.0)
@@ -381,10 +439,13 @@
         cell_of = lax.broadcasted_iota(jnp.int32, (group * length, length), 1)
         for h in range(group):
             pick = jnp.where(at == cell_of * group + h, 1.0, 0.0)
-            depth_ref[pl.ds(h * per_owner, per_owner), :] = jnp.dot(
+            depth_ref[pl.ds(h * msg.rows, msg.rows), :] = jnp.dot(
                 running, pick, precision=lax.Precision.HIGHEST, preferred_element_type=jnp.float32
             )
-    writing.wait()
+    writes.append(pltpu.make_async_copy(depth_ref, depth_hbm, sems.at[nx]))
+    writes[-1].start()
+    for write in writes:
+        write.wait()
 
 
 def around(value, axis, amount):
@@ -409,8 +470,7 @@
     slots = 2 * columns // n_slab
     length = nx * n_slab
     group = max(1, LANES // length)
-    width = -(-(2 * FIELDS * nx * group + 1) // LANES) * LANES
-    geometry = (n_slab, slots, group, width)
+    geometry = shape_of_message(nx, n_slab, slots, group)
     gas = (
         density.reshape(nx * ny, nz),
         velocity.reshape(3 * nx * ny, nz),
@@ -427,24 +487,30 @@
         [x_edge, x_edge, y_edge, (FIELDS, nx, nz), row, *shapes],
         "edges",
         20 * cells,
-        [pltpu.SemaphoreType.DMA((4,))],
+        [pltpu.SemaphoreType.DMA((6,))],
         in_specs=[HBM] * 4,
     )(*(pltpu.with_memory_space_constraint(a, pltpu.HBM) for a in (*gas, owners)))
+    tiles = (STRIDE // ROWS, FIELDS, nx, nz)
+    cells_at, change_at, target = call(
+        functools.partial(prepare_kernel, sizes, geometry),
+        [tiles, tiles, (ROWS, columns)],
+        "prepare",
+        PREPARE_COST * cells,
+    )(*gas, owners)
     y_near = to_partner(y_near, "sect", 1)
-    (y_far,) = call(join_kernel, [y_edge], "join", cells)(y_far, top, y_near)
+    y_far, target = call(join_kernel, [y_edge, (ROWS, columns)], "join", cells)(y_far, top, y_near, target)
     y_far = to_other(y_far, "sect")
     far = [around(top, "sect", d) for d in range(2, n_sect - 1)] if n_sect > 4 else []
     x_near = to_partner(x_near, "slab", 1)
     x_far = to_other(x_far, "slab")
-    rows = width // LANES * slots // group
     firsts = range(half) if direct else range(1)
     packed = call(
         functools.partial(pack_kernel, sizes, geometry, len(far), direct),
-        [(n_slab // len(firsts) * rows, LANES)] * len(firsts),
+        [(half // len(firsts) * geometry.count, LANES)] * len(firsts),
         "pack",
         PACK_COST * cells,
-        [pltpu.VMEM((group * width, columns), jnp.float32)],
-    )(*gas, y_near, y_far, top, owners, *far)
+        [pltpu.VMEM((group * spread_rows(geometry), columns), jnp.float32)],
+    )(cells_at, change_at, target, y_near, y_far, top, *far)
     if direct:
         arrived = [to_partner(m, "slab", 2 * d) if d else m for d, m in zip(firsts, packed)]
     else:
@@ -453,8 +519,8 @@
             lax.all_to_all(m, "slab", split_axis=0, concat_axis=0, axis_index_groups=alike, tiled=True) for m in packed
         ]
     (merged,) = call(
-        functools.partial(merge_kernel, rows, firsts[::-1]),
-        [(half * rows, LANES)],
+        functools.partial(merge_kernel, geometry, firsts[::-1]),
+        [(half * (geometry.rows + geometry.extra_rows) + ROWS, LANES)],
         "merge",
         cells,
     )(*arrived[::-1])
@@ -464,7 +530,7 @@
         [(FIELDS, nx * ny, nz)],
         "change",
         300_000 * cells,
-    )(*gas, x_near, x_far, y_near, y_far)
+    )(*gas, x_far, x_near, y_near, y_far)
     new_state, depth = call(
         functools.partial(final_kernel, sizes, geometry, firsts, direct),
         [(FIELDS, nx * ny, nz), (slots, length)],
@@ -472,10 +538,12 @@
         100 * cells,
         [
             pltpu.VMEM((FIELDS, nx * ny, nz), jnp.float32),
-            pltpu.VMEM((n_slab * slots // group, width), jnp.float32),
-            pltpu.SemaphoreType.DMA,
+            pltpu.VMEM((slots, length), jnp.float32),
+            pltpu.VMEM((n_slab, geometry.rows, LANES), jnp.float32),
+            pltpu.VMEM((n_slab, max(1, geometry.extra_rows), LANES), jnp.float32),
+            pltpu.SemaphoreType.DMA((nx + 1,)),
         ],
-        out_specs=[HBM, VMEM],
+        out_specs=[HBM, HBM],
     )(*gas, change, got, *arrived)
     return (new_state.reshape(FIELDS, nx, ny, nz), depth.reshape(1, 1, slots, length))
 

time: 25.3 us -> 23.8 us (0.941)
  waiting for transfers between devices: 4.88 us -> 3.12 us
  starting transfers between devices: 13.6 us -> 14.1 us
  Pallas kernels: 5.99 us -> 5.72 us
    ppermute x6, waiting for transfers between devices: 4.88 us -> 3.11 us  [to_partner(): lax.ppermute(value, axis, [(i, i ^ bits) for i in range(lax.axis_size(axi...]
    ppermute x2, starting transfers between devices: 6.14 us -> 7.16 us  [to_other(): lax.ppermute(value, axis, [(i, (i + 2 * (i % 2) - 1) % count) for i in ra...]
    pallas_call x2 -> x3, Pallas kernels: 0.01 us -> 0.62 us  [the longest x1 0.61 us: body(): call(functools.partial(prepare_kernel, sizes, geometry), [tiles, tiles, (...]
    pallas_call x1, Pallas kernels: 2.73 us -> 2.14 us  [body(): call(functools.partial(final_kernel, sizes, geometry, firsts, direct), [(...]
    ppermute x6, starting transfers between devices: 7.49 us -> 6.95 us  [to_partner(): lax.ppermute(value, axis, [(i, i ^ bits) for i in range(lax.axis_size(axi...]
    pallas_call x1, Pallas kernels: 0.89 us -> 0.48 us  [body(): call(functools.partial(pack_kernel, sizes, geometry, len(far), direct), [...]
  transfers between devices with their start and end apart: 8 -> 8, of which waited for: 4 -> 5; matrix products, arithmetic and copies ran while one was open for 0% -> 0% of each run, Pallas kernels for 8% -> 9%
where the time goes in v4:
time: 23.8 us; the launch traced here: 23.6 us
  starting transfers between devices  14.1 us (59%)
  Pallas kernels  5.72 us (24%)
  waiting for transfers between devices  3.12 us (13%)
  between operations  0.66 us (3%)
    ppermute x2, starting transfers between devices, to_other(): lax.ppermute(value, axis, [(i, (i + 2 * (i % 2) - 1) % count) for i in ra...  7.16 us
    ppermute x6, starting transfers between devices, to_partner(): lax.ppermute(value, axis, [(i, i ^ bits) for i in range(lax.axis_size(axi...  6.95 us
    ppermute x6, waiting for transfers between devices, to_partner(): lax.ppermute(value, axis, [(i, i ^ bits) for i in range(lax.axis_size(axi...  3.11 us
    pallas_call x1, Pallas kernels, body(): call(functools.partial(final_kernel, sizes, geometry, firsts, direct), [(...  2.14 us
    pallas_call x1, Pallas kernels, body(): call(functools.partial(edges_kernel, sizes), [x_edge, x_edge, y_edge, (FI...  1.35 us
    pallas_call x1, Pallas kernels, body(): call(functools.partial(change_kernel, sizes), [(FIELDS, nx * ny, nz)], 'c...  1.12 us
    pallas_call x1, Pallas kernels, body(): call(functools.partial(prepare_kernel, sizes, geometry), [tiles, tiles, (...  0.61 us
    pallas_call x1, Pallas kernels, body(): call(functools.partial(pack_kernel, sizes, geometry, len(far), direct), [...  0.48 us
  transfers between devices with their start and end apart: 8, of which 5 were waited for; matrix products, arithmetic and copies ran while one was open for 0% of the time, Pallas kernels for 9%

profile of v4, /device:TPU:0, one launch (start us, length us, event | category | flops | bytes accessed | tf_op | source)
XLA Modules:
  0.0 23.6 jit_solution(17521726254600738261)
XLA Ops:
  0.6 1.4 %edges.1 = (f32[5,32,128]{2,1,0:T(8,128)S(1)}, f32[5,32,128]{2,1,0:T(8,128)S(1)}, f32[6,8,128]{2,1,0:T(8,128)S(1)}, f32[5,8,128]{2,1,0:T(8,128)S(1)}, f32[8,128]...) custom-call(f32[256,128]{1,0:T(8,128)} %bitcast.7, ...), custom_call_target="tpu_custom_call" | custom-call | flops 655360 | bytes 1048576 | tf_op jit(solution)/shard_map/edges/pallas_call | solution.py:485
  2.0 0.5 %collective-permute-start.2 = (f32[6,8,128]{2,1,0:T(8,128)S(1)}, f32[6,8,128]{2,1,0:T(8,128)S(1)}, u32[]{:S(2)}, u32[]{:S(2)}) collective-permute-start(f32[6,8,128]{2,1,0:T(8,128)S(1)} %get-tuple-element.27), channel_id=1, source_target_pairs={{0,8},{8,0},{16,24},{24,16},{1,9},{9,1},{17,25},{25,17},{2,10},{10... | collective-permute-start | bytes 73736 | tf_op jit(solution)/shard_map/ppermute | solution.py:457
  2.5 0.6 %prepare.1 = (f32[4,5,8,128]{3,2,1,0:T(8,128)S(1)}, f32[4,5,8,128]{3,2,1,0:T(8,128)S(1)}, f32[8,128]{1,0:T(8,128)S(1)}) custom-call(f32[256,128]{1,0:T(8,128)S(1)} %get-tuple-element.22.r_ref, f32[768,128]{1,0:T(8,128)S(1)} %get-tuple-element.23.v_ref, f32[256,128]{1,0:T(8,128)S(1)} %get-tuple-element.24.p_ref, s32[4,1,32]{2,1,0:T(1,128)S(1)} %get-tuple-element.30.owner_ref), custom_call_target="tpu_custom_call" | custom-call | flops 9830400 | bytes 1048576 | tf_op jit(solution)/shard_map/prepare/pallas_call | solution.py:494
  3.1 0.2 collective-permute-done.2.near_ref.y_near
  3.4 2.6 %collective-permute-start.3 = (f32[6,8,128]{2,1,0:T(8,128)S(1)}, f32[6,8,128]{2,1,0:T(8,128)S(1)}, u32[]{:S(2)}, u32[]{:S(2)}) collective-permute-start(f32[6,8,128]{2,1,0:T(8,128)S(1)} %get-tuple-element.32), channel_id=1, source_target_pairs={{0,24},{8,16},{16,8},{24,0},{1,25},{9,17},{17,9},{25,1},{2,26},{10... | collective-permute-start | bytes 73736 | tf_op jit(solution)/shard_map/ppermute | solution.py:462
  6.0 4.6 %collective-permute-start = (f32[5,32,128]{2,1,0:T(8,128)S(1)}, f32[5,32,128]{2,1,0:T(8,128)S(1)}, u32[]{:S(2)}, u32[]{:S(2)}) collective-permute-start(f32[5,32,128]{2,1,0:T(8,128)S(1)} %get-tuple-element.25), channel_id=1, source_target_pairs={{0,7},{1,2},{2,1},{3,4},{4,3},{5,6},{6,5},{7,0},{8,15},{9,10},{10,... | collective-permute-start | bytes 245768 | tf_op jit(solution)/shard_map/ppermute | solution.py:462
  10.5 0.0 collective-permute-start.1
  10.5 0.0 collective-permute-done.3.y_far
  10.5 0.5 %pack.1 = (f32[48,128]{1,0:T(8,128)S(1)}, f32[48,128]{1,0:T(8,128)S(1)}, f32[48,128]{1,0:T(8,128)S(1)}, f32[48,128]{1,0:T(8,128)S(1)}) custom-call(f32[4,5,8,128]{3,2,1,0:T(8,128)S(1)} %get-tuple-element.33.cell_ref, f32[4,5,8,128]{3,2,1,0:T(8,128)S(1)} %get-tuple-element.34.change_ref, f32[8,128]{1,0:T(8,128)S(1)} %get-tuple-element.35.target_ref, ...), custom_call_target="tpu_custom_call" | custom-call | flops 983040000 | bytes 1048576 | tf_op jit(solution)/shard_map/pack/pallas_call | solution.py:507
  11.0 1.1 %collective-permute-start.4 = (f32[48,128]{1,0:T(8,128)S(1)}, f32[48,128]{1,0:T(8,128)S(1)}, u32[]{:S(2)}, u32[]{:S(2)}) collective-permute-start(f32[48,128]{1,0:T(8,128)S(1)} %get-tuple-element.36), channel_id=1, source_target_pairs={{0,6},{1,7},{2,4},{3,5},{4,2},{5,3},{6,0},{7,1},{8,14},{9,15},{10,... | collective-permute-start | bytes 73736 | tf_op jit(solution)/shard_map/ppermute | solution.py:457
  12.1 0.5 %collective-permute-start.5 = (f32[48,128]{1,0:T(8,128)S(1)}, f32[48,128]{1,0:T(8,128)S(1)}, u32[]{:S(2)}, u32[]{:S(2)}) collective-permute-start(f32[48,128]{1,0:T(8,128)S(1)} %get-tuple-element.37), channel_id=1, source_target_pairs={{0,4},{1,5},{2,6},{3,7},{4,0},{5,1},{6,2},{7,3},{8,12},{9,13},{10,... | collective-permute-start | bytes 73736 | tf_op jit(solution)/shard_map/ppermute | solution.py:457
  12.6 2.9 %collective-permute-start.6 = (f32[48,128]{1,0:T(8,128)S(1)}, f32[48,128]{1,0:T(8,128)S(1)}, u32[]{:S(2)}, u32[]{:S(2)}) collective-permute-start(f32[48,128]{1,0:T(8,128)S(1)} %get-tuple-element.38), channel_id=1, source_target_pairs={{0,2},{1,3},{2,0},{3,1},{4,6},{5,7},{6,4},{7,5},{8,10},{9,11},{10,... | collective-permute-start | bytes 73736 | tf_op jit(solution)/shard_map/ppermute | solution.py:457
  15.5 1.3 %collective-permute-done.4.refs_0_.rest_3_ = f32[48,128]{1,0:T(8,128)S(1)} collective-permute-done((f32[48,128]{1,0:T(8,128)S(1)}, f32[48,128]{1,0:T(8,128)S(1)}, u32[]{:S(2)}, u32[]{:S(2)}) %collective-permute-start.4) | collective-permute-done | bytes 24608 | tf_op jit(solution)/shard_map/ppermute | solution.py:457
  16.7 0.5 %collective-permute-done.5.refs_1_.rest_2_ = f32[48,128]{1,0:T(8,128)S(1)} collective-permute-done((f32[48,128]{1,0:T(8,128)S(1)}, f32[48,128]{1,0:T(8,128)S(1)}, u32[]{:S(2)}, u32[]{:S(2)}) %collective-permute-start.5) | collective-permute-done | bytes 24608 | tf_op jit(solution)/shard_map/ppermute | solution.py:457
  17.2 0.2 collective-permute-done.6.refs_2_.rest_1_
  17.4 2.0 %collective-permute-start.7 = (f32[88,128]{1,0:T(8,128)S(1)}, f32[88,128]{1,0:T(8,128)S(1)}, u32[]{:S(2)}, u32[]{:S(2)}) collective-permute-start(f32[88,128]{1,0:T(8,128)S(1)} %merge.1), channel_id=1, source_target_pairs={{0,1},{1,0},{2,3},{3,2},{4,5},{5,4},{6,7},{7,6},{8,9},{9,8},{10,11... | collective-permute-start | bytes 135176 | tf_op jit(solution)/shard_map/ppermute | solution.py:457
  19.4 0.0 collective-permute-done.x_far
  19.4 0.0 collective-permute-done.1.x_near
  19.4 1.1 %change.1.change_ref = f32[5,256,128]{2,1,0:T(8,128)S(1)} custom-call(f32[256,128]{1,0:T(8,128)S(1)} %get-tuple-element.22.r_ref, f32[768,128]{1,0:T(8,128)S(1)} %get-tuple-element.23.v_ref, f32[256,128]{1,0:T(8,128)S(1)} %get-tuple-element.24.p_ref, f32[5,32,128]{2,1,0:T(8,128)S(1)} %collective-permute-done.x_far, ...), custom_call_target="tpu_custom_call" | custom-call | flops 9830400000 | bytes 1048576 | tf_op jit(solution)/shard_map/change/pallas_call | solution.py:528
  20.5 1.0 %collective-permute-done.7.got_ref = f32[88,128]{1,0:T(8,128)S(1)} collective-permute-done((f32[88,128]{1,0:T(8,128)S(1)}, f32[88,128]{1,0:T(8,128)S(1)}, u32[]{:S(2)}, u32[]{:S(2)}) %collective-permute-start.7) | collective-permute-done | bytes 45088 | tf_op jit(solution)/shard_map/ppermute | solution.py:457
  21.5 2.1 %final.1 = (f32[5,256,128]{2,1,0:T(8,128)}, f32[32,64]{1,0:T(8,128)}) custom-call(f32[256,128]{1,0:T(8,128)S(1)} %get-tuple-element.22.r_ref, f32[768,128]{1,0:T(8,128)S(1)} %get-tuple-element.23.v_ref, f32[256,128]{1,0:T(8,128)S(1)} %get-tuple-element.24.p_ref, f32[5,256,128]{2,1,0:T(8,128)S(1)} %change.1.change_ref, ...), custom_call_target="tpu_custom_call" | custom-call | flops 3276800 | bytes 1048576 | tf_op jit(solution)/shard_map/final/pallas_call | solution.py:534
  (2 shorter events, 0.0 us)
Async XLA Ops:
  2.0 1.4 %collective-permute-start.2 = (f32[6,8,128]{2,1,0:T(8,128)S(1)}, f32[6,8,128]{2,1,0:T(8,128)S(1)}, u32[]{:S(2)}, u32[]{:S(2)}) collective-permute-start(f32[6,8,128]{2,1,0:T(8,128)S(1)} %get-tuple-element.27), channel_id=1, source_target_pairs={{0,8},{8,0},{16,24},{24,16},{1,9},{9,1},{17,25},{25,17},{2,10},{10... | collective-permute-start | bytes 73736 | tf_op jit(solution)/shard_map/ppermute | solution.py:457
  3.4 7.2 %collective-permute-start.3 = (f32[6,8,128]{2,1,0:T(8,128)S(1)}, f32[6,8,128]{2,1,0:T(8,128)S(1)}, u32[]{:S(2)}, u32[]{:S(2)}) collective-permute-start(f32[6,8,128]{2,1,0:T(8,128)S(1)} %get-tuple-element.32), channel_id=1, source_target_pairs={{0,24},{8,16},{16,8},{24,0},{1,25},{9,17},{17,9},{25,1},{2,26},{10... | collective-permute-start | bytes 73736 | tf_op jit(solution)/shard_map/ppermute | solution.py:462
  6.0 13.4 %collective-permute-start = (f32[5,32,128]{2,1,0:T(8,128)S(1)}, f32[5,32,128]{2,1,0:T(8,128)S(1)}, u32[]{:S(2)}, u32[]{:S(2)}) collective-permute-start(f32[5,32,128]{2,1,0:T(8,128)S(1)} %get-tuple-element.25), channel_id=1, source_target_pairs={{0,7},{1,2},{2,1},{3,4},{4,3},{5,6},{6,5},{7,0},{8,15},{9,10},{10,... | collective-permute-start | bytes 245768 | tf_op jit(solution)/shard_map/ppermute | solution.py:462
  10.5 8.8 %collective-permute-start.1 = (f32[5,32,128]{2,1,0:T(8,128)S(1)}, f32[5,32,128]{2,1,0:T(8,128)S(1)}, u32[]{:S(2)}, u32[]{:S(2)}) collective-permute-start(f32[5,32,128]{2,1,0:T(8,128)S(1)} %get-tuple-element.26), channel_id=1, source_target_pairs={{0,1},{1,0},{2,3},{3,2},{4,5},{5,4},{6,7},{7,6},{8,9},{9,8},{10,11... | collective-permute-start | bytes 245768 | tf_op jit(solution)/shard_map/ppermute | solution.py:457
  11.0 5.7 %collective-permute-start.4 = (f32[48,128]{1,0:T(8,128)S(1)}, f32[48,128]{1,0:T(8,128)S(1)}, u32[]{:S(2)}, u32[]{:S(2)}) collective-permute-start(f32[48,128]{1,0:T(8,128)S(1)} %get-tuple-element.36), channel_id=1, source_target_pairs={{0,6},{1,7},{2,4},{3,5},{4,2},{5,3},{6,0},{7,1},{8,14},{9,15},{10,... | collective-permute-start | bytes 73736 | tf_op jit(solution)/shard_map/ppermute | solution.py:457
  12.1 5.1 %collective-permute-start.5 = (f32[48,128]{1,0:T(8,128)S(1)}, f32[48,128]{1,0:T(8,128)S(1)}, u32[]{:S(2)}, u32[]{:S(2)}) collective-permute-start(f32[48,128]{1,0:T(8,128)S(1)} %get-tuple-element.37), channel_id=1, source_target_pairs={{0,4},{1,5},{2,6},{3,7},{4,0},{5,1},{6,2},{7,3},{8,12},{9,13},{10,... | collective-permute-start | bytes 73736 | tf_op jit(solution)/shard_map/ppermute | solution.py:457
  12.6 4.8 %collective-permute-start.6 = (f32[48,128]{1,0:T(8,128)S(1)}, f32[48,128]{1,0:T(8,128)S(1)}, u32[]{:S(2)}, u32[]{:S(2)}) collective-permute-start(f32[48,128]{1,0:T(8,128)S(1)} %get-tuple-element.38), channel_id=1, source_target_pairs={{0,2},{1,3},{2,0},{3,1},{4,6},{5,7},{6,4},{7,5},{8,10},{9,11},{10,... | collective-permute-start | bytes 73736 | tf_op jit(solution)/shard_map/ppermute | solution.py:457
  17.4 4.1 %collective-permute-start.7 = (f32[88,128]{1,0:T(8,128)S(1)}, f32[88,128]{1,0:T(8,128)S(1)}, u32[]{:S(2)}, u32[]{:S(2)}) collective-permute-start(f32[88,128]{1,0:T(8,128)S(1)} %merge.1), channel_id=1, source_target_pairs={{0,1},{1,0},{2,3},{3,2},{4,5},{5,4},{6,7},{7,6},{8,9},{9,8},{10,11... | collective-permute-start | bytes 135176 | tf_op jit(solution)/shard_map/ppermute | solution.py:457

commit v5 on v4

--- a/solution.py
+++ b/solution.py
@@ -23,6 +23,7 @@
 UNROLL = 64
 PACK_COST = 30_000
 PREPARE_COST = 300
+MERGE_COST = 30_000
 
 VMEM = pl.BlockSpec(memory_space=pltpu.VMEM)
 
@@ -119,12 +120,6 @@
     return (me // 2 if direct else 0), me % 2
 
 
-def layer_of(r_ref, v_ref, p_ref, at, rows):
-    total = r_ref.shape[0]
-    velocity = [v_ref[pl.ds(pl.multiple_of(k * total + at, ROWS), rows)] for k in range(3)]
-    return [r_ref[pl.ds(at, rows)], *velocity, p_ref[pl.ds(at, rows)]]
-
-
 def is_odd(axis, shape):
     return jnp.full(shape, lax.axis_index(axis) % 2) == 1
 
@@ -137,22 +132,17 @@
 
 
 def edges_kernel(
-    sizes, r_hbm, v_hbm, p_hbm, o_hbm, x_near, x_far, y_near, y_far, top_ref, r_ref, v_ref, p_ref, o_ref, sems
+    sizes, r_hbm, v_hbm, p_hbm, o_hbm, x_first, x_last, y_near, y_far, top_ref, r_ref, v_ref, p_ref, o_ref, sems
 ):
     nx, ny, nz = sizes
-    pairs = [(r_hbm, r_ref), (p_hbm, p_ref), (o_hbm, o_ref)]
-    for k in range(3):
-        component = pl.ds(k * nx * ny, nx * ny)
-        pairs.append((v_hbm.at[component], v_ref.at[component]))
+    pairs = [(r_hbm, r_ref), (v_hbm, v_ref), (p_hbm, p_ref), (o_hbm, o_ref)]
     loads = [pltpu.make_async_copy(source, target, sems.at[i]) for i, (source, target) in enumerate(pairs)]
     for load in loads:
         load.start()
     for load in loads:
         load.wait()
-    odd = lax.axis_index("slab") % 2
-    for out, end in ((x_near, 1 - odd), (x_far, odd)):
-        at = pl.multiple_of(end * ((nx - 1) * ny), ROWS)
-        for f, value in enumerate(layer_of(r_ref, v_ref, p_ref, at, ny)):
+    for out, x in ((x_first, 0), (x_last, nx - 1)):
+        for f, value in enumerate(fields_of(r_ref, v_ref, p_ref, pl.ds(x * ny, ny))):
             out[f] = value
     first, last = (fields_of(r_ref, v_ref, p_ref, pl.ds(y, nx, ny)) for y in (0, ny - 1))
     far, near = sides(last, first, "sect")
@@ -213,10 +203,11 @@
     target_ref[...] = jnp.broadcast_to(owner * msg.slots + rank, target_ref.shape)
 
 
-def pack_kernel(sizes, msg, n_far, direct, cell_ref, change_ref, target_ref, y_near, y_far, top_ref, *rest):
+def pack_kernel(sizes, msg, n_far, direct, cell_ref, change_ref, target_ref, y_near, y_far, top_ref, x_first, *rest):
     nx, ny, nz = sizes
     slots, group, width = msg.slots, msg.group, spread_rows(msg)
-    far, outs, spread = rest[:n_far], rest[n_far:-1], rest[-1]
+    far, x_out, outs, spread = rest[:n_far], rest[n_far], rest[n_far + 1 : -1], rest[-1]
+    x_out[...] = x_first[...]
     y_low, y_high = sides([y_near[f] for f in range(FIELDS)], [y_far[f] for f in range(FIELDS)], "sect")
     columns = ny * (nz // STRIDE)
     step = STRIDE // ROWS
@@ -285,10 +276,11 @@
             out[pl.ds((d + 1) * per - ROWS, ROWS), :] = top
 
 
-def merge_kernel(msg, firsts, *refs):
-    out = refs[-1]
+def merge_kernel(msg, firsts, x_low, *refs):
+    *refs, x_out, out = refs
+    x_out[...] = x_low[...]
     half, top = msg.owners // 2, None
-    for first, ref in zip(firsts, refs[:-1]):
+    for first, ref in zip(firsts, refs):
         for d in range(ref.shape[0] // msg.count):
             at, to = d * msg.count, first + d
             out[pl.ds(to * msg.rows, msg.rows), :] = ref[pl.ds(at + msg.rows, msg.rows), :]
@@ -300,10 +292,9 @@
     out[pl.ds(half * (msg.rows + msg.extra_rows), ROWS), :] = top
 
 
-def change_kernel(sizes, r_ref, v_ref, p_ref, x_far, x_near, y_near, y_far, out_ref):
+def change_kernel(sizes, r_ref, v_ref, p_ref, x_low, x_high, y_near, y_far, out_ref):
     nx, ny, nz = sizes
     every = range(FIELDS)
-    x_low, x_high = sides([x_near[f] for f in every], [x_far[f] for f in every], "slab")
     y_low, y_high = sides([y_near[f] for f in every], [y_far[f] for f in every], "sect")
     row = lax.broadcasted_iota(jnp.int32, (ny, nz), 0)
     half = 0.5
@@ -482,12 +473,12 @@
     x_edge, y_edge, row = (FIELDS, ny, nz), (FIELDS + 1, nx, nz), (ROWS, nz)
     owners = jnp.transpose(owners, (1, 2, 0))
     shapes = [(a.shape, a.dtype) for a in (*gas, owners)]
-    x_near, x_far, y_near, y_far, top, *gas, owners = call(
+    x_first, x_last, y_near, y_far, top, *gas, owners = call(
         functools.partial(edges_kernel, sizes),
         [x_edge, x_edge, y_edge, (FIELDS, nx, nz), row, *shapes],
         "edges",
         20 * cells,
-        [pltpu.SemaphoreType.DMA((6,))],
+        [pltpu.SemaphoreType.DMA((4,))],
         in_specs=[HBM] * 4,
     )(*(pltpu.with_memory_space_constraint(a, pltpu.HBM) for a in (*gas, owners)))
     tiles = (STRIDE // ROWS, FIELDS, nx, nz)
@@ -501,16 +492,15 @@
     y_far, target = call(join_kernel, [y_edge, (ROWS, columns)], "join", cells)(y_far, top, y_near, target)
     y_far = to_other(y_far, "sect")
     far = [around(top, "sect", d) for d in range(2, n_sect - 1)] if n_sect > 4 else []
-    x_near = to_partner(x_near, "slab", 1)
-    x_far = to_other(x_far, "slab")
+    x_low = around(x_last, "slab", 1)
     firsts = range(half) if direct else range(1)
-    packed = call(
+    x_first, *packed = call(
         functools.partial(pack_kernel, sizes, geometry, len(far), direct),
-        [(half // len(firsts) * geometry.count, LANES)] * len(firsts),
+        [x_edge] + [(half // len(firsts) * geometry.count, LANES)] * len(firsts),
         "pack",
         PACK_COST * cells,
         [pltpu.VMEM((group * spread_rows(geometry), columns), jnp.float32)],
-    )(cells_at, change_at, target, y_near, y_far, top, *far)
+    )(cells_at, change_at, target, y_near, y_far, top, x_first, *far)
     if direct:
         arrived = [to_partner(m, "slab", 2 * d) if d else m for d, m in zip(firsts, packed)]
     else:
@@ -518,19 +508,20 @@
         arrived = [
             lax.all_to_all(m, "slab", split_axis=0, concat_axis=0, axis_index_groups=alike, tiled=True) for m in packed
         ]
-    (merged,) = call(
-        functools.partial(merge_kernel, geometry, firsts[::-1]),
-        [(half * (geometry.rows + geometry.extra_rows) + ROWS, LANES)],
+    x_low, merged = call(
+        functools.partial(merge_kernel, geometry, [firsts[i] for i in [2, 3, 1, 0]] if direct else firsts),
+        [x_edge, (half * (geometry.rows + geometry.extra_rows) + ROWS, LANES)],
         "merge",
-        cells,
-    )(*arrived[::-1])
+        MERGE_COST * cells,
+    )(x_low, *([arrived[i] for i in [2, 3, 1, 0]] if direct else arrived))
     got = to_partner(merged, "slab", 1)
+    x_high = around(x_first, "slab", -1)
     (change,) = call(
         functools.partial(change_kernel, sizes),
         [(FIELDS, nx * ny, nz)],
         "change",
         300_000 * cells,
-    )(*gas, x_far, x_near, y_near, y_far)
+    )(*gas, x_low, x_high, y_near, y_far)
     new_state, depth = call(
         functools.partial(final_kernel, sizes, geometry, firsts, direct),
         [(FIELDS, nx * ny, nz), (slots, length)],

time: 23.8 us -> 23.1 us (0.971)
  waiting for transfers between devices: 3.12 us -> 2.02 us
  starting transfers between devices: 14.1 us -> 14.7 us
    ppermute x0 -> x2, starting transfers between devices: none -> 5.4 us  [around(): lax.ppermute(value, axis, [(i, (i + amount) % count) for i in range(count)])]
    ppermute x2 -> x1, starting transfers between devices: 7.16 us -> 2.6 us  [to_other(): lax.ppermute(value, axis, [(i, (i + 2 * (i % 2) - 1) % count) for i in ra...]
    ppermute x6 -> x5, waiting for transfers between devices: 3.11 us -> 1.73 us  [to_partner(): lax.ppermute(value, axis, [(i, i ^ bits) for i in range(lax.axis_size(axi...]
    ppermute x0 -> x2, waiting for transfers between devices: none -> 0.29 us  [around(): lax.ppermute(value, axis, [(i, (i + amount) % count) for i in range(count)])]
    ppermute x6 -> x5, starting transfers between devices: 6.95 us -> 6.69 us  [to_partner(): lax.ppermute(value, axis, [(i, i ^ bits) for i in range(lax.axis_size(axi...]
  transfers between devices with their start and end apart: 8 -> 8, of which waited for: 5 -> 4; matrix products, arithmetic and copies ran while one was open for 0% -> 0% of each run, Pallas kernels for 9% -> 10%
where the time goes in v5:
time: 23.1 us; the launch traced here: 23 us
  starting transfers between devices  14.7 us (64%)
  Pallas kernels  5.6 us (24%)
  waiting for transfers between devices  2.02 us (9%)
  between operations  0.66 us (3%)
    ppermute x5, starting transfers between devices, to_partner(): lax.ppermute(value, axis, [(i, i ^ bits) for i in range(lax.axis_size(axi...  6.69 us
    ppermute x2, starting transfers between devices, around(): lax.ppermute(value, axis, [(i, (i + amount) % count) for i in range(count)])  5.4 us
    ppermute x1, starting transfers between devices, to_other(): lax.ppermute(value, axis, [(i, (i + 2 * (i % 2) - 1) % count) for i in ra...  2.6 us
    pallas_call x1, Pallas kernels, body(): call(functools.partial(final_kernel, sizes, geometry, firsts, direct), [(...  2.14 us
    ppermute x5, waiting for transfers between devices, to_partner(): lax.ppermute(value, axis, [(i, i ^ bits) for i in range(lax.axis_size(axi...  1.73 us
    pallas_call x1, Pallas kernels, body(): call(functools.partial(edges_kernel, sizes), [x_edge, x_edge, y_edge, (FI...  1.24 us
    pallas_call x1, Pallas kernels, body(): call(functools.partial(change_kernel, sizes), [(FIELDS, nx * ny, nz)], 'c...  1.11 us
    pallas_call x1, Pallas kernels, body(): call(functools.partial(prepare_kernel, sizes, geometry), [tiles, tiles, (...  0.61 us
  transfers between devices with their start and end apart: 8, of which 4 were waited for; matrix products, arithmetic and copies ran while one was open for 0% of the time, Pallas kernels for 10%

profile of v5, /device:TPU:0, one launch (start us, length us, event | category | flops | bytes accessed | tf_op | source)
XLA Modules:
  0.0 23.0 jit_solution(9990471995108928656)
XLA Ops:
  0.6 1.2 %edges.1 = (f32[5,32,128]{2,1,0:T(8,128)S(1)}, f32[5,32,128]{2,1,0:T(8,128)S(1)}, f32[6,8,128]{2,1,0:T(8,128)S(1)}, f32[5,8,128]{2,1,0:T(8,128)S(1)}, f32[8,128]...) custom-call(f32[256,128]{1,0:T(8,128)} %bitcast.7, ...), custom_call_target="tpu_custom_call" | custom-call | flops 655360 | bytes 1048576 | tf_op jit(solution)/shard_map/edges/pallas_call | solution.py:476
  1.9 0.5 %collective-permute-start.1 = (f32[6,8,128]{2,1,0:T(8,128)S(1)}, f32[6,8,128]{2,1,0:T(8,128)S(1)}, u32[]{:S(2)}, u32[]{:S(2)}) collective-permute-start(f32[6,8,128]{2,1,0:T(8,128)S(1)} %get-tuple-element.34), channel_id=1, source_target_pairs={{0,8},{8,0},{16,24},{24,16},{1,9},{9,1},{17,25},{25,17},{2,10},{10... | collective-permute-start | bytes 73736 | tf_op jit(solution)/shard_map/ppermute | solution.py:448
  2.4 0.6 %prepare.1 = (f32[4,5,8,128]{3,2,1,0:T(8,128)S(1)}, f32[4,5,8,128]{3,2,1,0:T(8,128)S(1)}, f32[8,128]{1,0:T(8,128)S(1)}) custom-call(f32[256,128]{1,0:T(8,128)S(1)} %get-tuple-element.25.r_ref, f32[768,128]{1,0:T(8,128)S(1)} %get-tuple-element.26.v_ref, f32[256,128]{1,0:T(8,128)S(1)} %get-tuple-element.27.p_ref, s32[4,1,32]{2,1,0:T(1,128)S(1)} %get-tuple-element.29.owner_ref), custom_call_target="tpu_custom_call" | custom-call | flops 9830400 | bytes 1048576 | tf_op jit(solution)/shard_map/prepare/pallas_call | solution.py:485
  3.0 0.2 %collective-permute-done.1.near_ref.y_near = f32[6,8,128]{2,1,0:T(8,128)S(1)} collective-permute-done((f32[6,8,128]{2,1,0:T(8,128)S(1)}, f32[6,8,128]{2,1,0:T(8,128)S(1)}, u32[]{:S(2)}, u32[]{:S(2)}) %collective-permute-start.1) | collective-permute-done | bytes 24608 | tf_op jit(solution)/shard_map/ppermute | solution.py:448
  3.3 2.6 %collective-permute-start.2 = (f32[6,8,128]{2,1,0:T(8,128)S(1)}, f32[6,8,128]{2,1,0:T(8,128)S(1)}, u32[]{:S(2)}, u32[]{:S(2)}) collective-permute-start(f32[6,8,128]{2,1,0:T(8,128)S(1)} %get-tuple-element.37), channel_id=1, source_target_pairs={{0,24},{8,16},{16,8},{24,0},{1,25},{9,17},{17,9},{25,1},{2,26},{10... | collective-permute-start | bytes 73736 | tf_op jit(solution)/shard_map/ppermute | solution.py:453
  5.9 1.5 %collective-permute-start = (f32[5,32,128]{2,1,0:T(8,128)S(1)}, f32[5,32,128]{2,1,0:T(8,128)S(1)}, u32[]{:S(2)}, u32[]{:S(2)}) collective-permute-start(f32[5,32,128]{2,1,0:T(8,128)S(1)} %get-tuple-element.28), channel_id=1, source_target_pairs={{0,1},{1,2},{2,3},{3,4},{4,5},{5,6},{6,7},{7,0},{8,9},{9,10},{10,1... | collective-permute-start | bytes 245768 | tf_op jit(solution)/shard_map/ppermute | solution.py:444
  7.4 0.0 collective-permute-done.2.y_far
  7.4 0.5 %pack.1 = (f32[5,32,128]{2,1,0:T(8,128)S(1)}, f32[48,128]{1,0:T(8,128)S(1)}, f32[48,128]{1,0:T(8,128)S(1)}, f32[48,128]{1,0:T(8,128)S(1)}, f32[48,128]{1,0:T(8,128)S(1)}) custom-call(f32[4,5,8,128]{3,2,1,0:T(8,128)S(1)} %get-tuple-element.30.cell_ref, f32[4,5,8,128]{3,2,1,0:T(8,128)S(1)} %get-tuple-element.31.change_ref, ...), custom_call_target="tpu_custom_call" | custom-call | flops 983040000 | bytes 1048576 | tf_op jit(solution)/shard_map/pack/pallas_call | solution.py:497
  7.9 3.1 %collective-permute-start.3 = (f32[48,128]{1,0:T(8,128)S(1)}, f32[48,128]{1,0:T(8,128)S(1)}, u32[]{:S(2)}, u32[]{:S(2)}) collective-permute-start(f32[48,128]{1,0:T(8,128)S(1)} %get-tuple-element.39), channel_id=1, source_target_pairs={{0,4},{1,5},{2,6},{3,7},{4,0},{5,1},{6,2},{7,3},{8,12},{9,13},{10,... | collective-permute-start | bytes 73736 | tf_op jit(solution)/shard_map/ppermute | solution.py:448
  11.0 1.3 %collective-permute-start.4 = (f32[48,128]{1,0:T(8,128)S(1)}, f32[48,128]{1,0:T(8,128)S(1)}, u32[]{:S(2)}, u32[]{:S(2)}) collective-permute-start(f32[48,128]{1,0:T(8,128)S(1)} %get-tuple-element.40), channel_id=1, source_target_pairs={{0,6},{1,7},{2,4},{3,5},{4,2},{5,3},{6,0},{7,1},{8,14},{9,15},{10,... | collective-permute-start | bytes 73736 | tf_op jit(solution)/shard_map/ppermute | solution.py:448
  12.3 0.2 %collective-permute-start.5 = (f32[48,128]{1,0:T(8,128)S(1)}, f32[48,128]{1,0:T(8,128)S(1)}, u32[]{:S(2)}, u32[]{:S(2)}) collective-permute-start(f32[48,128]{1,0:T(8,128)S(1)} %get-tuple-element.41), channel_id=1, source_target_pairs={{0,2},{1,3},{2,0},{3,1},{4,6},{5,7},{6,4},{7,5},{8,10},{9,11},{10,... | collective-permute-start | bytes 73736 | tf_op jit(solution)/shard_map/ppermute | solution.py:448
  12.5 3.9 %collective-permute-start.6 = (f32[5,32,128]{2,1,0:T(8,128)S(1)}, f32[5,32,128]{2,1,0:T(8,128)S(1)}, u32[]{:S(2)}, u32[]{:S(2)}) collective-permute-start(f32[5,32,128]{2,1,0:T(8,128)S(1)} %get-tuple-element.44), channel_id=1, source_target_pairs={{0,7},{1,0},{2,1},{3,2},{4,3},{5,4},{6,5},{7,6},{8,15},{9,8},{10,9... | collective-permute-start | bytes 245768 | tf_op jit(solution)/shard_map/ppermute | solution.py:444
  16.4 0.0 collective-permute-done.3.refs_0_.rest_2_
  16.4 0.3 %collective-permute-done.4.refs_1_.rest_3_ = f32[48,128]{1,0:T(8,128)S(1)} collective-permute-done((f32[48,128]{1,0:T(8,128)S(1)}, f32[48,128]{1,0:T(8,128)S(1)}, u32[]{:S(2)}, u32[]{:S(2)}) %collective-permute-start.4) | collective-permute-done | bytes 24608 | tf_op jit(solution)/shard_map/ppermute | solution.py:448
  16.7 0.0 collective-permute-done.5.refs_2_.rest_1_
  16.7 0.0 collective-permute-done.x_low
  16.7 1.5 %collective-permute-start.7 = (f32[88,128]{1,0:T(8,128)S(1)}, f32[88,128]{1,0:T(8,128)S(1)}, u32[]{:S(2)}, u32[]{:S(2)}) collective-permute-start(f32[88,128]{1,0:T(8,128)S(1)} %get-tuple-element.45), channel_id=1, source_target_pairs={{0,1},{1,0},{2,3},{3,2},{4,5},{5,4},{6,7},{7,6},{8,9},{9,8},{10,11... | collective-permute-start | bytes 135176 | tf_op jit(solution)/shard_map/ppermute | solution.py:448
  18.2 0.3 %collective-permute-done.6.x_high = f32[5,32,128]{2,1,0:T(8,128)S(1)} collective-permute-done((f32[5,32,128]{2,1,0:T(8,128)S(1)}, f32[5,32,128]{2,1,0:T(8,128)S(1)}, u32[]{:S(2)}, u32[]{:S(2)}) %collective-permute-start.6) | collective-permute-done | bytes 81952 | tf_op jit(solution)/shard_map/ppermute | solution.py:444
  18.5 1.1 %change.1.change_ref = f32[5,256,128]{2,1,0:T(8,128)S(1)} custom-call(f32[256,128]{1,0:T(8,128)S(1)} %get-tuple-element.25.r_ref, f32[768,128]{1,0:T(8,128)S(1)} %get-tuple-element.26.v_ref, f32[256,128]{1,0:T(8,128)S(1)} %get-tuple-element.27.p_ref, f32[5,32,128]{2,1,0:T(8,128)S(1)} %get-tuple-element.43.x_low, ...), custom_call_target="tpu_custom_call" | custom-call | flops 9830400000 | bytes 1048576 | tf_op jit(solution)/shard_map/change/pallas_call | solution.py:519
  19.6 1.2 %collective-permute-done.7.got_ref = f32[88,128]{1,0:T(8,128)S(1)} collective-permute-done((f32[88,128]{1,0:T(8,128)S(1)}, f32[88,128]{1,0:T(8,128)S(1)}, u32[]{:S(2)}, u32[]{:S(2)}) %collective-permute-start.7) | collective-permute-done | bytes 45088 | tf_op jit(solution)/shard_map/ppermute | solution.py:448
  20.8 2.1 %final.1 = (f32[5,256,128]{2,1,0:T(8,128)}, f32[32,64]{1,0:T(8,128)}) custom-call(f32[256,128]{1,0:T(8,128)S(1)} %get-tuple-element.25.r_ref, f32[768,128]{1,0:T(8,128)S(1)} %get-tuple-element.26.v_ref, f32[256,128]{1,0:T(8,128)S(1)} %get-tuple-element.27.p_ref, f32[5,256,128]{2,1,0:T(8,128)S(1)} %change.1.change_ref, ...), custom_call_target="tpu_custom_call" | custom-call | flops 3276800 | bytes 1048576 | tf_op jit(solution)/shard_map/final/pallas_call | solution.py:525
  (2 shorter events, 0.0 us)
Async XLA Ops:
  1.9 1.4 %collective-permute-start.1 = (f32[6,8,128]{2,1,0:T(8,128)S(1)}, f32[6,8,128]{2,1,0:T(8,128)S(1)}, u32[]{:S(2)}, u32[]{:S(2)}) collective-permute-start(f32[6,8,128]{2,1,0:T(8,128)S(1)} %get-tuple-element.34), channel_id=1, source_target_pairs={{0,8},{8,0},{16,24},{24,16},{1,9},{9,1},{17,25},{25,17},{2,10},{10... | collective-permute-start | bytes 73736 | tf_op jit(solution)/shard_map/ppermute | solution.py:448
  3.3 4.1 %collective-permute-start.2 = (f32[6,8,128]{2,1,0:T(8,128)S(1)}, f32[6,8,128]{2,1,0:T(8,128)S(1)}, u32[]{:S(2)}, u32[]{:S(2)}) collective-permute-start(f32[6,8,128]{2,1,0:T(8,128)S(1)} %get-tuple-element.37), channel_id=1, source_target_pairs={{0,24},{8,16},{16,8},{24,0},{1,25},{9,17},{17,9},{25,1},{2,26},{10... | collective-permute-start | bytes 73736 | tf_op jit(solution)/shard_map/ppermute | solution.py:453
  5.9 10.8 %collective-permute-start = (f32[5,32,128]{2,1,0:T(8,128)S(1)}, f32[5,32,128]{2,1,0:T(8,128)S(1)}, u32[]{:S(2)}, u32[]{:S(2)}) collective-permute-start(f32[5,32,128]{2,1,0:T(8,128)S(1)} %get-tuple-element.28), channel_id=1, source_target_pairs={{0,1},{1,2},{2,3},{3,4},{4,5},{5,6},{6,7},{7,0},{8,9},{9,10},{10,1... | collective-permute-start | bytes 245768 | tf_op jit(solution)/shard_map/ppermute | solution.py:444
  7.9 8.6 %collective-permute-start.3 = (f32[48,128]{1,0:T(8,128)S(1)}, f32[48,128]{1,0:T(8,128)S(1)}, u32[]{:S(2)}, u32[]{:S(2)}) collective-permute-start(f32[48,128]{1,0:T(8,128)S(1)} %get-tuple-element.39), channel_id=1, source_target_pairs={{0,4},{1,5},{2,6},{3,7},{4,0},{5,1},{6,2},{7,3},{8,12},{9,13},{10,... | collective-permute-start | bytes 73736 | tf_op jit(solution)/shard_map/ppermute | solution.py:448
  11.0 5.7 %collective-permute-start.4 = (f32[48,128]{1,0:T(8,128)S(1)}, f32[48,128]{1,0:T(8,128)S(1)}, u32[]{:S(2)}, u32[]{:S(2)}) collective-permute-start(f32[48,128]{1,0:T(8,128)S(1)} %get-tuple-element.40), channel_id=1, source_target_pairs={{0,6},{1,7},{2,4},{3,5},{4,2},{5,3},{6,0},{7,1},{8,14},{9,15},{10,... | collective-permute-start | bytes 73736 | tf_op jit(solution)/shard_map/ppermute | solution.py:448
  12.3 4.4 %collective-permute-start.5 = (f32[48,128]{1,0:T(8,128)S(1)}, f32[48,128]{1,0:T(8,128)S(1)}, u32[]{:S(2)}, u32[]{:S(2)}) collective-permute-start(f32[48,128]{1,0:T(8,128)S(1)} %get-tuple-element.41), channel_id=1, source_target_pairs={{0,2},{1,3},{2,0},{3,1},{4,6},{5,7},{6,4},{7,5},{8,10},{9,11},{10,... | collective-permute-start | bytes 73736 | tf_op jit(solution)/shard_map/ppermute | solution.py:448
  12.5 5.9 %collective-permute-start.6 = (f32[5,32,128]{2,1,0:T(8,128)S(1)}, f32[5,32,128]{2,1,0:T(8,128)S(1)}, u32[]{:S(2)}, u32[]{:S(2)}) collective-permute-start(f32[5,32,128]{2,1,0:T(8,128)S(1)} %get-tuple-element.44), channel_id=1, source_target_pairs={{0,7},{1,0},{2,1},{3,2},{4,3},{5,4},{6,5},{7,6},{8,15},{9,8},{10,9... | collective-permute-start | bytes 245768 | tf_op jit(solution)/shard_map/ppermute | solution.py:444
  16.7 4.1 %collective-permute-start.7 = (f32[88,128]{1,0:T(8,128)S(1)}, f32[88,128]{1,0:T(8,128)S(1)}, u32[]{:S(2)}, u32[]{:S(2)}) collective-permute-start(f32[88,128]{1,0:T(8,128)S(1)} %get-tuple-element.45), channel_id=1, source_target_pairs={{0,1},{1,0},{2,3},{3,2},{4,5},{5,4},{6,7},{7,6},{8,9},{9,8},{10,11... | collective-permute-start | bytes 135176 | tf_op jit(solution)/shard_map/ppermute | solution.py:448

commit v6 on v5

--- a/solution.py
+++ b/solution.py
@@ -237,7 +237,7 @@
         own_of = 2 * ((block // 2) ^ z_me) + ((block % 2) ^ y_me)
         out = []
         for h in range(group):
-            slot = (own_of * slots + h * msg.rows + first + row % rows).astype(jnp.float32)
+            slot = (own_of * slots + (first + row % rows) * group + h).astype(jnp.float32)
             out.append(jnp.where(slot == target, 1.0, 0.0))
         return jnp.concatenate(out, axis=1).astype(jnp.bfloat16)
 
@@ -247,13 +247,11 @@
         for _ in range(3):
             out.append(value.astype(jnp.bfloat16))
             value = value - out[-1].astype(jnp.float32)
-        return out
+        return jnp.concatenate(out, axis=1)
 
     def pick(selection, values):
-        parts = [
-            lax.dot_general(selection, v, (((1,), (1,)), ((), ())), preferred_element_type=jnp.float32) for v in values
-        ]
-        return (parts[0] + parts[1]) + parts[2]
+        selection = jnp.concatenate([selection] * 3, axis=1)
+        return lax.dot_general(selection, values, (((1,), (1,)), ((), ())), preferred_element_type=jnp.float32)
 
     per = msg.count
     each = msg.owners // len(outs)
@@ -396,43 +394,61 @@
     scaled = inverse * math.sqrt(math.log2(math.e))
     centre = (BAND / 8.0) * (new[1] / density)
     turns = BAND // length
-    strides = [scaled * float(length * m) for m in range(turns)]
-
     block = min(length, UNROLL)
 
-    def offsets(count, running):
-        e = (length - block - block * count) * 1.0 - float(BAND // 2)
-        for b in range(block):
-            start = (e + float(b) - centre) * scaled
-            total = None
-            for m in range(turns):
-                t = start + strides[m] if m else start
-                value = jnp.exp2(-(t * t))
-                total = value if total is None else total + value
-            part = shift(amplitude * total, b * group, 1)
-            block_sum = part if b == 0 else block_sum + part
-        return block_sum if running is None else shift(running, block * group, 1) + block_sum
-
-    if length == block:
-        running = offsets(0, None)
+    def skewers(rows):
+        scale, middle, size = scaled[:rows], centre[:rows], amplitude[:rows]
+        strides = [scale * float(length * m) for m in range(turns)]
+
+        def offsets(count, running):
+            e = (length - block - block * count) * 1.0 - float(BAND // 2)
+            for b in range(block):
+                start = (e + float(b) - middle) * scale
+                total = None
+                for m in range(turns):
+                    t = start + strides[m] if m else start
+                    value = jnp.exp2(-(t * t))
+                    total = value if total is None else total + value
+                part = shift(size * total, b * group, 1)
+                block_sum = part if b == 0 else block_sum + part
+            return block_sum if running is None else shift(running, block * group, 1) + block_sum
+
+        if length == block:
+            running = offsets(0, None)
+        else:
+            running = lax.fori_loop(
+                0,
+                length // block,
+                lambda i, c: offsets(i.astype(jnp.float32), c),
+                jnp.zeros_like(size),
+            )
+        running = shift(running, -(BAND // 2) * group, 1)
+        if group > 1:
+            wide = jnp.broadcast_to(running[:, None, :], (rows, group, group * length))
+            wide = wide.reshape(rows * group, group * length)
+            at = lax.broadcasted_iota(jnp.int32, wide.shape, 1)
+            of = lax.broadcasted_iota(jnp.int32, wide.shape, 0)
+            wide = jnp.where(at % group == of % group, wide, 0.0)
+            at = lax.broadcasted_iota(jnp.int32, (group * length, length), 0)
+            of = lax.broadcasted_iota(jnp.int32, (group * length, length), 1)
+            pick = jnp.where(at // group == of, 1.0, 0.0)
+            running = jnp.dot(wide, pick, precision=lax.Precision.HIGHEST, preferred_element_type=jnp.float32)
+        depth_ref[pl.ds(0, rows * group), :] = running
+
+    if msg.rows > ROWS:
+        more = jnp.max(jnp.where(taken[ROWS:], 1.0, 0.0)) > 0.0
+
+        @pl.when(more)
+        def _():
+            skewers(msg.rows)
+
+        @pl.when(jnp.logical_not(more))
+        def _():
+            depth_ref[...] = jnp.zeros_like(depth_ref)
+            skewers(ROWS)
+
     else:
-        running = lax.fori_loop(
-            0,
-            length // block,
-            lambda i, c: offsets(i.astype(jnp.float32), c),
-            jnp.zeros_like(amplitude),
-        )
-    running = shift(running, -(BAND // 2) * group, 1)
-    if group == 1:
-        depth_ref[...] = running
-    else:
-        at = lax.broadcasted_iota(jnp.int32, (group * length, length), 0)
-        cell_of = lax.broadcasted_iota(jnp.int32, (group * length, length), 1)
-        for h in range(group):
-            pick = jnp.where(at == cell_of * group + h, 1.0, 0.0)
-            depth_ref[pl.ds(h * msg.rows, msg.rows), :] = jnp.dot(
-                running, pick, precision=lax.Precision.HIGHEST, preferred_element_type=jnp.float32
-            )
+        skewers(msg.rows)
     writes.append(pltpu.make_async_copy(depth_ref, depth_hbm, sems.at[nx]))
     writes[-1].start()
     for write in writes:

time: 23.1 us -> 22.7 us (0.983)
  Pallas kernels: 5.6 us -> 5.21 us
    pallas_call x1, Pallas kernels: 2.14 us -> 1.75 us  [body(): call(functools.partial(final_kernel, sizes, geometry, firsts, direct), [(...]
where the time goes in v6:
time: 22.7 us; the launch traced here: 22.6 us
  starting transfers between devices  14.7 us (65%)
  Pallas kernels  5.21 us (23%)
  waiting for transfers between devices  2.02 us (9%)
  between operations  0.66 us (3%)
    ppermute x5, starting transfers between devices, to_partner(): lax.ppermute(value, axis, [(i, i ^ bits) for i in range(lax.axis_size(axi...  6.69 us
    ppermute x2, starting transfers between devices, around(): lax.ppermute(value, axis, [(i, (i + amount) % count) for i in range(count)])  5.4 us
    ppermute x1, starting transfers between devices, to_other(): lax.ppermute(value, axis, [(i, (i + 2 * (i % 2) - 1) % count) for i in ra...  2.6 us
    pallas_call x1, Pallas kernels, body(): call(functools.partial(final_kernel, sizes, geometry, firsts, direct), [(...  1.75 us
    ppermute x5, waiting for transfers between devices, to_partner(): lax.ppermute(value, axis, [(i, i ^ bits) for i in range(lax.axis_size(axi...  1.73 us
    pallas_call x1, Pallas kernels, body(): call(functools.partial(edges_kernel, sizes), [x_edge, x_edge, y_edge, (FI...  1.24 us
    pallas_call x1, Pallas kernels, body(): call(functools.partial(change_kernel, sizes), [(FIELDS, nx * ny, nz)], 'c...  1.11 us
    pallas_call x1, Pallas kernels, body(): call(functools.partial(prepare_kernel, sizes, geometry), [tiles, tiles, (...  0.61 us
  transfers between devices with their start and end apart: 8, of which 4 were waited for; matrix products, arithmetic and copies ran while one was open for 0% of the time, Pallas kernels for 10%

profile of v6, /device:TPU:0, one launch (start us, length us, event | category | flops | bytes accessed | tf_op | source)
XLA Modules:
  0.0 22.6 jit_solution(12442337399313851901)
XLA Ops:
  0.6 1.2 %edges.1 = (f32[5,32,128]{2,1,0:T(8,128)S(1)}, f32[5,32,128]{2,1,0:T(8,128)S(1)}, f32[6,8,128]{2,1,0:T(8,128)S(1)}, f32[5,8,128]{2,1,0:T(8,128)S(1)}, f32[8,128]...) custom-call(f32[256,128]{1,0:T(8,128)} %bitcast.7, ...), custom_call_target="tpu_custom_call" | custom-call | flops 655360 | bytes 1048576 | tf_op jit(solution)/shard_map/edges/pallas_call | solution.py:492
  1.9 0.5 %collective-permute-start.1 = (f32[6,8,128]{2,1,0:T(8,128)S(1)}, f32[6,8,128]{2,1,0:T(8,128)S(1)}, u32[]{:S(2)}, u32[]{:S(2)}) collective-permute-start(f32[6,8,128]{2,1,0:T(8,128)S(1)} %get-tuple-element.34), channel_id=1, source_target_pairs={{0,8},{8,0},{16,24},{24,16},{1,9},{9,1},{17,25},{25,17},{2,10},{10... | collective-permute-start | bytes 73736 | tf_op jit(solution)/shard_map/ppermute | solution.py:464
  2.4 0.6 %prepare.1 = (f32[4,5,8,128]{3,2,1,0:T(8,128)S(1)}, f32[4,5,8,128]{3,2,1,0:T(8,128)S(1)}, f32[8,128]{1,0:T(8,128)S(1)}) custom-call(f32[256,128]{1,0:T(8,128)S(1)} %get-tuple-element.25.r_ref, f32[768,128]{1,0:T(8,128)S(1)} %get-tuple-element.26.v_ref, f32[256,128]{1,0:T(8,128)S(1)} %get-tuple-element.27.p_ref, s32[4,1,32]{2,1,0:T(1,128)S(1)} %get-tuple-element.29.owner_ref), custom_call_target="tpu_custom_call" | custom-call | flops 9830400 | bytes 1048576 | tf_op jit(solution)/shard_map/prepare/pallas_call | solution.py:501
  3.0 0.2 %collective-permute-done.1.near_ref.y_near = f32[6,8,128]{2,1,0:T(8,128)S(1)} collective-permute-done((f32[6,8,128]{2,1,0:T(8,128)S(1)}, f32[6,8,128]{2,1,0:T(8,128)S(1)}, u32[]{:S(2)}, u32[]{:S(2)}) %collective-permute-start.1) | collective-permute-done | bytes 24608 | tf_op jit(solution)/shard_map/ppermute | solution.py:464
  3.3 2.6 %collective-permute-start.2 = (f32[6,8,128]{2,1,0:T(8,128)S(1)}, f32[6,8,128]{2,1,0:T(8,128)S(1)}, u32[]{:S(2)}, u32[]{:S(2)}) collective-permute-start(f32[6,8,128]{2,1,0:T(8,128)S(1)} %get-tuple-element.37), channel_id=1, source_target_pairs={{0,24},{8,16},{16,8},{24,0},{1,25},{9,17},{17,9},{25,1},{2,26},{10... | collective-permute-start | bytes 73736 | tf_op jit(solution)/shard_map/ppermute | solution.py:469
  5.9 1.5 %collective-permute-start = (f32[5,32,128]{2,1,0:T(8,128)S(1)}, f32[5,32,128]{2,1,0:T(8,128)S(1)}, u32[]{:S(2)}, u32[]{:S(2)}) collective-permute-start(f32[5,32,128]{2,1,0:T(8,128)S(1)} %get-tuple-element.28), channel_id=1, source_target_pairs={{0,1},{1,2},{2,3},{3,4},{4,5},{5,6},{6,7},{7,0},{8,9},{9,10},{10,1... | collective-permute-start | bytes 245768 | tf_op jit(solution)/shard_map/ppermute | solution.py:460
  7.4 0.0 collective-permute-done.2.y_far
  7.4 0.5 %pack.1 = (f32[5,32,128]{2,1,0:T(8,128)S(1)}, f32[48,128]{1,0:T(8,128)S(1)}, f32[48,128]{1,0:T(8,128)S(1)}, f32[48,128]{1,0:T(8,128)S(1)}, f32[48,128]{1,0:T(8,128)S(1)}) custom-call(f32[4,5,8,128]{3,2,1,0:T(8,128)S(1)} %get-tuple-element.30.cell_ref, f32[4,5,8,128]{3,2,1,0:T(8,128)S(1)} %get-tuple-element.31.change_ref, ...), custom_call_target="tpu_custom_call" | custom-call | flops 983040000 | bytes 1048576 | tf_op jit(solution)/shard_map/pack/pallas_call | solution.py:513
  7.9 3.1 %collective-permute-start.3 = (f32[48,128]{1,0:T(8,128)S(1)}, f32[48,128]{1,0:T(8,128)S(1)}, u32[]{:S(2)}, u32[]{:S(2)}) collective-permute-start(f32[48,128]{1,0:T(8,128)S(1)} %get-tuple-element.39), channel_id=1, source_target_pairs={{0,4},{1,5},{2,6},{3,7},{4,0},{5,1},{6,2},{7,3},{8,12},{9,13},{10,... | collective-permute-start | bytes 73736 | tf_op jit(solution)/shard_map/ppermute | solution.py:464
  11.0 1.3 %collective-permute-start.4 = (f32[48,128]{1,0:T(8,128)S(1)}, f32[48,128]{1,0:T(8,128)S(1)}, u32[]{:S(2)}, u32[]{:S(2)}) collective-permute-start(f32[48,128]{1,0:T(8,128)S(1)} %get-tuple-element.40), channel_id=1, source_target_pairs={{0,6},{1,7},{2,4},{3,5},{4,2},{5,3},{6,0},{7,1},{8,14},{9,15},{10,... | collective-permute-start | bytes 73736 | tf_op jit(solution)/shard_map/ppermute | solution.py:464
  12.3 0.2 %collective-permute-start.5 = (f32[48,128]{1,0:T(8,128)S(1)}, f32[48,128]{1,0:T(8,128)S(1)}, u32[]{:S(2)}, u32[]{:S(2)}) collective-permute-start(f32[48,128]{1,0:T(8,128)S(1)} %get-tuple-element.41), channel_id=1, source_target_pairs={{0,2},{1,3},{2,0},{3,1},{4,6},{5,7},{6,4},{7,5},{8,10},{9,11},{10,... | collective-permute-start | bytes 73736 | tf_op jit(solution)/shard_map/ppermute | solution.py:464
  12.5 3.9 %collective-permute-start.6 = (f32[5,32,128]{2,1,0:T(8,128)S(1)}, f32[5,32,128]{2,1,0:T(8,128)S(1)}, u32[]{:S(2)}, u32[]{:S(2)}) collective-permute-start(f32[5,32,128]{2,1,0:T(8,128)S(1)} %get-tuple-element.44), channel_id=1, source_target_pairs={{0,7},{1,0},{2,1},{3,2},{4,3},{5,4},{6,5},{7,6},{8,15},{9,8},{10,9... | collective-permute-start | bytes 245768 | tf_op jit(solution)/shard_map/ppermute | solution.py:460
  16.4 0.0 collective-permute-done.3.refs_0_.rest_2_
  16.4 0.3 %collective-permute-done.4.refs_1_.rest_3_ = f32[48,128]{1,0:T(8,128)S(1)} collective-permute-done((f32[48,128]{1,0:T(8,128)S(1)}, f32[48,128]{1,0:T(8,128)S(1)}, u32[]{:S(2)}, u32[]{:S(2)}) %collective-permute-start.4) | collective-permute-done | bytes 24608 | tf_op jit(solution)/shard_map/ppermute | solution.py:464
  16.7 0.0 collective-permute-done.5.refs_2_.rest_1_
  16.7 0.0 collective-permute-done.x_low
  16.7 1.5 %collective-permute-start.7 = (f32[88,128]{1,0:T(8,128)S(1)}, f32[88,128]{1,0:T(8,128)S(1)}, u32[]{:S(2)}, u32[]{:S(2)}) collective-permute-start(f32[88,128]{1,0:T(8,128)S(1)} %get-tuple-element.45), channel_id=1, source_target_pairs={{0,1},{1,0},{2,3},{3,2},{4,5},{5,4},{6,7},{7,6},{8,9},{9,8},{10,11... | collective-permute-start | bytes 135176 | tf_op jit(solution)/shard_map/ppermute | solution.py:464
  18.2 0.3 %collective-permute-done.6.x_high = f32[5,32,128]{2,1,0:T(8,128)S(1)} collective-permute-done((f32[5,32,128]{2,1,0:T(8,128)S(1)}, f32[5,32,128]{2,1,0:T(8,128)S(1)}, u32[]{:S(2)}, u32[]{:S(2)}) %collective-permute-start.6) | collective-permute-done | bytes 81952 | tf_op jit(solution)/shard_map/ppermute | solution.py:460
  18.5 1.1 %change.1.change_ref = f32[5,256,128]{2,1,0:T(8,128)S(1)} custom-call(f32[256,128]{1,0:T(8,128)S(1)} %get-tuple-element.25.r_ref, f32[768,128]{1,0:T(8,128)S(1)} %get-tuple-element.26.v_ref, f32[256,128]{1,0:T(8,128)S(1)} %get-tuple-element.27.p_ref, f32[5,32,128]{2,1,0:T(8,128)S(1)} %get-tuple-element.43.x_low, ...), custom_call_target="tpu_custom_call" | custom-call | flops 9830400000 | bytes 1048576 | tf_op jit(solution)/shard_map/change/pallas_call | solution.py:535
  19.6 1.2 %collective-permute-done.7.got_ref = f32[88,128]{1,0:T(8,128)S(1)} collective-permute-done((f32[88,128]{1,0:T(8,128)S(1)}, f32[88,128]{1,0:T(8,128)S(1)}, u32[]{:S(2)}, u32[]{:S(2)}) %collective-permute-start.7) | collective-permute-done | bytes 45088 | tf_op jit(solution)/shard_map/ppermute | solution.py:464
  20.8 1.7 %final.1 = (f32[5,256,128]{2,1,0:T(8,128)}, f32[32,64]{1,0:T(8,128)}) custom-call(f32[256,128]{1,0:T(8,128)S(1)} %get-tuple-element.25.r_ref, f32[768,128]{1,0:T(8,128)S(1)} %get-tuple-element.26.v_ref, f32[256,128]{1,0:T(8,128)S(1)} %get-tuple-element.27.p_ref, f32[5,256,128]{2,1,0:T(8,128)S(1)} %change.1.change_ref, ...), custom_call_target="tpu_custom_call" | custom-call | flops 3276800 | bytes 1048576 | tf_op jit(solution)/shard_map/final/pallas_call | solution.py:541
  (2 shorter events, 0.0 us)
Async XLA Ops:
  1.9 1.4 %collective-permute-start.1 = (f32[6,8,128]{2,1,0:T(8,128)S(1)}, f32[6,8,128]{2,1,0:T(8,128)S(1)}, u32[]{:S(2)}, u32[]{:S(2)}) collective-permute-start(f32[6,8,128]{2,1,0:T(8,128)S(1)} %get-tuple-element.34), channel_id=1, source_target_pairs={{0,8},{8,0},{16,24},{24,16},{1,9},{9,1},{17,25},{25,17},{2,10},{10... | collective-permute-start | bytes 73736 | tf_op jit(solution)/shard_map/ppermute | solution.py:464
  3.3 4.1 %collective-permute-start.2 = (f32[6,8,128]{2,1,0:T(8,128)S(1)}, f32[6,8,128]{2,1,0:T(8,128)S(1)}, u32[]{:S(2)}, u32[]{:S(2)}) collective-permute-start(f32[6,8,128]{2,1,0:T(8,128)S(1)} %get-tuple-element.37), channel_id=1, source_target_pairs={{0,24},{8,16},{16,8},{24,0},{1,25},{9,17},{17,9},{25,1},{2,26},{10... | collective-permute-start | bytes 73736 | tf_op jit(solution)/shard_map/ppermute | solution.py:469
  5.9 10.8 %collective-permute-start = (f32[5,32,128]{2,1,0:T(8,128)S(1)}, f32[5,32,128]{2,1,0:T(8,128)S(1)}, u32[]{:S(2)}, u32[]{:S(2)}) collective-permute-start(f32[5,32,128]{2,1,0:T(8,128)S(1)} %get-tuple-element.28), channel_id=1, source_target_pairs={{0,1},{1,2},{2,3},{3,4},{4,5},{5,6},{6,7},{7,0},{8,9},{9,10},{10,1... | collective-permute-start | bytes 245768 | tf_op jit(solution)/shard_map/ppermute | solution.py:460
  7.9 8.6 %collective-permute-start.3 = (f32[48,128]{1,0:T(8,128)S(1)}, f32[48,128]{1,0:T(8,128)S(1)}, u32[]{:S(2)}, u32[]{:S(2)}) collective-permute-start(f32[48,128]{1,0:T(8,128)S(1)} %get-tuple-element.39), channel_id=1, source_target_pairs={{0,4},{1,5},{2,6},{3,7},{4,0},{5,1},{6,2},{7,3},{8,12},{9,13},{10,... | collective-permute-start | bytes 73736 | tf_op jit(solution)/shard_map/ppermute | solution.py:464
  11.0 5.7 %collective-permute-start.4 = (f32[48,128]{1,0:T(8,128)S(1)}, f32[48,128]{1,0:T(8,128)S(1)}, u32[]{:S(2)}, u32[]{:S(2)}) collective-permute-start(f32[48,128]{1,0:T(8,128)S(1)} %get-tuple-element.40), channel_id=1, source_target_pairs={{0,6},{1,7},{2,4},{3,5},{4,2},{5,3},{6,0},{7,1},{8,14},{9,15},{10,... | collective-permute-start | bytes 73736 | tf_op jit(solution)/shard_map/ppermute | solution.py:464
  12.3 4.4 %collective-permute-start.5 = (f32[48,128]{1,0:T(8,128)S(1)}, f32[48,128]{1,0:T(8,128)S(1)}, u32[]{:S(2)}, u32[]{:S(2)}) collective-permute-start(f32[48,128]{1,0:T(8,128)S(1)} %get-tuple-element.41), channel_id=1, source_target_pairs={{0,2},{1,3},{2,0},{3,1},{4,6},{5,7},{6,4},{7,5},{8,10},{9,11},{10,... | collective-permute-start | bytes 73736 | tf_op jit(solution)/shard_map/ppermute | solution.py:464
  12.5 5.9 %collective-permute-start.6 = (f32[5,32,128]{2,1,0:T(8,128)S(1)}, f32[5,32,128]{2,1,0:T(8,128)S(1)}, u32[]{:S(2)}, u32[]{:S(2)}) collective-permute-start(f32[5,32,128]{2,1,0:T(8,128)S(1)} %get-tuple-element.44), channel_id=1, source_target_pairs={{0,7},{1,0},{2,1},{3,2},{4,3},{5,4},{6,5},{7,6},{8,15},{9,8},{10,9... | collective-permute-start | bytes 245768 | tf_op jit(solution)/shard_map/ppermute | solution.py:460
  16.7 4.1 %collective-permute-start.7 = (f32[88,128]{1,0:T(8,128)S(1)}, f32[88,128]{1,0:T(8,128)S(1)}, u32[]{:S(2)}, u32[]{:S(2)}) collective-permute-start(f32[88,128]{1,0:T(8,128)S(1)} %get-tuple-element.45), channel_id=1, source_target_pairs={{0,1},{1,0},{2,3},{3,2},{4,5},{5,4},{6,7},{7,6},{8,9},{9,8},{10,11... | collective-permute-start | bytes 135176 | tf_op jit(solution)/shard_map/ppermute | solution.py:464

commit v7 on v6

--- a/solution.py
+++ b/solution.py
@@ -24,6 +24,7 @@
 PACK_COST = 30_000
 PREPARE_COST = 300
 MERGE_COST = 30_000
+HOLD_COST = 1
 
 VMEM = pl.BlockSpec(memory_space=pltpu.VMEM)
 
@@ -274,20 +275,28 @@
             out[pl.ds((d + 1) * per - ROWS, ROWS), :] = top
 
 
-def merge_kernel(msg, firsts, x_low, *refs):
-    *refs, x_out, out = refs
-    x_out[...] = x_low[...]
+def merge_kernel(msg, firsts, *refs):
+    *refs, other_ref, own_ref = refs
     half, top = msg.owners // 2, None
     for first, ref in zip(firsts, refs):
         for d in range(ref.shape[0] // msg.count):
             at, to = d * msg.count, first + d
-            out[pl.ds(to * msg.rows, msg.rows), :] = ref[pl.ds(at + msg.rows, msg.rows), :]
-            if msg.extra:
-                rows = msg.extra_rows
-                out[pl.ds(half * msg.rows + to * rows, rows), :] = ref[pl.ds(at + 2 * msg.rows + rows, rows), :]
+            for odd, out in ((0, own_ref), (1, other_ref)):
+                out[pl.ds(to * msg.rows, msg.rows), :] = ref[pl.ds(at + odd * msg.rows, msg.rows), :]
+                if msg.extra:
+                    rows = msg.extra_rows
+                    out[pl.ds(half * msg.rows + to * rows, rows), :] = ref[
+                        pl.ds(at + 2 * msg.rows + odd * rows, rows), :
+                    ]
             new = ref[pl.ds(at + msg.count - ROWS, ROWS), :]
             top = new if top is None else jnp.maximum(top, new)
-    out[pl.ds(half * (msg.rows + msg.extra_rows), ROWS), :] = top
+    for out in (own_ref, other_ref):
+        out[pl.ds(half * (msg.rows + msg.extra_rows), ROWS), :] = top
+
+
+def hold_kernel(first_ref, second_ref, first_out, second_out):
+    first_out[...] = first_ref[...]
+    second_out[...] = second_ref[...]
 
 
 def change_kernel(sizes, r_ref, v_ref, p_ref, x_low, x_high, y_near, y_far, out_ref):
@@ -336,16 +345,13 @@
         here = following
 
 
-def final_kernel(sizes, msg, firsts, direct, r_ref, v_ref, p_ref, change_ref, got_ref, *rest):
-    blocks = rest[: len(firsts)]
-    new_hbm, depth_hbm, new_ref, depth_ref, main_ref, extra_ref, sems = rest[len(firsts) :]
+def final_kernel(sizes, msg, direct, r_ref, v_ref, p_ref, change_ref, other_ref, own_ref, kept_ref, *rest):
+    new_hbm, depth_hbm, new_ref, depth_ref, main_ref, extra_ref, sems = rest
     nx, ny, nz = sizes
     n_owner, group, part = msg.owners, msg.group, msg.part
     half, length = n_owner // 2, nx * n_owner
-    top = got_ref[pl.ds(half * (msg.rows + msg.extra_rows), ROWS), :]
-    for ref in blocks:
-        for d in range(ref.shape[0] // msg.count):
-            top = jnp.maximum(top, ref[pl.ds((d + 1) * msg.count - ROWS, ROWS), :])
+    at = pl.ds(half * (msg.rows + msg.extra_rows), ROWS)
+    top = jnp.maximum(other_ref[at, :], own_ref[at, :])
     step = COURANT / jnp.max(top, keepdims=True)
     writes = []
     for x in range(nx):
@@ -363,11 +369,13 @@
         if msg.extra:
             extra_ref[owner] = source[pl.ds(extra_at, msg.extra_rows), :]
 
-    for first, ref in zip(firsts, blocks):
-        for d in range(ref.shape[0] // msg.count):
-            settle(ref, d * msg.count, d * msg.count + 2 * msg.rows, first + d, 0)
     for d in range(half):
-        settle(got_ref, d * msg.rows, half * msg.rows + d * msg.extra_rows, d, 1)
+        extra_at = half * msg.rows + d * msg.extra_rows
+        if direct and d == 0:
+            settle(kept_ref, 0, 2 * msg.rows, 0, 0)
+        else:
+            settle(own_ref, d * msg.rows, extra_at, d, 0)
+        settle(other_ref, d * msg.rows, extra_at, d, 1)
     line = []
     for f in range(msg.main):
         line.append(jnp.concatenate([main_ref[q, :, pl.ds(f * part, part)] for q in range(n_owner)], axis=1))
@@ -462,6 +470,13 @@
 
 def to_partner(value, axis, bits):
     return lax.ppermute(value, axis, [(i, i ^ bits) for i in range(lax.axis_size(axis))])
+
+
+def crossed(value, bits):
+    count = lax.axis_size("slab")
+    every = [(s, q) for s in range(lax.axis_size("sect")) for q in range(count)]
+    pairs = [(s * count + q, (s ^ 1) * count + (q ^ bits)) for s, q in every]
+    return lax.ppermute(value, ("sect", "slab"), pairs)
 
 
 def to_other(value, axis):
@@ -517,20 +532,25 @@
         PACK_COST * cells,
         [pltpu.VMEM((group * spread_rows(geometry), columns), jnp.float32)],
     )(cells_at, change_at, target, y_near, y_far, top, x_first, *far)
+    merge = functools.partial(
+        call,
+        out_shapes=[(half * (geometry.rows + geometry.extra_rows) + ROWS, LANES)] * 2,
+        name="merge",
+        flops=MERGE_COST * cells,
+    )
     if direct:
-        arrived = [to_partner(m, "slab", 2 * d) if d else m for d, m in zip(firsts, packed)]
+        arrived = [crossed(m, 2 * d) for d, m in zip(firsts, packed)]
+        turn = [2, 3, 1, 0] if half == 4 else list(firsts)
+        other, own = merge(functools.partial(merge_kernel, geometry, turn))(*(arrived[d] for d in turn))
+        other, own = crossed(other, 1), crossed(own, 0)
     else:
         alike = [[2 * i + odd for i in range(half)] for odd in range(2)]
         arrived = [
             lax.all_to_all(m, "slab", split_axis=0, concat_axis=0, axis_index_groups=alike, tiled=True) for m in packed
         ]
-    x_low, merged = call(
-        functools.partial(merge_kernel, geometry, [firsts[i] for i in [2, 3, 1, 0]] if direct else firsts),
-        [x_edge, (half * (geometry.rows + geometry.extra_rows) + ROWS, LANES)],
-        "merge",
-        MERGE_COST * cells,
-    )(x_low, *([arrived[i] for i in [2, 3, 1, 0]] if direct else arrived))
-    got = to_partner(merged, "slab", 1)
+        other, own = merge(functools.partial(merge_kernel, geometry, firsts))(*arrived)
+        other = to_partner(other, "slab", 1)
+    x_low, x_first = call(hold_kernel, [x_edge] * 2, "hold", HOLD_COST * cells)(x_low, x_first)
     x_high = around(x_first, "slab", -1)
     (change,) = call(
         functools.partial(change_kernel, sizes),
@@ -539,7 +559,7 @@
         300_000 * cells,
     )(*gas, x_low, x_high, y_near, y_far)
     new_state, depth = call(
-        functools.partial(final_kernel, sizes, geometry, firsts, direct),
+        functools.partial(final_kernel, sizes, geometry, direct),
         [(FIELDS, nx * ny, nz), (slots, length)],
         "final",
         100 * cells,
@@ -551,7 +571,7 @@
             pltpu.SemaphoreType.DMA((nx + 1,)),
         ],
         out_specs=[HBM, HBM],
-    )(*gas, change, got, *arrived)
+    )(*gas, change, other, own, packed[0])
     return (new_state.reshape(FIELDS, nx, ny, nz), depth.reshape(1, 1, slots, length))
 
 

time: 22.7 us -> 22.5 us (level)
  starting transfers between devices: 14.7 us -> 13.4 us
  waiting for transfers between devices: 2.02 us -> 2.72 us
  Pallas kernels: 5.21 us -> 5.55 us
    ppermute x5 -> x1, starting transfers between devices: 6.69 us -> 0.52 us  [to_partner(): lax.ppermute(value, axis, [(i, i ^ bits) for i in range(lax.axis_size(axi...]
    ppermute x0 -> x6, starting transfers between devices: none -> 5.82 us  [crossed(): return lax.ppermute(value, ('sect', 'slab'), pairs)]
    ppermute x5 -> x1, waiting for transfers between devices: 1.73 us -> 0.23 us  [to_partner(): lax.ppermute(value, axis, [(i, i ^ bits) for i in range(lax.axis_size(axi...]
    ppermute x2, waiting for transfers between devices: 0.29 us -> 1.71 us  [around(): lax.ppermute(value, axis, [(i, (i + amount) % count) for i in range(count)])]
    ppermute x2, starting transfers between devices: 5.4 us -> 4.46 us  [around(): lax.ppermute(value, axis, [(i, (i + amount) % count) for i in range(count)])]
    ppermute x0 -> x6, waiting for transfers between devices: none -> 0.77 us  [crossed(): return lax.ppermute(value, ('sect', 'slab'), pairs)]
    pallas_call x2 -> x3, Pallas kernels: 1.76 us -> 2.1 us  [the longest x1 2.07 us: body(): call(functools.partial(final_kernel, sizes, geometry, direct), [(FIELDS,...]
  transfers between devices with their start and end apart: 8 -> 10, of which waited for: 4 -> 4; matrix products, arithmetic and copies ran while one was open for 0% -> 0% of each run, Pallas kernels for 10% -> 10%
where the time goes in v7:
time: 22.5 us; the launch traced here: 22.3 us
  starting transfers between devices  13.4 us (60%)
  Pallas kernels  5.55 us (25%)
  waiting for transfers between devices  2.72 us (12%)
  between operations  0.68 us (3%)
    ppermute x6, starting transfers between devices, crossed(): return lax.ppermute(value, ('sect', 'slab'), pairs)  5.82 us
    ppermute x2, starting transfers between devices, around(): lax.ppermute(value, axis, [(i, (i + amount) % count) for i in range(count)])  4.46 us
    ppermute x1, starting transfers between devices, to_other(): lax.ppermute(value, axis, [(i, (i + 2 * (i % 2) - 1) % count) for i in ra...  2.6 us
    pallas_call x1, Pallas kernels, body(): call(functools.partial(final_kernel, sizes, geometry, direct), [(FIELDS,...  2.07 us
    ppermute x2, waiting for transfers between devices, around(): lax.ppermute(value, axis, [(i, (i + amount) % count) for i in range(count)])  1.71 us
    pallas_call x1, Pallas kernels, body(): call(functools.partial(edges_kernel, sizes), [x_edge, x_edge, y_edge, (FI...  1.24 us
    pallas_call x1, Pallas kernels, body(): call(functools.partial(change_kernel, sizes), [(FIELDS, nx * ny, nz)], 'c...  1.11 us
    ppermute x6, waiting for transfers between devices, crossed(): return lax.ppermute(value, ('sect', 'slab'), pairs)  0.77 us
  transfers between devices with their start and end apart: 10, of which 4 were waited for; matrix products, arithmetic and copies ran while one was open for 0% of the time, Pallas kernels for 10%

profile of v7, /device:TPU:0, one launch (start us, length us, event | category | flops | bytes accessed | tf_op | source)
XLA Modules:
  0.0 22.3 jit_solution(10043876060913847780)
XLA Ops:
  0.6 1.2 %edges.1 = (f32[5,32,128]{2,1,0:T(8,128)S(1)}, f32[5,32,128]{2,1,0:T(8,128)S(1)}, f32[6,8,128]{2,1,0:T(8,128)S(1)}, f32[5,8,128]{2,1,0:T(8,128)S(1)}, f32[8,128]...) custom-call(f32[256,128]{1,0:T(8,128)} %bitcast.7, ...), custom_call_target="tpu_custom_call" | custom-call | flops 655360 | bytes 1048576 | tf_op jit(solution)/shard_map/edges/pallas_call | solution.py:507
  1.9 0.5 %collective-permute-start.1 = (f32[6,8,128]{2,1,0:T(8,128)S(1)}, f32[6,8,128]{2,1,0:T(8,128)S(1)}, u32[]{:S(2)}, u32[]{:S(2)}) collective-permute-start(f32[6,8,128]{2,1,0:T(8,128)S(1)} %get-tuple-element.36), channel_id=1, source_target_pairs={{0,8},{8,0},{16,24},{24,16},{1,9},{9,1},{17,25},{25,17},{2,10},{10... | collective-permute-start | bytes 73736 | tf_op jit(solution)/shard_map/ppermute | solution.py:472
  2.4 0.6 %prepare.1 = (f32[4,5,8,128]{3,2,1,0:T(8,128)S(1)}, f32[4,5,8,128]{3,2,1,0:T(8,128)S(1)}, f32[8,128]{1,0:T(8,128)S(1)}) custom-call(f32[256,128]{1,0:T(8,128)S(1)} %get-tuple-element.27.r_ref, f32[768,128]{1,0:T(8,128)S(1)} %get-tuple-element.28.v_ref, f32[256,128]{1,0:T(8,128)S(1)} %get-tuple-element.29.p_ref, s32[4,1,32]{2,1,0:T(1,128)S(1)} %get-tuple-element.31.owner_ref), custom_call_target="tpu_custom_call" | custom-call | flops 9830400 | bytes 1048576 | tf_op jit(solution)/shard_map/prepare/pallas_call | solution.py:516
  3.0 0.2 %collective-permute-done.1.near_ref.y_near = f32[6,8,128]{2,1,0:T(8,128)S(1)} collective-permute-done((f32[6,8,128]{2,1,0:T(8,128)S(1)}, f32[6,8,128]{2,1,0:T(8,128)S(1)}, u32[]{:S(2)}, u32[]{:S(2)}) %collective-permute-start.1) | collective-permute-done | bytes 24608 | tf_op jit(solution)/shard_map/ppermute | solution.py:472
  3.3 2.6 %collective-permute-start.2 = (f32[6,8,128]{2,1,0:T(8,128)S(1)}, f32[6,8,128]{2,1,0:T(8,128)S(1)}, u32[]{:S(2)}, u32[]{:S(2)}) collective-permute-start(f32[6,8,128]{2,1,0:T(8,128)S(1)} %get-tuple-element.39), channel_id=1, source_target_pairs={{0,24},{8,16},{16,8},{24,0},{1,25},{9,17},{17,9},{25,1},{2,26},{10... | collective-permute-start | bytes 73736 | tf_op jit(solution)/shard_map/ppermute | solution.py:484
  5.9 1.5 %collective-permute-start = (f32[5,32,128]{2,1,0:T(8,128)S(1)}, f32[5,32,128]{2,1,0:T(8,128)S(1)}, u32[]{:S(2)}, u32[]{:S(2)}) collective-permute-start(f32[5,32,128]{2,1,0:T(8,128)S(1)} %get-tuple-element.30), channel_id=1, source_target_pairs={{0,1},{1,2},{2,3},{3,4},{4,5},{5,6},{6,7},{7,0},{8,9},{9,10},{10,1... | collective-permute-start | bytes 245768 | tf_op jit(solution)/shard_map/ppermute | solution.py:468
  7.4 0.0 collective-permute-done.2.y_far
  7.4 0.5 %pack.1 = (f32[5,32,128]{2,1,0:T(8,128)S(1)}, f32[48,128]{1,0:T(8,128)S(1)}, f32[48,128]{1,0:T(8,128)S(1)}, f32[48,128]{1,0:T(8,128)S(1)}, f32[48,128]{1,0:T(8,128)S(1)}) custom-call(f32[4,5,8,128]{3,2,1,0:T(8,128)S(1)} %get-tuple-element.32.cell_ref, f32[4,5,8,128]{3,2,1,0:T(8,128)S(1)} %get-tuple-element.33.change_ref, ...), custom_call_target="tpu_custom_call" | custom-call | flops 983040000 | bytes 1048576 | tf_op jit(solution)/shard_map/pack/pallas_call | solution.py:528
  7.9 2.9 %collective-permute-start.4 = (f32[48,128]{1,0:T(8,128)S(1)}, f32[48,128]{1,0:T(8,128)S(1)}, u32[]{:S(2)}, u32[]{:S(2)}) collective-permute-start(f32[48,128]{1,0:T(8,128)S(1)} %get-tuple-element.44), channel_id=1, source_target_pairs={{0,12},{1,13},{2,14},{3,15},{4,8},{5,9},{6,10},{7,11},{8,4},{9,5},... | collective-permute-start | bytes 73736 | tf_op jit(solution)/shard_map/ppermute | solution.py:479
  10.7 1.3 %collective-permute-start.5 = (f32[48,128]{1,0:T(8,128)S(1)}, f32[48,128]{1,0:T(8,128)S(1)}, u32[]{:S(2)}, u32[]{:S(2)}) collective-permute-start(f32[48,128]{1,0:T(8,128)S(1)} %get-tuple-element.45), channel_id=1, source_target_pairs={{0,14},{1,15},{2,12},{3,13},{4,10},{5,11},{6,8},{7,9},{8,6},{9,7},... | collective-permute-start | bytes 73736 | tf_op jit(solution)/shard_map/ppermute | solution.py:479
  12.0 0.2 %collective-permute-start.6 = (f32[48,128]{1,0:T(8,128)S(1)}, f32[48,128]{1,0:T(8,128)S(1)}, u32[]{:S(2)}, u32[]{:S(2)}) collective-permute-start(f32[48,128]{1,0:T(8,128)S(1)} %get-tuple-element.46), channel_id=1, source_target_pairs={{0,10},{1,11},{2,8},{3,9},{4,14},{5,15},{6,12},{7,13},{8,2},{9,3},... | collective-permute-start | bytes 73736 | tf_op jit(solution)/shard_map/ppermute | solution.py:479
  12.3 0.2 collective-permute-start.7
  12.4 0.9 %collective-permute-done.first_ref = f32[5,32,128]{2,1,0:T(8,128)S(1)} collective-permute-done((f32[5,32,128]{2,1,0:T(8,128)S(1)}, f32[5,32,128]{2,1,0:T(8,128)S(1)}, u32[]{:S(2)}, u32[]{:S(2)}) %collective-permute-start) | collective-permute-done | bytes 81952 | tf_op jit(solution)/shard_map/ppermute | solution.py:468
  13.4 2.9 %collective-permute-start.3 = (f32[5,32,128]{2,1,0:T(8,128)S(1)}, f32[5,32,128]{2,1,0:T(8,128)S(1)}, u32[]{:S(2)}, u32[]{:S(2)}) collective-permute-start(f32[5,32,128]{2,1,0:T(8,128)S(1)} %get-tuple-element.43), channel_id=1, source_target_pairs={{0,7},{1,0},{2,1},{3,2},{4,3},{5,4},{6,5},{7,6},{8,15},{9,8},{10,9... | collective-permute-start | bytes 245768 | tf_op jit(solution)/shard_map/ppermute | solution.py:468
  16.3 0.0 collective-permute-done.4.refs_0_
  16.3 0.0 collective-permute-done.5.refs_1_
  16.3 0.0 collective-permute-done.6.refs_2_
  16.3 0.0 collective-permute-done.7.refs_3_
  16.4 1.2 %collective-permute-start.8 = (f32[88,128]{1,0:T(8,128)S(1)}, f32[88,128]{1,0:T(8,128)S(1)}, u32[]{:S(2)}, u32[]{:S(2)}) collective-permute-start(f32[88,128]{1,0:T(8,128)S(1)} %get-tuple-element.48), channel_id=1, source_target_pairs={{0,9},{1,8},{2,11},{3,10},{4,13},{5,12},{6,15},{7,14},{8,1},{9,0},... | collective-permute-start | bytes 135176 | tf_op jit(solution)/shard_map/ppermute | solution.py:479
  17.5 0.1 collective-permute-start.9
  17.6 0.8 %collective-permute-done.3.x_high = f32[5,32,128]{2,1,0:T(8,128)S(1)} collective-permute-done((f32[5,32,128]{2,1,0:T(8,128)S(1)}, f32[5,32,128]{2,1,0:T(8,128)S(1)}, u32[]{:S(2)}, u32[]{:S(2)}) %collective-permute-start.3) | collective-permute-done | bytes 81952 | tf_op jit(solution)/shard_map/ppermute | solution.py:468
  18.4 1.1 %change.1.change_ref = f32[5,256,128]{2,1,0:T(8,128)S(1)} custom-call(f32[256,128]{1,0:T(8,128)S(1)} %get-tuple-element.27.r_ref, f32[768,128]{1,0:T(8,128)S(1)} %get-tuple-element.28.v_ref, f32[256,128]{1,0:T(8,128)S(1)} %get-tuple-element.29.p_ref, f32[5,32,128]{2,1,0:T(8,128)S(1)} %get-tuple-element.42.x_low, ...), custom_call_target="tpu_custom_call" | custom-call | flops 9830400000 | bytes 1048576 | tf_op jit(solution)/shard_map/change/pallas_call | solution.py:555
  19.5 0.8 %collective-permute-done.8.other_ref = f32[88,128]{1,0:T(8,128)S(1)} collective-permute-done((f32[88,128]{1,0:T(8,128)S(1)}, f32[88,128]{1,0:T(8,128)S(1)}, u32[]{:S(2)}, u32[]{:S(2)}) %collective-permute-start.8) | collective-permute-done | bytes 45088 | tf_op jit(solution)/shard_map/ppermute | solution.py:479
  20.3 0.0 collective-permute-done.9.own_ref
  20.3 2.1 %final.1 = (f32[5,256,128]{2,1,0:T(8,128)}, f32[32,64]{1,0:T(8,128)}) custom-call(f32[256,128]{1,0:T(8,128)S(1)} %get-tuple-element.27.r_ref, f32[768,128]{1,0:T(8,128)S(1)} %get-tuple-element.28.v_ref, f32[256,128]{1,0:T(8,128)S(1)} %get-tuple-element.29.p_ref, f32[5,256,128]{2,1,0:T(8,128)S(1)} %change.1.change_ref, ...), custom_call_target="tpu_custom_call" | custom-call | flops 3276800 | bytes 1048576 | tf_op jit(solution)/shard_map/final/pallas_call | solution.py:561
  (3 shorter events, 0.0 us)
Async XLA Ops:
  1.9 1.4 %collective-permute-start.1 = (f32[6,8,128]{2,1,0:T(8,128)S(1)}, f32[6,8,128]{2,1,0:T(8,128)S(1)}, u32[]{:S(2)}, u32[]{:S(2)}) collective-permute-start(f32[6,8,128]{2,1,0:T(8,128)S(1)} %get-tuple-element.36), channel_id=1, source_target_pairs={{0,8},{8,0},{16,24},{24,16},{1,9},{9,1},{17,25},{25,17},{2,10},{10... | collective-permute-start | bytes 73736 | tf_op jit(solution)/shard_map/ppermute | solution.py:472
  3.3 4.1 %collective-permute-start.2 = (f32[6,8,128]{2,1,0:T(8,128)S(1)}, f32[6,8,128]{2,1,0:T(8,128)S(1)}, u32[]{:S(2)}, u32[]{:S(2)}) collective-permute-start(f32[6,8,128]{2,1,0:T(8,128)S(1)} %get-tuple-element.39), channel_id=1, source_target_pairs={{0,24},{8,16},{16,8},{24,0},{1,25},{9,17},{17,9},{25,1},{2,26},{10... | collective-permute-start | bytes 73736 | tf_op jit(solution)/shard_map/ppermute | solution.py:484
  5.9 7.5 %collective-permute-start = (f32[5,32,128]{2,1,0:T(8,128)S(1)}, f32[5,32,128]{2,1,0:T(8,128)S(1)}, u32[]{:S(2)}, u32[]{:S(2)}) collective-permute-start(f32[5,32,128]{2,1,0:T(8,128)S(1)} %get-tuple-element.30), channel_id=1, source_target_pairs={{0,1},{1,2},{2,3},{3,4},{4,5},{5,6},{6,7},{7,0},{8,9},{9,10},{10,1... | collective-permute-start | bytes 245768 | tf_op jit(solution)/shard_map/ppermute | solution.py:468
  7.9 8.5 %collective-permute-start.4 = (f32[48,128]{1,0:T(8,128)S(1)}, f32[48,128]{1,0:T(8,128)S(1)}, u32[]{:S(2)}, u32[]{:S(2)}) collective-permute-start(f32[48,128]{1,0:T(8,128)S(1)} %get-tuple-element.44), channel_id=1, source_target_pairs={{0,12},{1,13},{2,14},{3,15},{4,8},{5,9},{6,10},{7,11},{8,4},{9,5},... | collective-permute-start | bytes 73736 | tf_op jit(solution)/shard_map/ppermute | solution.py:479
  10.7 5.6 %collective-permute-start.5 = (f32[48,128]{1,0:T(8,128)S(1)}, f32[48,128]{1,0:T(8,128)S(1)}, u32[]{:S(2)}, u32[]{:S(2)}) collective-permute-start(f32[48,128]{1,0:T(8,128)S(1)} %get-tuple-element.45), channel_id=1, source_target_pairs={{0,14},{1,15},{2,12},{3,13},{4,10},{5,11},{6,8},{7,9},{8,6},{9,7},... | collective-permute-start | bytes 73736 | tf_op jit(solution)/shard_map/ppermute | solution.py:479
  12.0 4.3 %collective-permute-start.6 = (f32[48,128]{1,0:T(8,128)S(1)}, f32[48,128]{1,0:T(8,128)S(1)}, u32[]{:S(2)}, u32[]{:S(2)}) collective-permute-start(f32[48,128]{1,0:T(8,128)S(1)} %get-tuple-element.46), channel_id=1, source_target_pairs={{0,10},{1,11},{2,8},{3,9},{4,14},{5,15},{6,12},{7,13},{8,2},{9,3},... | collective-permute-start | bytes 73736 | tf_op jit(solution)/shard_map/ppermute | solution.py:479
  12.3 4.1 %collective-permute-start.7 = (f32[48,128]{1,0:T(8,128)S(1)}, f32[48,128]{1,0:T(8,128)S(1)}, u32[]{:S(2)}, u32[]{:S(2)}) collective-permute-start(f32[48,128]{1,0:T(8,128)S(1)} %get-tuple-element.47.kept_ref), channel_id=1, source_target_pairs={{0,8},{1,9},{2,10},{3,11},{4,12},{5,13},{6,14},{7,15},{8,0},{9,1},... | collective-permute-start | bytes 73736 | tf_op jit(solution)/shard_map/ppermute | solution.py:479
  13.4 5.0 %collective-permute-start.3 = (f32[5,32,128]{2,1,0:T(8,128)S(1)}, f32[5,32,128]{2,1,0:T(8,128)S(1)}, u32[]{:S(2)}, u32[]{:S(2)}) collective-permute-start(f32[5,32,128]{2,1,0:T(8,128)S(1)} %get-tuple-element.43), channel_id=1, source_target_pairs={{0,7},{1,0},{2,1},{3,2},{4,3},{5,4},{6,5},{7,6},{8,15},{9,8},{10,9... | collective-permute-start | bytes 245768 | tf_op jit(solution)/shard_map/ppermute | solution.py:468
  16.4 3.9 %collective-permute-start.8 = (f32[88,128]{1,0:T(8,128)S(1)}, f32[88,128]{1,0:T(8,128)S(1)}, u32[]{:S(2)}, u32[]{:S(2)}) collective-permute-start(f32[88,128]{1,0:T(8,128)S(1)} %get-tuple-element.48), channel_id=1, source_target_pairs={{0,9},{1,8},{2,11},{3,10},{4,13},{5,12},{6,15},{7,14},{8,1},{9,0},... | collective-permute-start | bytes 135176 | tf_op jit(solution)/shard_map/ppermute | solution.py:479
  17.5 2.7 %collective-permute-start.9 = (f32[88,128]{1,0:T(8,128)S(1)}, f32[88,128]{1,0:T(8,128)S(1)}, u32[]{:S(2)}, u32[]{:S(2)}) collective-permute-start(f32[88,128]{1,0:T(8,128)S(1)} %get-tuple-element.49), channel_id=1, source_target_pairs={{0,8},{1,9},{2,10},{3,11},{4,12},{5,13},{6,14},{7,15},{8,0},{9,1},... | collective-permute-start | bytes 135176 | tf_op jit(solution)/shard_map/ppermute | solution.py:479

commit v8 on v7

--- a/solution.py
+++ b/solution.py
@@ -23,6 +23,8 @@
 UNROLL = 64
 PACK_COST = 30_000
 PREPARE_COST = 300
+SELECT_COST = 300
+PIECES = 3
 MERGE_COST = 30_000
 HOLD_COST = 1
 
@@ -159,23 +161,26 @@
     top_ref[...] = top
 
 
-def join_kernel(y_far, top_ref, near_ref, target_ref, out_ref, target_out):
+def join_kernel(y_far, top_ref, near_ref, edge_ref, out_ref, edge_out):
     for f in range(FIELDS):
         out_ref[f] = y_far[f]
     out_ref[FIELDS] = jnp.maximum(top_ref[...], near_ref[FIELDS])
-    target_out[...] = target_ref[...]
+    edge_out[...] = edge_ref[...]
 
 
 def spread_rows(msg):
     return LANES + msg.extra * msg.part
 
 
-def prepare_kernel(sizes, msg, r_ref, v_ref, p_ref, owner_ref, cell_ref, change_ref, target_ref):
+def prepare_kernel(sizes, msg, r_ref, v_ref, p_ref, owner_ref, spread, edge_ref, target_ref):
     nx, ny, nz = sizes
     lines = nz // STRIDE
     columns = ny * lines
     step = STRIDE // ROWS
     lane = lax.broadcasted_iota(jnp.int32, (nx, nz), 1)
+    first = lane % STRIDE < step
+    last = lane % STRIDE >= ny - step
+    tiles, changes, parts = [], [], []
     for t in range(step):
         cell = None
         for s in range(ny // step):
@@ -186,90 +191,138 @@
             else:
                 mine = (lane - step * s + 1) % STRIDE < 3
                 cell = [jnp.where(mine, a, b) for a, b in zip(rows, cell)]
-        here = flux_parts(cell, *derived(cell), 2)
+        state, sound = derived(cell)
+        here = flux_parts(cell, state, sound, 2)
         after = face(here, [shift(a, -1, 1) for a in here])
-        for f in range(FIELDS):
-            cell_ref[t, f] = cell[f]
-            change_ref[t, f] = after[f] - shift(after[f], 1, 1)
-    owner = jnp.concatenate([owner_ref[k] for k in range(lines)], axis=1).astype(jnp.float32)
-    own = jnp.broadcast_to(owner, (columns, columns))
-    own_t = own.T
-
-    def place(dim):
-        at = lax.broadcasted_iota(jnp.int32, (columns, columns), dim)
-        return (at % ny) * lines + at // ny
-
-    ahead = (own == own_t) & (place(0) < place(1))
-    rank = jnp.sum(jnp.where(ahead, 1.0, 0.0), axis=0, keepdims=True)
-    target_ref[...] = jnp.broadcast_to(owner * msg.slots + rank, target_ref.shape)
-
-
-def pack_kernel(sizes, msg, n_far, direct, cell_ref, change_ref, target_ref, y_near, y_far, top_ref, x_first, *rest):
-    nx, ny, nz = sizes
-    slots, group, width = msg.slots, msg.group, spread_rows(msg)
-    far, x_out, outs, spread = rest[:n_far], rest[n_far], rest[n_far + 1 : -1], rest[-1]
-    x_out[...] = x_first[...]
-    y_low, y_high = sides([y_near[f] for f in range(FIELDS)], [y_far[f] for f in range(FIELDS)], "sect")
-    columns = ny * (nz // STRIDE)
-    step = STRIDE // ROWS
-    lane = lax.broadcasted_iota(jnp.int32, (nx, nz), 1)
-    target = target_ref[0:1]
-    tiles = [[cell_ref[t, f] for f in range(FIELDS)] for t in range(step)]
-    first = lane % STRIDE < step
-    last = lane % STRIDE >= ny - step
-    below = [jnp.where(first, y_low[f], shift(a, step, 1)) for f, a in enumerate(tiles[-1])]
-    above = [jnp.where(last, shift(y_high[f], ny - step, 1), shift(a, -step, 1)) for f, a in enumerate(tiles[0])]
-    parts = [flux_parts(cell, *derived(cell), 1) for cell in (below, *tiles, above)]
-    faces = [face(a, b) for a, b in zip(parts, parts[1:])]
+        tiles.append(cell)
+        changes.append([a - shift(a, 1, 1) for a in after])
+        parts.append(flux_parts(cell, state, sound, 1))
+    inner = [face(a, b) for a, b in zip(parts, parts[1:])]
+    around_face = face([shift(a, step, 1) for a in parts[-1]], parts[0])
+    low = [jnp.where(first, 0.0, a) for a in around_face]
+    high = [jnp.where(last, 0.0, shift(a, -step, 1)) for a in around_face]
+    faces = [low, *inner, high]
     dense = None
     for t in range(step):
-        total = [(high - low) + change_ref[t, f] for f, (low, high) in enumerate(zip(faces[t], faces[t + 1]))]
+        total = [c + (b - a) for c, a, b in zip(changes[t], faces[t], faces[t + 1])]
         values = [shift(a, t, 1) for a in [*tiles[t], *total]]
         dense = values if dense is None else [jnp.where(lane % step == t, a, b) for a, b in zip(values, dense)]
+    group, width = msg.group, spread_rows(msg)
     spread[...] = jnp.zeros_like(spread)
     for f, value in enumerate(dense):
         for h in range(group):
             spread[pl.ds(h * width + f * nx * group + h, nx, group), :] = value
+    for i, (a, b) in enumerate(zip(parts[0], parts[-1])):
+        edge_ref[0, i] = a
+        edge_ref[1, i] = shift(b, step - ny, 1)
+    owner = jnp.concatenate([owner_ref[k] for k in range(lines)], axis=1).astype(jnp.float32)
+    own = jnp.broadcast_to(owner, (columns, columns))
+    own_t = own.T
+
+    def place(dim):
+        at = lax.broadcasted_iota(jnp.int32, (columns, columns), dim)
+        return (at % ny) * lines + at // ny
+
+    ahead = (own == own_t) & (place(0) < place(1))
+    rank = jnp.sum(jnp.where(ahead, 1.0, 0.0), axis=0, keepdims=True)
+    target_ref[...] = jnp.broadcast_to(owner * msg.slots + rank, target_ref.shape)
+
+
+def lane_of(side, piece, place, group):
+    return (side * PIECES + piece) * group + place
+
+
+def product(selection, values):
+    return lax.dot_general(
+        selection.astype(jnp.bfloat16), values, (((1,), (1,)), ((), ())), preferred_element_type=jnp.float32
+    )
+
+
+def folded(msg, picked):
+    every = msg.owners * msg.extra_rows
+    return jnp.concatenate([picked[a * every : (a + 1) * every] for a in range(msg.fold)], axis=1)
+
+
+def select_kernel(sizes, msg, direct, spread, edge_ref, target_ref, edge_out, *outs):
+    _, ny, nz = sizes
+    group, width, columns = msg.group, spread_rows(msg), ny * (nz // STRIDE)
+    edge_out[...] = edge_ref[...]
+    target = target_ref[0:1]
     z_me, y_me = place_of(direct)
-
-    def chosen(rows, first):
+    at = lax.broadcasted_iota(jnp.int32, (1, columns), 1) % ny
+    edges = jnp.full((1, columns), -1.0)
+    for side, y in enumerate((0, ny - 1)):
+        for p in range(PIECES):
+            for h in range(group):
+                some = jnp.where(at == y, target - float(h), -1.0)
+                edges = jnp.maximum(edges, shift(some, lane_of(side, p, h, group) - y, 1))
+
+    def slot_of(rows, first):
         row = lax.broadcasted_iota(jnp.int32, (msg.owners * rows, columns), 0)
         block = row // rows
         own_of = 2 * ((block // 2) ^ z_me) + ((block % 2) ^ y_me)
-        out = []
-        for h in range(group):
-            slot = (own_of * slots + (first + row % rows) * group + h).astype(jnp.float32)
-            out.append(jnp.where(slot == target, 1.0, 0.0))
-        return jnp.concatenate(out, axis=1).astype(jnp.bfloat16)
-
-    def pieces(first, count):
+        return (own_of * msg.slots + (first + row % rows) * group).astype(jnp.float32)
+
+    def pick(rows, folds, first, count):
+        slot = jnp.concatenate([slot_of(rows, a * rows) for a in range(folds)], axis=0)
+        every = [jnp.where(slot == target - float(h), 1.0, 0.0) for h in range(group)]
+        every = jnp.concatenate(every, axis=1).astype(jnp.bfloat16)
         value = jnp.concatenate([spread[pl.ds(h * width + first, count), :] for h in range(group)], axis=1)
         out = []
-        for _ in range(3):
+        for _ in range(PIECES):
             out.append(value.astype(jnp.bfloat16))
             value = value - out[-1].astype(jnp.float32)
-        return jnp.concatenate(out, axis=1)
-
-    def pick(selection, values):
-        selection = jnp.concatenate([selection] * 3, axis=1)
-        return lax.dot_general(selection, values, (((1,), (1,)), ((), ())), preferred_element_type=jnp.float32)
-
+        picked = product(jnp.concatenate([every] * PIECES, axis=1), jnp.concatenate(out, axis=1))
+        return picked, jnp.where(slot == edges, 1.0, 0.0)
+
+    outs[0][...], outs[1][...] = pick(msg.rows, 1, 0, LANES)
+    if msg.extra:
+        picked, outs[3][...] = pick(msg.extra_rows, msg.fold, LANES, msg.extra * msg.part)
+        outs[2][...] = folded(msg, picked)
+
+
+def pack_kernel(sizes, msg, n_far, edge_ref, y_near, y_far, top_ref, x_first, main_ref, main_edges, *rest):
+    nx, ny, nz = sizes
+    group = msg.group
+    (extra_ref, extra_edges), rest = (rest[:2], rest[2:]) if msg.extra else ((None, None), rest)
+    far, x_out, outs, spread = rest[:n_far], rest[n_far], rest[n_far + 1 : -1], rest[-1]
+    x_out[...] = x_first[...]
+    on = lax.broadcasted_iota(jnp.int32, (nx, nz), 1) % STRIDE == 0
+    spread[pl.ds(0, LANES), :] = jnp.zeros((LANES, spread.shape[1]), jnp.float32)
+    rows = [[None] * group for _ in range(FIELDS)]
+    cells = sides([y_near[f] for f in range(FIELDS)], [y_far[f] for f in range(FIELDS)], "sect")
+    for side, cell in enumerate(cells):
+        beyond = flux_parts(cell, *derived(cell), 1)
+        edge = [edge_ref[side, i] for i in range(len(beyond))]
+        faces = face(edge, beyond) if side else [-a for a in face(beyond, edge)]
+        for f, value in enumerate(faces):
+            value = jnp.where(on, value, 0.0)
+            for p in range(PIECES):
+                piece = value.astype(jnp.bfloat16).astype(jnp.float32)
+                value = value - piece
+                for h in range(group):
+                    moved = shift(piece, lane_of(side, p, h, group), 1)
+                    rows[f][h] = moved if rows[f][h] is None else rows[f][h] + moved
+    for f in range(FIELDS):
+        for h in range(group):
+            spread[pl.ds((FIELDS + f) * nx * group + h, nx, group), :] = rows[f][h]
+    top = jnp.maximum(jnp.maximum(top_ref[...], y_near[FIELDS]), y_far[FIELDS])
+    for ref in far:
+        top = jnp.maximum(top, ref[...])
+    top = jnp.broadcast_to(jnp.max(top, keepdims=True), top.shape)
     per = msg.count
     each = msg.owners // len(outs)
-    picked = pick(chosen(msg.rows, 0), pieces(0, LANES))
+    picked = main_ref[...] + product(main_edges[...], spread[pl.ds(0, LANES), :].astype(jnp.bfloat16))
     for b in range(msg.owners):
         at = (b % each) // 2 * per + b % 2 * msg.rows
         outs[b // each][pl.ds(at, msg.rows), :] = picked[b * msg.rows : (b + 1) * msg.rows]
     if msg.extra:
-        values = pieces(LANES, msg.extra * msg.part)
         rows = msg.extra_rows
-        picked = jnp.concatenate([pick(chosen(rows, a * rows), values) for a in range(msg.fold)], axis=1)
+        values = spread[pl.ds(LANES, msg.extra * msg.part), :].astype(jnp.bfloat16)
+        picked = extra_ref[...] + folded(msg, product(extra_edges[...], values))
         for b in range(msg.owners):
             at = (b % each) // 2 * per + 2 * msg.rows + b % 2 * rows
             outs[b // each][pl.ds(at, rows), :] = picked[b * rows : (b + 1) * rows]
-    top = jnp.maximum(jnp.maximum(top_ref[...], y_near[FIELDS]), y_far[FIELDS])
-    for ref in far:
-        top = jnp.maximum(top, ref[...])
     for out in outs:
         for d in range(each // 2):
             out[pl.ds((d + 1) * per - ROWS, ROWS), :] = top
@@ -352,7 +405,7 @@
     half, length = n_owner // 2, nx * n_owner
     at = pl.ds(half * (msg.rows + msg.extra_rows), ROWS)
     top = jnp.maximum(other_ref[at, :], own_ref[at, :])
-    step = COURANT / jnp.max(top, keepdims=True)
+    step = COURANT / top[0:1, 0:1]
     writes = []
     for x in range(nx):
         rows = pl.ds(x * ny, ny)
@@ -512,26 +565,36 @@
         [pltpu.SemaphoreType.DMA((4,))],
         in_specs=[HBM] * 4,
     )(*(pltpu.with_memory_space_constraint(a, pltpu.HBM) for a in (*gas, owners)))
-    tiles = (STRIDE // ROWS, FIELDS, nx, nz)
-    cells_at, change_at, target = call(
+    parts = (2, 2 * FIELDS + 1, nx, nz)
+    spread, edge, target = call(
         functools.partial(prepare_kernel, sizes, geometry),
-        [tiles, tiles, (ROWS, columns)],
+        [(group * spread_rows(geometry), columns), parts, (ROWS, columns)],
         "prepare",
         PREPARE_COST * cells,
     )(*gas, owners)
     y_near = to_partner(y_near, "sect", 1)
-    y_far, target = call(join_kernel, [y_edge, (ROWS, columns)], "join", cells)(y_far, top, y_near, target)
+    y_far, edge = call(join_kernel, [y_edge, parts], "join", cells)(y_far, top, y_near, edge)
     y_far = to_other(y_far, "sect")
+    selected = [(n_slab * geometry.rows, LANES), (n_slab * geometry.rows, columns)]
+    if geometry.extra:
+        count = n_slab * geometry.extra_rows
+        selected += [(count, LANES), (geometry.fold * count, columns)]
+    edge, *selected = call(
+        functools.partial(select_kernel, sizes, geometry, direct),
+        [parts, *selected],
+        "select",
+        SELECT_COST * cells,
+    )(spread, edge, target)
     far = [around(top, "sect", d) for d in range(2, n_sect - 1)] if n_sect > 4 else []
     x_low = around(x_last, "slab", 1)
     firsts = range(half) if direct else range(1)
     x_first, *packed = call(
-        functools.partial(pack_kernel, sizes, geometry, len(far), direct),
+        functools.partial(pack_kernel, sizes, geometry, len(far)),
         [x_edge] + [(half // len(firsts) * geometry.count, LANES)] * len(firsts),
         "pack",
         PACK_COST * cells,
-        [pltpu.VMEM((group * spread_rows(geometry), columns), jnp.float32)],
-    )(cells_at, change_at, target, y_near, y_far, top, x_first, *far)
+        [pltpu.VMEM((spread_rows(geometry), columns), jnp.float32)],
+    )(edge, y_near, y_far, top, x_first, *selected, *far)
     merge = functools.partial(
         call,
         out_shapes=[(half * (geometry.rows + geometry.extra_rows) + ROWS, LANES)] * 2,

time: 22.5 us -> 22.2 us (0.987)
  starting transfers between devices: 13.4 us -> 13 us
  Pallas kernels: 5.55 us -> 5.8 us
    ppermute x6, starting transfers between devices: 5.82 us -> 5.48 us  [crossed(): return lax.ppermute(value, ('sect', 'slab'), pairs)]
    pallas_call x3 -> x4, Pallas kernels: 1.1 us -> 1.4 us  [the longest x1 0.73 us: body(): call(functools.partial(prepare_kernel, sizes, geometry), [(group * spread...]
  transfers between devices with their start and end apart: 10 -> 10, of which waited for: 4 -> 4; matrix products, arithmetic and copies ran while one was open for 0% -> 0% of each run, Pallas kernels for 10% -> 11%
where the time goes in v8:
time: 22.2 us; the launch traced here: 22.3 us
  starting transfers between devices  13 us (59%)
  Pallas kernels  5.8 us (26%)
  waiting for transfers between devices  2.78 us (13%)
  between operations  0.7 us (3%)
    ppermute x6, starting transfers between devices, crossed(): return lax.ppermute(value, ('sect', 'slab'), pairs)  5.48 us
    ppermute x2, starting transfers between devices, around(): lax.ppermute(value, axis, [(i, (i + amount) % count) for i in range(count)])  4.31 us
    ppermute x1, starting transfers between devices, to_other(): lax.ppermute(value, axis, [(i, (i + 2 * (i % 2) - 1) % count) for i in ra...  2.67 us
    pallas_call x1, Pallas kernels, body(): call(functools.partial(final_kernel, sizes, geometry, direct), [(FIELDS,...  2.06 us
    ppermute x2, waiting for transfers between devices, around(): lax.ppermute(value, axis, [(i, (i + amount) % count) for i in range(count)])  1.86 us
    pallas_call x1, Pallas kernels, body(): call(functools.partial(edges_kernel, sizes), [x_edge, x_edge, y_edge, (FI...  1.23 us
    pallas_call x1, Pallas kernels, body(): call(functools.partial(change_kernel, sizes), [(FIELDS, nx * ny, nz)], 'c...  1.09 us
    ppermute x6, waiting for transfers between devices, crossed(): return lax.ppermute(value, ('sect', 'slab'), pairs)  0.8 us
  transfers between devices with their start and end apart: 10, of which 4 were waited for; matrix products, arithmetic and copies ran while one was open for 0% of the time, Pallas kernels for 11%

profile of v8, /device:TPU:0, one launch (start us, length us, event | category | flops | bytes accessed | tf_op | source)
XLA Modules:
  0.0 22.3 jit_solution(16608783151742517906)
XLA Ops:
  0.6 1.2 %edges.1 = (f32[5,32,128]{2,1,0:T(8,128)S(1)}, f32[5,32,128]{2,1,0:T(8,128)S(1)}, f32[6,8,128]{2,1,0:T(8,128)S(1)}, f32[5,8,128]{2,1,0:T(8,128)S(1)}, f32[8,128]...) custom-call(f32[256,128]{1,0:T(8,128)} %bitcast.7, ...), custom_call_target="tpu_custom_call" | custom-call | flops 655360 | bytes 1048576 | tf_op jit(solution)/shard_map/edges/pallas_call | solution.py:560
  1.9 0.5 %collective-permute-start.1 = (f32[6,8,128]{2,1,0:T(8,128)S(1)}, f32[6,8,128]{2,1,0:T(8,128)S(1)}, u32[]{:S(2)}, u32[]{:S(2)}) collective-permute-start(f32[6,8,128]{2,1,0:T(8,128)S(1)} %get-tuple-element.40), channel_id=1, source_target_pairs={{0,8},{8,0},{16,24},{24,16},{1,9},{9,1},{17,25},{25,17},{2,10},{10... | collective-permute-start | bytes 73736 | tf_op jit(solution)/shard_map/ppermute | solution.py:525
  2.4 0.7 %prepare.1 = (f32[320,128]{1,0:T(8,128)S(1)}, f32[2,11,8,128]{3,2,1,0:T(8,128)S(1)}, f32[8,128]{1,0:T(8,128)S(1)}) custom-call(f32[256,128]{1,0:T(8,128)S(1)} %get-tuple-element.32.r_ref, f32[768,128]{1,0:T(8,128)S(1)} %get-tuple-element.33.v_ref, f32[256,128]{1,0:T(8,128)S(1)} %get-tuple-element.34.p_ref, s32[4,1,32]{2,1,0:T(1,128)S(1)} %get-tuple-element.36.owner_ref), custom_call_target="tpu_custom_call" | custom-call | flops 9830400 | bytes 1048576 | tf_op jit(solution)/shard_map/prepare/pallas_call | solution.py:569
  3.1 0.1 collective-permute-done.1.near_ref.y_near
  3.2 2.7 %collective-permute-start.2 = (f32[6,8,128]{2,1,0:T(8,128)S(1)}, f32[6,8,128]{2,1,0:T(8,128)S(1)}, u32[]{:S(2)}, u32[]{:S(2)}) collective-permute-start(f32[6,8,128]{2,1,0:T(8,128)S(1)} %get-tuple-element.45), channel_id=1, source_target_pairs={{0,24},{8,16},{16,8},{24,0},{1,25},{9,17},{17,9},{25,1},{2,26},{10... | collective-permute-start | bytes 73736 | tf_op jit(solution)/shard_map/ppermute | solution.py:537
  5.9 1.5 %collective-permute-start = (f32[5,32,128]{2,1,0:T(8,128)S(1)}, f32[5,32,128]{2,1,0:T(8,128)S(1)}, u32[]{:S(2)}, u32[]{:S(2)}) collective-permute-start(f32[5,32,128]{2,1,0:T(8,128)S(1)} %get-tuple-element.35), channel_id=1, source_target_pairs={{0,1},{1,2},{2,3},{3,4},{4,5},{5,6},{6,7},{7,0},{8,9},{9,10},{10,1... | collective-permute-start | bytes 245768 | tf_op jit(solution)/shard_map/ppermute | solution.py:521
  7.4 0.3 %select.1 = (f32[2,11,8,128]{3,2,1,0:T(8,128)S(1)}, f32[128,128]{1,0:T(8,128)S(1)}, f32[128,128]{1,0:T(8,128)S(1)}, f32[32,128]{1,0:T(8,128)S(1)}, f32[128,128]{1,0:T(8,128)S(1)}) custom-call(f32[320,128]{1,0:T(8,128)S(1)} %get-tuple-element.37.spread, f32[2,11,8,128]{3,2,1,0:T(8,128)S(1)} %get-tuple-element.42.edge_ref, ...), custom_call_target="tpu_custom_call" | custom-call | flops 9830400 | bytes 1048576 | tf_op jit(solution)/shard_map/select/pallas_call | solution.py:582
  7.8 0.0 collective-permute-done.2.y_far
  7.8 0.3 %pack.1 = (f32[5,32,128]{2,1,0:T(8,128)S(1)}, f32[48,128]{1,0:T(8,128)S(1)}, f32[48,128]{1,0:T(8,128)S(1)}, f32[48,128]{1,0:T(8,128)S(1)}, f32[48,128]{1,0:T(8,128)S(1)}) custom-call(f32[2,11,8,128]{3,2,1,0:T(8,128)S(1)} %get-tuple-element.44.edge_ref, f32[6,8,128]{2,1,0:T(8,128)S(1)} %collective-permute-done.1.near_ref.y_near, ...), custom_call_target="tpu_custom_call" | custom-call | flops 983040000 | bytes 1048576 | tf_op jit(solution)/shard_map/pack/pallas_call | solution.py:591
  8.1 2.5 %collective-permute-start.4 = (f32[48,128]{1,0:T(8,128)S(1)}, f32[48,128]{1,0:T(8,128)S(1)}, u32[]{:S(2)}, u32[]{:S(2)}) collective-permute-start(f32[48,128]{1,0:T(8,128)S(1)} %get-tuple-element.54), channel_id=1, source_target_pairs={{0,12},{1,13},{2,14},{3,15},{4,8},{5,9},{6,10},{7,11},{8,4},{9,5},... | collective-permute-start | bytes 73736 | tf_op jit(solution)/shard_map/ppermute | solution.py:532
  10.7 1.3 %collective-permute-start.5 = (f32[48,128]{1,0:T(8,128)S(1)}, f32[48,128]{1,0:T(8,128)S(1)}, u32[]{:S(2)}, u32[]{:S(2)}) collective-permute-start(f32[48,128]{1,0:T(8,128)S(1)} %get-tuple-element.55), channel_id=1, source_target_pairs={{0,14},{1,15},{2,12},{3,13},{4,10},{5,11},{6,8},{7,9},{8,6},{9,7},... | collective-permute-start | bytes 73736 | tf_op jit(solution)/shard_map/ppermute | solution.py:532
  12.0 0.2 %collective-permute-start.6 = (f32[48,128]{1,0:T(8,128)S(1)}, f32[48,128]{1,0:T(8,128)S(1)}, u32[]{:S(2)}, u32[]{:S(2)}) collective-permute-start(f32[48,128]{1,0:T(8,128)S(1)} %get-tuple-element.56), channel_id=1, source_target_pairs={{0,10},{1,11},{2,8},{3,9},{4,14},{5,15},{6,12},{7,13},{8,2},{9,3},... | collective-permute-start | bytes 73736 | tf_op jit(solution)/shard_map/ppermute | solution.py:532
  12.2 0.2 collective-permute-start.7
  12.4 1.1 %collective-permute-done.first_ref = f32[5,32,128]{2,1,0:T(8,128)S(1)} collective-permute-done((f32[5,32,128]{2,1,0:T(8,128)S(1)}, f32[5,32,128]{2,1,0:T(8,128)S(1)}, u32[]{:S(2)}, u32[]{:S(2)}) %collective-permute-start) | collective-permute-done | bytes 81952 | tf_op jit(solution)/shard_map/ppermute | solution.py:521
  13.5 2.8 %collective-permute-start.3 = (f32[5,32,128]{2,1,0:T(8,128)S(1)}, f32[5,32,128]{2,1,0:T(8,128)S(1)}, u32[]{:S(2)}, u32[]{:S(2)}) collective-permute-start(f32[5,32,128]{2,1,0:T(8,128)S(1)} %get-tuple-element.53), channel_id=1, source_target_pairs={{0,7},{1,0},{2,1},{3,2},{4,3},{5,4},{6,5},{7,6},{8,15},{9,8},{10,9... | collective-permute-start | bytes 245768 | tf_op jit(solution)/shard_map/ppermute | solution.py:521
  16.3 0.0 collective-permute-done.4.refs_0_
  16.3 0.0 collective-permute-done.5.refs_1_
  16.3 0.0 collective-permute-done.6.refs_2_
  16.3 0.0 collective-permute-done.7.refs_3_
  16.3 1.2 %collective-permute-start.8 = (f32[88,128]{1,0:T(8,128)S(1)}, f32[88,128]{1,0:T(8,128)S(1)}, u32[]{:S(2)}, u32[]{:S(2)}) collective-permute-start(f32[88,128]{1,0:T(8,128)S(1)} %get-tuple-element.58), channel_id=1, source_target_pairs={{0,9},{1,8},{2,11},{3,10},{4,13},{5,12},{6,15},{7,14},{8,1},{9,0},... | collective-permute-start | bytes 135176 | tf_op jit(solution)/shard_map/ppermute | solution.py:532
  17.5 0.1 collective-permute-start.9
  17.5 0.8 %collective-permute-done.3.x_high = f32[5,32,128]{2,1,0:T(8,128)S(1)} collective-permute-done((f32[5,32,128]{2,1,0:T(8,128)S(1)}, f32[5,32,128]{2,1,0:T(8,128)S(1)}, u32[]{:S(2)}, u32[]{:S(2)}) %collective-permute-start.3) | collective-permute-done | bytes 81952 | tf_op jit(solution)/shard_map/ppermute | solution.py:521
  18.3 1.1 %change.1.change_ref = f32[5,256,128]{2,1,0:T(8,128)S(1)} custom-call(f32[256,128]{1,0:T(8,128)S(1)} %get-tuple-element.32.r_ref, f32[768,128]{1,0:T(8,128)S(1)} %get-tuple-element.33.v_ref, f32[256,128]{1,0:T(8,128)S(1)} %get-tuple-element.34.p_ref, f32[5,32,128]{2,1,0:T(8,128)S(1)} %get-tuple-element.52.x_low, ...), custom_call_target="tpu_custom_call" | custom-call | flops 9830400000 | bytes 1048576 | tf_op jit(solution)/shard_map/change/pallas_call | solution.py:618
  19.4 0.8 %collective-permute-done.8.other_ref = f32[88,128]{1,0:T(8,128)S(1)} collective-permute-done((f32[88,128]{1,0:T(8,128)S(1)}, f32[88,128]{1,0:T(8,128)S(1)}, u32[]{:S(2)}, u32[]{:S(2)}) %collective-permute-start.8) | collective-permute-done | bytes 45088 | tf_op jit(solution)/shard_map/ppermute | solution.py:532
  20.2 0.0 collective-permute-done.9.own_ref
  20.2 2.1 %final.1 = (f32[5,256,128]{2,1,0:T(8,128)}, f32[32,64]{1,0:T(8,128)}) custom-call(f32[256,128]{1,0:T(8,128)S(1)} %get-tuple-element.32.r_ref, f32[768,128]{1,0:T(8,128)S(1)} %get-tuple-element.33.v_ref, f32[256,128]{1,0:T(8,128)S(1)} %get-tuple-element.34.p_ref, f32[5,256,128]{2,1,0:T(8,128)S(1)} %change.1.change_ref, ...), custom_call_target="tpu_custom_call" | custom-call | flops 3276800 | bytes 1048576 | tf_op jit(solution)/shard_map/final/pallas_call | solution.py:624
  (3 shorter events, 0.0 us)
Async XLA Ops:
  1.9 1.4 %collective-permute-start.1 = (f32[6,8,128]{2,1,0:T(8,128)S(1)}, f32[6,8,128]{2,1,0:T(8,128)S(1)}, u32[]{:S(2)}, u32[]{:S(2)}) collective-permute-start(f32[6,8,128]{2,1,0:T(8,128)S(1)} %get-tuple-element.40), channel_id=1, source_target_pairs={{0,8},{8,0},{16,24},{24,16},{1,9},{9,1},{17,25},{25,17},{2,10},{10... | collective-permute-start | bytes 73736 | tf_op jit(solution)/shard_map/ppermute | solution.py:525
  3.2 4.5 %collective-permute-start.2 = (f32[6,8,128]{2,1,0:T(8,128)S(1)}, f32[6,8,128]{2,1,0:T(8,128)S(1)}, u32[]{:S(2)}, u32[]{:S(2)}) collective-permute-start(f32[6,8,128]{2,1,0:T(8,128)S(1)} %get-tuple-element.45), channel_id=1, source_target_pairs={{0,24},{8,16},{16,8},{24,0},{1,25},{9,17},{17,9},{25,1},{2,26},{10... | collective-permute-start | bytes 73736 | tf_op jit(solution)/shard_map/ppermute | solution.py:537
  5.9 7.5 %collective-permute-start = (f32[5,32,128]{2,1,0:T(8,128)S(1)}, f32[5,32,128]{2,1,0:T(8,128)S(1)}, u32[]{:S(2)}, u32[]{:S(2)}) collective-permute-start(f32[5,32,128]{2,1,0:T(8,128)S(1)} %get-tuple-element.35), channel_id=1, source_target_pairs={{0,1},{1,2},{2,3},{3,4},{4,5},{5,6},{6,7},{7,0},{8,9},{9,10},{10,1... | collective-permute-start | bytes 245768 | tf_op jit(solution)/shard_map/ppermute | solution.py:521
  8.1 8.1 %collective-permute-start.4 = (f32[48,128]{1,0:T(8,128)S(1)}, f32[48,128]{1,0:T(8,128)S(1)}, u32[]{:S(2)}, u32[]{:S(2)}) collective-permute-start(f32[48,128]{1,0:T(8,128)S(1)} %get-tuple-element.54), channel_id=1, source_target_pairs={{0,12},{1,13},{2,14},{3,15},{4,8},{5,9},{6,10},{7,11},{8,4},{9,5},... | collective-permute-start | bytes 73736 | tf_op jit(solution)/shard_map/ppermute | solution.py:532
  10.7 5.6 %collective-permute-start.5 = (f32[48,128]{1,0:T(8,128)S(1)}, f32[48,128]{1,0:T(8,128)S(1)}, u32[]{:S(2)}, u32[]{:S(2)}) collective-permute-start(f32[48,128]{1,0:T(8,128)S(1)} %get-tuple-element.55), channel_id=1, source_target_pairs={{0,14},{1,15},{2,12},{3,13},{4,10},{5,11},{6,8},{7,9},{8,6},{9,7},... | collective-permute-start | bytes 73736 | tf_op jit(solution)/shard_map/ppermute | solution.py:532
  12.0 4.3 %collective-permute-start.6 = (f32[48,128]{1,0:T(8,128)S(1)}, f32[48,128]{1,0:T(8,128)S(1)}, u32[]{:S(2)}, u32[]{:S(2)}) collective-permute-start(f32[48,128]{1,0:T(8,128)S(1)} %get-tuple-element.56), channel_id=1, source_target_pairs={{0,10},{1,11},{2,8},{3,9},{4,14},{5,15},{6,12},{7,13},{8,2},{9,3},... | collective-permute-start | bytes 73736 | tf_op jit(solution)/shard_map/ppermute | solution.py:532
  12.2 4.1 %collective-permute-start.7 = (f32[48,128]{1,0:T(8,128)S(1)}, f32[48,128]{1,0:T(8,128)S(1)}, u32[]{:S(2)}, u32[]{:S(2)}) collective-permute-start(f32[48,128]{1,0:T(8,128)S(1)} %get-tuple-element.57.kept_ref), channel_id=1, source_target_pairs={{0,8},{1,9},{2,10},{3,11},{4,12},{5,13},{6,14},{7,15},{8,0},{9,1},... | collective-permute-start | bytes 73736 | tf_op jit(solution)/shard_map/ppermute | solution.py:532
  13.5 4.9 %collective-permute-start.3 = (f32[5,32,128]{2,1,0:T(8,128)S(1)}, f32[5,32,128]{2,1,0:T(8,128)S(1)}, u32[]{:S(2)}, u32[]{:S(2)}) collective-permute-start(f32[5,32,128]{2,1,0:T(8,128)S(1)} %get-tuple-element.53), channel_id=1, source_target_pairs={{0,7},{1,0},{2,1},{3,2},{4,3},{5,4},{6,5},{7,6},{8,15},{9,8},{10,9... | collective-permute-start | bytes 245768 | tf_op jit(solution)/shard_map/ppermute | solution.py:521
  16.3 3.9 %collective-permute-start.8 = (f32[88,128]{1,0:T(8,128)S(1)}, f32[88,128]{1,0:T(8,128)S(1)}, u32[]{:S(2)}, u32[]{:S(2)}) collective-permute-start(f32[88,128]{1,0:T(8,128)S(1)} %get-tuple-element.58), channel_id=1, source_target_pairs={{0,9},{1,8},{2,11},{3,10},{4,13},{5,12},{6,15},{7,14},{8,1},{9,0},... | collective-permute-start | bytes 135176 | tf_op jit(solution)/shard_map/ppermute | solution.py:532
  17.5 2.7 %collective-permute-start.9 = (f32[88,128]{1,0:T(8,128)S(1)}, f32[88,128]{1,0:T(8,128)S(1)}, u32[]{:S(2)}, u32[]{:S(2)}) collective-permute-start(f32[88,128]{1,0:T(8,128)S(1)} %get-tuple-element.59), channel_id=1, source_target_pairs={{0,8},{1,9},{2,10},{3,11},{4,12},{5,13},{6,14},{7,15},{8,0},{9,1},... | collective-permute-start | bytes 135176 | tf_op jit(solution)/shard_map/ppermute | solution.py:532

commit v9 on v8

--- a/solution.py
+++ b/solution.py
@@ -352,7 +352,7 @@
     second_out[...] = second_ref[...]
 
 
-def change_kernel(sizes, r_ref, v_ref, p_ref, x_low, x_high, y_near, y_far, out_ref):
+def change_kernel(sizes, r_ref, v_ref, p_ref, x_low, x_high, y_near, y_far, out_ref, state_ref):
     nx, ny, nz = sizes
     every = range(FIELDS)
     y_low, y_high = sides([y_near[f] for f in every], [y_far[f] for f in every], "sect")
@@ -395,10 +395,11 @@
         total = [t + (a - shift(a, 1, 1)) for t, a in zip(total, after)]
         for f in range(FIELDS):
             out_ref[f, pl.ds(x * ny, ny), :] = half * total[f]
+            state_ref[f, pl.ds(x * ny, ny), :] = state[f]
         here = following
 
 
-def final_kernel(sizes, msg, direct, r_ref, v_ref, p_ref, change_ref, other_ref, own_ref, kept_ref, *rest):
+def final_kernel(sizes, msg, direct, state_ref, change_ref, other_ref, own_ref, kept_ref, *rest):
     new_hbm, depth_hbm, new_ref, depth_ref, main_ref, extra_ref, sems = rest
     nx, ny, nz = sizes
     n_owner, group, part = msg.owners, msg.group, msg.part
@@ -409,9 +410,8 @@
     writes = []
     for x in range(nx):
         rows = pl.ds(x * ny, ny)
-        state, _ = derived(fields_of(r_ref, v_ref, p_ref, rows))
         for f in range(FIELDS):
-            new_ref[f, rows, :] = state[f] - step * change_ref[f, rows, :]
+            new_ref[f, rows, :] = state_ref[f, rows, :] - step * change_ref[f, rows, :]
         writes.append(pltpu.make_async_copy(new_ref.at[:, rows], new_hbm.at[:, rows], sems.at[x]))
         writes[-1].start()
     z_me, y_me = place_of(direct)
@@ -493,11 +493,17 @@
             at = lax.broadcasted_iota(jnp.int32, (group * length, length), 0)
             of = lax.broadcasted_iota(jnp.int32, (group * length, length), 1)
             pick = jnp.where(at // group == of, 1.0, 0.0)
-            running = jnp.dot(wide, pick, precision=lax.Precision.HIGHEST, preferred_element_type=jnp.float32)
+            pieces = []
+            for _ in range(PIECES):
+                pieces.append(wide.astype(jnp.bfloat16))
+                wide = wide - pieces[-1].astype(jnp.float32)
+            pick = jnp.concatenate([pick.astype(jnp.bfloat16)] * PIECES, axis=0)
+            running = jnp.dot(jnp.concatenate(pieces, axis=1), pick, preferred_element_type=jnp.float32)
         depth_ref[pl.ds(0, rows * group), :] = running
 
     if msg.rows > ROWS:
-        more = jnp.max(jnp.where(taken[ROWS:], 1.0, 0.0)) > 0.0
+        some = kept_ref if direct else own_ref
+        more = jnp.max(some[pl.ds(ROWS, msg.rows - ROWS), pl.ds(0, part)]) > 0.0
 
         @pl.when(more)
         def _():
@@ -615,9 +621,9 @@
         other = to_partner(other, "slab", 1)
     x_low, x_first = call(hold_kernel, [x_edge] * 2, "hold", HOLD_COST * cells)(x_low, x_first)
     x_high = around(x_first, "slab", -1)
-    (change,) = call(
+    change, state = call(
         functools.partial(change_kernel, sizes),
-        [(FIELDS, nx * ny, nz)],
+        [(FIELDS, nx * ny, nz)] * 2,
         "change",
         300_000 * cells,
     )(*gas, x_low, x_high, y_near, y_far)
@@ -634,7 +640,7 @@
             pltpu.SemaphoreType.DMA((nx + 1,)),
         ],
         out_specs=[HBM, HBM],
-    )(*gas, change, other, own, packed[0])
+    )(state, change, other, own, packed[0])
     return (new_state.reshape(FIELDS, nx, ny, nz), depth.reshape(1, 1, slots, length))
 
 

time: 22.2 us -> 22.2 us (level); the launches traced: 22.3 us -> 21.9 us
  Pallas kernels: 5.8 us -> 5.4 us
    pallas_call x1, Pallas kernels: 2.06 us -> 1.65 us  [body(): call(functools.partial(final_kernel, sizes, geometry, direct), [(FIELDS,...]
where the time goes in v9:
time: 22.2 us; the launch traced here: 21.9 us
  starting transfers between devices  13 us (59%)
  Pallas kernels  5.4 us (24%)
  waiting for transfers between devices  2.77 us (12%)
  between operations  0.7 us (3%)
    ppermute x6, starting transfers between devices, crossed(): return lax.ppermute(value, ('sect', 'slab'), pairs)  5.48 us
    ppermute x2, starting transfers between devices, around(): lax.ppermute(value, axis, [(i, (i + amount) % count) for i in range(count)])  4.31 us
    ppermute x1, starting transfers between devices, to_other(): lax.ppermute(value, axis, [(i, (i + 2 * (i % 2) - 1) % count) for i in ra...  2.67 us
    ppermute x2, waiting for transfers between devices, around(): lax.ppermute(value, axis, [(i, (i + amount) % count) for i in range(count)])  1.86 us
    pallas_call x1, Pallas kernels, body(): call(functools.partial(final_kernel, sizes, geometry, direct), [(FIELDS,...  1.65 us
    pallas_call x1, Pallas kernels, body(): call(functools.partial(edges_kernel, sizes), [x_edge, x_edge, y_edge, (FI...  1.23 us
    pallas_call x1, Pallas kernels, body(): call(functools.partial(change_kernel, sizes), [(FIELDS, nx * ny, nz)] * 2...  1.09 us
    ppermute x6, waiting for transfers between devices, crossed(): return lax.ppermute(value, ('sect', 'slab'), pairs)  0.79 us
  transfers between devices with their start and end apart: 10, of which 4 were waited for; matrix products, arithmetic and copies ran while one was open for 0% of the time, Pallas kernels for 11%

profile of v9, /device:TPU:0, one launch (start us, length us, event | category | flops | bytes accessed | tf_op | source)
XLA Modules:
  0.0 21.9 jit_solution(10454970218069748853)
XLA Ops:
  0.6 1.2 %edges.1 = (f32[5,32,128]{2,1,0:T(8,128)S(1)}, f32[5,32,128]{2,1,0:T(8,128)S(1)}, f32[6,8,128]{2,1,0:T(8,128)S(1)}, f32[5,8,128]{2,1,0:T(8,128)S(1)}, f32[8,128]...) custom-call(f32[256,128]{1,0:T(8,128)} %bitcast.7, ...), custom_call_target="tpu_custom_call" | custom-call | flops 655360 | bytes 1048576 | tf_op jit(solution)/shard_map/edges/pallas_call | solution.py:566
  1.9 0.5 %collective-permute-start.1 = (f32[6,8,128]{2,1,0:T(8,128)S(1)}, f32[6,8,128]{2,1,0:T(8,128)S(1)}, u32[]{:S(2)}, u32[]{:S(2)}) collective-permute-start(f32[6,8,128]{2,1,0:T(8,128)S(1)} %get-tuple-element.42), channel_id=1, source_target_pairs={{0,8},{8,0},{16,24},{24,16},{1,9},{9,1},{17,25},{25,17},{2,10},{10... | collective-permute-start | bytes 73736 | tf_op jit(solution)/shard_map/ppermute | solution.py:531
  2.4 0.7 %prepare.1 = (f32[320,128]{1,0:T(8,128)S(1)}, f32[2,11,8,128]{3,2,1,0:T(8,128)S(1)}, f32[8,128]{1,0:T(8,128)S(1)}) custom-call(f32[256,128]{1,0:T(8,128)S(1)} %get-tuple-element.34.r_ref, f32[768,128]{1,0:T(8,128)S(1)} %get-tuple-element.35.v_ref, f32[256,128]{1,0:T(8,128)S(1)} %get-tuple-element.36.p_ref, s32[4,1,32]{2,1,0:T(1,128)S(1)} %get-tuple-element.38.owner_ref), custom_call_target="tpu_custom_call" | custom-call | flops 9830400 | bytes 1048576 | tf_op jit(solution)/shard_map/prepare/pallas_call | solution.py:575
  3.1 0.1 collective-permute-done.1.near_ref.y_near
  3.2 2.7 %collective-permute-start.2 = (f32[6,8,128]{2,1,0:T(8,128)S(1)}, f32[6,8,128]{2,1,0:T(8,128)S(1)}, u32[]{:S(2)}, u32[]{:S(2)}) collective-permute-start(f32[6,8,128]{2,1,0:T(8,128)S(1)} %get-tuple-element.47), channel_id=1, source_target_pairs={{0,24},{8,16},{16,8},{24,0},{1,25},{9,17},{17,9},{25,1},{2,26},{10... | collective-permute-start | bytes 73736 | tf_op jit(solution)/shard_map/ppermute | solution.py:543
  5.9 1.5 %collective-permute-start = (f32[5,32,128]{2,1,0:T(8,128)S(1)}, f32[5,32,128]{2,1,0:T(8,128)S(1)}, u32[]{:S(2)}, u32[]{:S(2)}) collective-permute-start(f32[5,32,128]{2,1,0:T(8,128)S(1)} %get-tuple-element.37), channel_id=1, source_target_pairs={{0,1},{1,2},{2,3},{3,4},{4,5},{5,6},{6,7},{7,0},{8,9},{9,10},{10,1... | collective-permute-start | bytes 245768 | tf_op jit(solution)/shard_map/ppermute | solution.py:527
  7.4 0.3 %select.1 = (f32[2,11,8,128]{3,2,1,0:T(8,128)S(1)}, f32[128,128]{1,0:T(8,128)S(1)}, f32[128,128]{1,0:T(8,128)S(1)}, f32[32,128]{1,0:T(8,128)S(1)}, f32[128,128]{1,0:T(8,128)S(1)}) custom-call(f32[320,128]{1,0:T(8,128)S(1)} %get-tuple-element.39.spread, f32[2,11,8,128]{3,2,1,0:T(8,128)S(1)} %get-tuple-element.44.edge_ref, ...), custom_call_target="tpu_custom_call" | custom-call | flops 9830400 | bytes 1048576 | tf_op jit(solution)/shard_map/select/pallas_call | solution.py:588
  7.8 0.0 collective-permute-done.2.y_far
  7.8 0.3 %pack.1 = (f32[5,32,128]{2,1,0:T(8,128)S(1)}, f32[48,128]{1,0:T(8,128)S(1)}, f32[48,128]{1,0:T(8,128)S(1)}, f32[48,128]{1,0:T(8,128)S(1)}, f32[48,128]{1,0:T(8,128)S(1)}) custom-call(f32[2,11,8,128]{3,2,1,0:T(8,128)S(1)} %get-tuple-element.46.edge_ref, f32[6,8,128]{2,1,0:T(8,128)S(1)} %collective-permute-done.1.near_ref.y_near, ...), custom_call_target="tpu_custom_call" | custom-call | flops 983040000 | bytes 1048576 | tf_op jit(solution)/shard_map/pack/pallas_call | solution.py:597
  8.1 2.5 %collective-permute-start.4 = (f32[48,128]{1,0:T(8,128)S(1)}, f32[48,128]{1,0:T(8,128)S(1)}, u32[]{:S(2)}, u32[]{:S(2)}) collective-permute-start(f32[48,128]{1,0:T(8,128)S(1)} %get-tuple-element.58), channel_id=1, source_target_pairs={{0,12},{1,13},{2,14},{3,15},{4,8},{5,9},{6,10},{7,11},{8,4},{9,5},... | collective-permute-start | bytes 73736 | tf_op jit(solution)/shard_map/ppermute | solution.py:538
  10.7 1.3 %collective-permute-start.5 = (f32[48,128]{1,0:T(8,128)S(1)}, f32[48,128]{1,0:T(8,128)S(1)}, u32[]{:S(2)}, u32[]{:S(2)}) collective-permute-start(f32[48,128]{1,0:T(8,128)S(1)} %get-tuple-element.59), channel_id=1, source_target_pairs={{0,14},{1,15},{2,12},{3,13},{4,10},{5,11},{6,8},{7,9},{8,6},{9,7},... | collective-permute-start | bytes 73736 | tf_op jit(solution)/shard_map/ppermute | solution.py:538
  12.0 0.2 %collective-permute-start.6 = (f32[48,128]{1,0:T(8,128)S(1)}, f32[48,128]{1,0:T(8,128)S(1)}, u32[]{:S(2)}, u32[]{:S(2)}) collective-permute-start(f32[48,128]{1,0:T(8,128)S(1)} %get-tuple-element.60), channel_id=1, source_target_pairs={{0,10},{1,11},{2,8},{3,9},{4,14},{5,15},{6,12},{7,13},{8,2},{9,3},... | collective-permute-start | bytes 73736 | tf_op jit(solution)/shard_map/ppermute | solution.py:538
  12.2 0.2 collective-permute-start.7
  12.4 1.1 %collective-permute-done.first_ref = f32[5,32,128]{2,1,0:T(8,128)S(1)} collective-permute-done((f32[5,32,128]{2,1,0:T(8,128)S(1)}, f32[5,32,128]{2,1,0:T(8,128)S(1)}, u32[]{:S(2)}, u32[]{:S(2)}) %collective-permute-start) | collective-permute-done | bytes 81952 | tf_op jit(solution)/shard_map/ppermute | solution.py:527
  13.5 2.8 %collective-permute-start.3 = (f32[5,32,128]{2,1,0:T(8,128)S(1)}, f32[5,32,128]{2,1,0:T(8,128)S(1)}, u32[]{:S(2)}, u32[]{:S(2)}) collective-permute-start(f32[5,32,128]{2,1,0:T(8,128)S(1)} %get-tuple-element.55), channel_id=1, source_target_pairs={{0,7},{1,0},{2,1},{3,2},{4,3},{5,4},{6,5},{7,6},{8,15},{9,8},{10,9... | collective-permute-start | bytes 245768 | tf_op jit(solution)/shard_map/ppermute | solution.py:527
  16.3 0.0 collective-permute-done.4.refs_0_
  16.3 0.0 collective-permute-done.5.refs_1_
  16.3 0.0 collective-permute-done.6.refs_2_
  16.3 0.0 collective-permute-done.7.refs_3_
  16.3 1.2 %collective-permute-start.8 = (f32[88,128]{1,0:T(8,128)S(1)}, f32[88,128]{1,0:T(8,128)S(1)}, u32[]{:S(2)}, u32[]{:S(2)}) collective-permute-start(f32[88,128]{1,0:T(8,128)S(1)} %get-tuple-element.62), channel_id=1, source_target_pairs={{0,9},{1,8},{2,11},{3,10},{4,13},{5,12},{6,15},{7,14},{8,1},{9,0},... | collective-permute-start | bytes 135176 | tf_op jit(solution)/shard_map/ppermute | solution.py:538
  17.5 0.1 collective-permute-start.9
  17.5 0.8 %collective-permute-done.3.x_high = f32[5,32,128]{2,1,0:T(8,128)S(1)} collective-permute-done((f32[5,32,128]{2,1,0:T(8,128)S(1)}, f32[5,32,128]{2,1,0:T(8,128)S(1)}, u32[]{:S(2)}, u32[]{:S(2)}) %collective-permute-start.3) | collective-permute-done | bytes 81952 | tf_op jit(solution)/shard_map/ppermute | solution.py:527
  18.3 1.1 %change.1 = (f32[5,256,128]{2,1,0:T(8,128)S(1)}, f32[5,256,128]{2,1,0:T(8,128)S(1)}) custom-call(f32[256,128]{1,0:T(8,128)S(1)} %get-tuple-element.34.r_ref, f32[768,128]{1,0:T(8,128)S(1)} %get-tuple-element.35.v_ref, f32[256,128]{1,0:T(8,128)S(1)} %get-tuple-element.36.p_ref, f32[5,32,128]{2,1,0:T(8,128)S(1)} %get-tuple-element.54.x_low, ...), custom_call_target="tpu_custom_call" | custom-call | flops 9830400000 | bytes 1048576 | tf_op jit(solution)/shard_map/change/pallas_call | solution.py:624
  19.4 0.8 %collective-permute-done.8.other_ref = f32[88,128]{1,0:T(8,128)S(1)} collective-permute-done((f32[88,128]{1,0:T(8,128)S(1)}, f32[88,128]{1,0:T(8,128)S(1)}, u32[]{:S(2)}, u32[]{:S(2)}) %collective-permute-start.8) | collective-permute-done | bytes 45088 | tf_op jit(solution)/shard_map/ppermute | solution.py:538
  20.2 0.0 collective-permute-done.9.own_ref
  20.2 1.7 %final.1 = (f32[5,256,128]{2,1,0:T(8,128)}, f32[32,64]{1,0:T(8,128)}) custom-call(f32[5,256,128]{2,1,0:T(8,128)S(1)} %get-tuple-element.56.state_ref, f32[5,256,128]{2,1,0:T(8,128)S(1)} %get-tuple-element.57.change_ref, f32[88,128]{1,0:T(8,128)S(1)} %collective-permute-done.8.other_ref, f32[88,128]{1,0:T(8,128)S(1)} %collective-permute-done.9.own_ref, ...), custom_call_target="tpu_custom_call" | custom-call | flops 3276800 | bytes 1048576 | tf_op jit(solution)/shard_map/final/pallas_call | solution.py:630
  (3 shorter events, 0.0 us)
Async XLA Ops:
  1.9 1.4 %collective-permute-start.1 = (f32[6,8,128]{2,1,0:T(8,128)S(1)}, f32[6,8,128]{2,1,0:T(8,128)S(1)}, u32[]{:S(2)}, u32[]{:S(2)}) collective-permute-start(f32[6,8,128]{2,1,0:T(8,128)S(1)} %get-tuple-element.42), channel_id=1, source_target_pairs={{0,8},{8,0},{16,24},{24,16},{1,9},{9,1},{17,25},{25,17},{2,10},{10... | collective-permute-start | bytes 73736 | tf_op jit(solution)/shard_map/ppermute | solution.py:531
  3.2 4.5 %collective-permute-start.2 = (f32[6,8,128]{2,1,0:T(8,128)S(1)}, f32[6,8,128]{2,1,0:T(8,128)S(1)}, u32[]{:S(2)}, u32[]{:S(2)}) collective-permute-start(f32[6,8,128]{2,1,0:T(8,128)S(1)} %get-tuple-element.47), channel_id=1, source_target_pairs={{0,24},{8,16},{16,8},{24,0},{1,25},{9,17},{17,9},{25,1},{2,26},{10... | collective-permute-start | bytes 73736 | tf_op jit(solution)/shard_map/ppermute | solution.py:543
  5.9 7.5 %collective-permute-start = (f32[5,32,128]{2,1,0:T(8,128)S(1)}, f32[5,32,128]{2,1,0:T(8,128)S(1)}, u32[]{:S(2)}, u32[]{:S(2)}) collective-permute-start(f32[5,32,128]{2,1,0:T(8,128)S(1)} %get-tuple-element.37), channel_id=1, source_target_pairs={{0,1},{1,2},{2,3},{3,4},{4,5},{5,6},{6,7},{7,0},{8,9},{9,10},{10,1... | collective-permute-start | bytes 245768 | tf_op jit(solution)/shard_map/ppermute | solution.py:527
  8.1 8.1 %collective-permute-start.4 = (f32[48,128]{1,0:T(8,128)S(1)}, f32[48,128]{1,0:T(8,128)S(1)}, u32[]{:S(2)}, u32[]{:S(2)}) collective-permute-start(f32[48,128]{1,0:T(8,128)S(1)} %get-tuple-element.58), channel_id=1, source_target_pairs={{0,12},{1,13},{2,14},{3,15},{4,8},{5,9},{6,10},{7,11},{8,4},{9,5},... | collective-permute-start | bytes 73736 | tf_op jit(solution)/shard_map/ppermute | solution.py:538
  10.7 5.6 %collective-permute-start.5 = (f32[48,128]{1,0:T(8,128)S(1)}, f32[48,128]{1,0:T(8,128)S(1)}, u32[]{:S(2)}, u32[]{:S(2)}) collective-permute-start(f32[48,128]{1,0:T(8,128)S(1)} %get-tuple-element.59), channel_id=1, source_target_pairs={{0,14},{1,15},{2,12},{3,13},{4,10},{5,11},{6,8},{7,9},{8,6},{9,7},... | collective-permute-start | bytes 73736 | tf_op jit(solution)/shard_map/ppermute | solution.py:538
  12.0 4.3 %collective-permute-start.6 = (f32[48,128]{1,0:T(8,128)S(1)}, f32[48,128]{1,0:T(8,128)S(1)}, u32[]{:S(2)}, u32[]{:S(2)}) collective-permute-start(f32[48,128]{1,0:T(8,128)S(1)} %get-tuple-element.60), channel_id=1, source_target_pairs={{0,10},{1,11},{2,8},{3,9},{4,14},{5,15},{6,12},{7,13},{8,2},{9,3},... | collective-permute-start | bytes 73736 | tf_op jit(solution)/shard_map/ppermute | solution.py:538
  12.2 4.1 %collective-permute-start.7 = (f32[48,128]{1,0:T(8,128)S(1)}, f32[48,128]{1,0:T(8,128)S(1)}, u32[]{:S(2)}, u32[]{:S(2)}) collective-permute-start(f32[48,128]{1,0:T(8,128)S(1)} %get-tuple-element.61.kept_ref), channel_id=1, source_target_pairs={{0,8},{1,9},{2,10},{3,11},{4,12},{5,13},{6,14},{7,15},{8,0},{9,1},... | collective-permute-start | bytes 73736 | tf_op jit(solution)/shard_map/ppermute | solution.py:538
  13.5 4.9 %collective-permute-start.3 = (f32[5,32,128]{2,1,0:T(8,128)S(1)}, f32[5,32,128]{2,1,0:T(8,128)S(1)}, u32[]{:S(2)}, u32[]{:S(2)}) collective-permute-start(f32[5,32,128]{2,1,0:T(8,128)S(1)} %get-tuple-element.55), channel_id=1, source_target_pairs={{0,7},{1,0},{2,1},{3,2},{4,3},{5,4},{6,5},{7,6},{8,15},{9,8},{10,9... | collective-permute-start | bytes 245768 | tf_op jit(solution)/shard_map/ppermute | solution.py:527
  16.3 3.9 %collective-permute-start.8 = (f32[88,128]{1,0:T(8,128)S(1)}, f32[88,128]{1,0:T(8,128)S(1)}, u32[]{:S(2)}, u32[]{:S(2)}) collective-permute-start(f32[88,128]{1,0:T(8,128)S(1)} %get-tuple-element.62), channel_id=1, source_target_pairs={{0,9},{1,8},{2,11},{3,10},{4,13},{5,12},{6,15},{7,14},{8,1},{9,0},... | collective-permute-start | bytes 135176 | tf_op jit(solution)/shard_map/ppermute | solution.py:538
  17.5 2.7 %collective-permute-start.9 = (f32[88,128]{1,0:T(8,128)S(1)}, f32[88,128]{1,0:T(8,128)S(1)}, u32[]{:S(2)}, u32[]{:S(2)}) collective-permute-start(f32[88,128]{1,0:T(8,128)S(1)} %get-tuple-element.63), channel_id=1, source_target_pairs={{0,8},{1,9},{2,10},{3,11},{4,12},{5,13},{6,14},{7,15},{8,0},{9,1},... | collective-permute-start | bytes 135176 | tf_op jit(solution)/shard_map/ppermute | solution.py:538

commit v10 on v9

--- a/solution.py
+++ b/solution.py
@@ -347,9 +347,10 @@
         out[pl.ds(half * (msg.rows + msg.extra_rows), ROWS), :] = top
 
 
-def hold_kernel(first_ref, second_ref, first_out, second_out):
-    first_out[...] = first_ref[...]
-    second_out[...] = second_ref[...]
+def hold_kernel(*refs):
+    half = len(refs) // 2
+    for ref, out in zip(refs[:half], refs[half:]):
+        out[...] = ref[...]
 
 
 def change_kernel(sizes, r_ref, v_ref, p_ref, x_low, x_high, y_near, y_far, out_ref, state_ref):
@@ -601,6 +602,9 @@
         PACK_COST * cells,
         [pltpu.VMEM((spread_rows(geometry), columns), jnp.float32)],
     )(edge, y_near, y_far, top, x_first, *selected, *far)
+    shapes = [a.shape for a in (x_low, x_first, packed[0])]
+    x_low, x_first, first = call(hold_kernel, shapes, "hold", HOLD_COST * cells)(x_low, x_first, packed[0])
+    x_high = around(x_first, "slab", -1)
     merge = functools.partial(
         call,
         out_shapes=[(half * (geometry.rows + geometry.extra_rows) + ROWS, LANES)] * 2,
@@ -608,7 +612,7 @@
         flops=MERGE_COST * cells,
     )
     if direct:
-        arrived = [crossed(m, 2 * d) for d, m in zip(firsts, packed)]
+        arrived = [crossed(m, 2 * d) for d, m in zip(firsts, [first, *packed[1:]])]
         turn = [2, 3, 1, 0] if half == 4 else list(firsts)
         other, own = merge(functools.partial(merge_kernel, geometry, turn))(*(arrived[d] for d in turn))
         other, own = crossed(other, 1), crossed(own, 0)
@@ -619,8 +623,6 @@
         ]
         other, own = merge(functools.partial(merge_kernel, geometry, firsts))(*arrived)
         other = to_partner(other, "slab", 1)
-    x_low, x_first = call(hold_kernel, [x_edge] * 2, "hold", HOLD_COST * cells)(x_low, x_first)
-    x_high = around(x_first, "slab", -1)
     change, state = call(
         functools.partial(change_kernel, sizes),
         [(FIELDS, nx * ny, nz)] * 2,

time: 22.2 us -> 22.4 us (level)
  Pallas kernels: 5.4 us -> 5.74 us
    pallas_call x1, Pallas kernels: 1.65 us -> 1.99 us  [body(): call(functools.partial(final_kernel, sizes, geometry, direct), [(FIELDS,...]
    ppermute x2, waiting for transfers between devices: 1.86 us -> 2.1 us  [around(): lax.ppermute(value, axis, [(i, (i + amount) % count) for i in range(count)])]
where the time goes in v10:
time: 22.4 us; the launch traced here: 22.2 us
  starting transfers between devices  12.8 us (57%)
  Pallas kernels  5.74 us (26%)
  waiting for transfers between devices  2.97 us (13%)
  between operations  0.71 us (3%)
    ppermute x6, starting transfers between devices, crossed(): return lax.ppermute(value, ('sect', 'slab'), pairs)  5.38 us
    ppermute x2, starting transfers between devices, around(): lax.ppermute(value, axis, [(i, (i + amount) % count) for i in range(count)])  4.25 us
    ppermute x1, starting transfers between devices, to_other(): lax.ppermute(value, axis, [(i, (i + 2 * (i % 2) - 1) % count) for i in ra...  2.67 us
    ppermute x2, waiting for transfers between devices, around(): lax.ppermute(value, axis, [(i, (i + amount) % count) for i in range(count)])  2.1 us
    pallas_call x1, Pallas kernels, body(): call(functools.partial(final_kernel, sizes, geometry, direct), [(FIELDS,...  1.99 us
    pallas_call x1, Pallas kernels, body(): call(functools.partial(edges_kernel, sizes), [x_edge, x_edge, y_edge, (FI...  1.23 us
    pallas_call x1, Pallas kernels, body(): call(functools.partial(change_kernel, sizes), [(FIELDS, nx * ny, nz)] * 2...  1.09 us
    ppermute x6, waiting for transfers between devices, crossed(): return lax.ppermute(value, ('sect', 'slab'), pairs)  0.75 us
  transfers between devices with their start and end apart: 10, of which 4 were waited for; matrix products, arithmetic and copies ran while one was open for 0% of the time, Pallas kernels for 11%

profile of v10, /device:TPU:0, one launch (start us, length us, event | category | flops | bytes accessed | tf_op | source)
XLA Modules:
  0.0 22.2 jit_solution(8712343084234135540)
XLA Ops:
  0.6 1.2 %edges.1 = (f32[5,32,128]{2,1,0:T(8,128)S(1)}, f32[5,32,128]{2,1,0:T(8,128)S(1)}, f32[6,8,128]{2,1,0:T(8,128)S(1)}, f32[5,8,128]{2,1,0:T(8,128)S(1)}, f32[8,128]...) custom-call(f32[256,128]{1,0:T(8,128)} %bitcast.7, ...), custom_call_target="tpu_custom_call" | custom-call | flops 655360 | bytes 1048576 | tf_op jit(solution)/shard_map/edges/pallas_call | solution.py:567
  1.9 0.5 %collective-permute-start.1 = (f32[6,8,128]{2,1,0:T(8,128)S(1)}, f32[6,8,128]{2,1,0:T(8,128)S(1)}, u32[]{:S(2)}, u32[]{:S(2)}) collective-permute-start(f32[6,8,128]{2,1,0:T(8,128)S(1)} %get-tuple-element.43), channel_id=1, source_target_pairs={{0,8},{8,0},{16,24},{24,16},{1,9},{9,1},{17,25},{25,17},{2,10},{10... | collective-permute-start | bytes 73736 | tf_op jit(solution)/shard_map/ppermute | solution.py:532
  2.4 0.7 %prepare.1 = (f32[320,128]{1,0:T(8,128)S(1)}, f32[2,11,8,128]{3,2,1,0:T(8,128)S(1)}, f32[8,128]{1,0:T(8,128)S(1)}) custom-call(f32[256,128]{1,0:T(8,128)S(1)} %get-tuple-element.35.r_ref, f32[768,128]{1,0:T(8,128)S(1)} %get-tuple-element.36.v_ref, f32[256,128]{1,0:T(8,128)S(1)} %get-tuple-element.37.p_ref, s32[4,1,32]{2,1,0:T(1,128)S(1)} %get-tuple-element.39.owner_ref), custom_call_target="tpu_custom_call" | custom-call | flops 9830400 | bytes 1048576 | tf_op jit(solution)/shard_map/prepare/pallas_call | solution.py:576
  3.1 0.1 collective-permute-done.1.near_ref.y_near
  3.2 2.7 %collective-permute-start.2 = (f32[6,8,128]{2,1,0:T(8,128)S(1)}, f32[6,8,128]{2,1,0:T(8,128)S(1)}, u32[]{:S(2)}, u32[]{:S(2)}) collective-permute-start(f32[6,8,128]{2,1,0:T(8,128)S(1)} %get-tuple-element.48), channel_id=1, source_target_pairs={{0,24},{8,16},{16,8},{24,0},{1,25},{9,17},{17,9},{25,1},{2,26},{10... | collective-permute-start | bytes 73736 | tf_op jit(solution)/shard_map/ppermute | solution.py:544
  5.9 1.5 %collective-permute-start = (f32[5,32,128]{2,1,0:T(8,128)S(1)}, f32[5,32,128]{2,1,0:T(8,128)S(1)}, u32[]{:S(2)}, u32[]{:S(2)}) collective-permute-start(f32[5,32,128]{2,1,0:T(8,128)S(1)} %get-tuple-element.38), channel_id=1, source_target_pairs={{0,1},{1,2},{2,3},{3,4},{4,5},{5,6},{6,7},{7,0},{8,9},{9,10},{10,1... | collective-permute-start | bytes 245768 | tf_op jit(solution)/shard_map/ppermute | solution.py:528
  7.4 0.3 %select.1 = (f32[2,11,8,128]{3,2,1,0:T(8,128)S(1)}, f32[128,128]{1,0:T(8,128)S(1)}, f32[128,128]{1,0:T(8,128)S(1)}, f32[32,128]{1,0:T(8,128)S(1)}, f32[128,128]{1,0:T(8,128)S(1)}) custom-call(f32[320,128]{1,0:T(8,128)S(1)} %get-tuple-element.40.spread, f32[2,11,8,128]{3,2,1,0:T(8,128)S(1)} %get-tuple-element.45.edge_ref, ...), custom_call_target="tpu_custom_call" | custom-call | flops 9830400 | bytes 1048576 | tf_op jit(solution)/shard_map/select/pallas_call | solution.py:589
  7.8 0.0 collective-permute-done.2.y_far
  7.8 0.3 %pack.1 = (f32[5,32,128]{2,1,0:T(8,128)S(1)}, f32[48,128]{1,0:T(8,128)S(1)}, f32[48,128]{1,0:T(8,128)S(1)}, f32[48,128]{1,0:T(8,128)S(1)}, f32[48,128]{1,0:T(8,128)S(1)}) custom-call(f32[2,11,8,128]{3,2,1,0:T(8,128)S(1)} %get-tuple-element.47.edge_ref, f32[6,8,128]{2,1,0:T(8,128)S(1)} %collective-permute-done.1.near_ref.y_near, ...), custom_call_target="tpu_custom_call" | custom-call | flops 983040000 | bytes 1048576 | tf_op jit(solution)/shard_map/pack/pallas_call | solution.py:598
  8.1 2.5 %collective-permute-start.4 = (f32[48,128]{1,0:T(8,128)S(1)}, f32[48,128]{1,0:T(8,128)S(1)}, u32[]{:S(2)}, u32[]{:S(2)}) collective-permute-start(f32[48,128]{1,0:T(8,128)S(1)} %get-tuple-element.60), channel_id=1, source_target_pairs={{0,12},{1,13},{2,14},{3,15},{4,8},{5,9},{6,10},{7,11},{8,4},{9,5},... | collective-permute-start | bytes 73736 | tf_op jit(solution)/shard_map/ppermute | solution.py:539
  10.7 1.3 %collective-permute-start.5 = (f32[48,128]{1,0:T(8,128)S(1)}, f32[48,128]{1,0:T(8,128)S(1)}, u32[]{:S(2)}, u32[]{:S(2)}) collective-permute-start(f32[48,128]{1,0:T(8,128)S(1)} %get-tuple-element.61), channel_id=1, source_target_pairs={{0,14},{1,15},{2,12},{3,13},{4,10},{5,11},{6,8},{7,9},{8,6},{9,7},... | collective-permute-start | bytes 73736 | tf_op jit(solution)/shard_map/ppermute | solution.py:539
  12.0 0.2 %collective-permute-start.6 = (f32[48,128]{1,0:T(8,128)S(1)}, f32[48,128]{1,0:T(8,128)S(1)}, u32[]{:S(2)}, u32[]{:S(2)}) collective-permute-start(f32[48,128]{1,0:T(8,128)S(1)} %get-tuple-element.62), channel_id=1, source_target_pairs={{0,10},{1,11},{2,8},{3,9},{4,14},{5,15},{6,12},{7,13},{8,2},{9,3},... | collective-permute-start | bytes 73736 | tf_op jit(solution)/shard_map/ppermute | solution.py:539
  12.2 1.3 %collective-permute-done.refs_0_ = f32[5,32,128]{2,1,0:T(8,128)S(1)} collective-permute-done((f32[5,32,128]{2,1,0:T(8,128)S(1)}, f32[5,32,128]{2,1,0:T(8,128)S(1)}, u32[]{:S(2)}, u32[]{:S(2)}) %collective-permute-start) | collective-permute-done | bytes 81952 | tf_op jit(solution)/shard_map/ppermute | solution.py:528
  13.5 0.1 collective-permute-start.7
  13.5 2.7 %collective-permute-start.3 = (f32[5,32,128]{2,1,0:T(8,128)S(1)}, f32[5,32,128]{2,1,0:T(8,128)S(1)}, u32[]{:S(2)}, u32[]{:S(2)}) collective-permute-start(f32[5,32,128]{2,1,0:T(8,128)S(1)} %get-tuple-element.57), channel_id=1, source_target_pairs={{0,7},{1,0},{2,1},{3,2},{4,3},{5,4},{6,5},{7,6},{8,15},{9,8},{10,9... | collective-permute-start | bytes 245768 | tf_op jit(solution)/shard_map/ppermute | solution.py:528
  16.3 0.0 collective-permute-done.4.refs_0_
  16.3 0.0 collective-permute-done.5.refs_1_
  16.3 0.0 collective-permute-done.6.refs_2_
  16.3 0.0 collective-permute-done.7.refs_3_
  16.3 1.1 %collective-permute-start.8 = (f32[88,128]{1,0:T(8,128)S(1)}, f32[88,128]{1,0:T(8,128)S(1)}, u32[]{:S(2)}, u32[]{:S(2)}) collective-permute-start(f32[88,128]{1,0:T(8,128)S(1)} %get-tuple-element.64), channel_id=1, source_target_pairs={{0,9},{1,8},{2,11},{3,10},{4,13},{5,12},{6,15},{7,14},{8,1},{9,0},... | collective-permute-start | bytes 135176 | tf_op jit(solution)/shard_map/ppermute | solution.py:539
  17.5 0.1 collective-permute-start.9
  17.5 0.8 %collective-permute-done.3.x_high = f32[5,32,128]{2,1,0:T(8,128)S(1)} collective-permute-done((f32[5,32,128]{2,1,0:T(8,128)S(1)}, f32[5,32,128]{2,1,0:T(8,128)S(1)}, u32[]{:S(2)}, u32[]{:S(2)}) %collective-permute-start.3) | collective-permute-done | bytes 81952 | tf_op jit(solution)/shard_map/ppermute | solution.py:528
  18.4 1.1 %change.1 = (f32[5,256,128]{2,1,0:T(8,128)S(1)}, f32[5,256,128]{2,1,0:T(8,128)S(1)}) custom-call(f32[256,128]{1,0:T(8,128)S(1)} %get-tuple-element.35.r_ref, f32[768,128]{1,0:T(8,128)S(1)} %get-tuple-element.36.v_ref, f32[256,128]{1,0:T(8,128)S(1)} %get-tuple-element.37.p_ref, f32[5,32,128]{2,1,0:T(8,128)S(1)} %get-tuple-element.56.x_low, ...), custom_call_target="tpu_custom_call" | custom-call | flops 9830400000 | bytes 1048576 | tf_op jit(solution)/shard_map/change/pallas_call | solution.py:626
  19.5 0.7 %collective-permute-done.8.other_ref = f32[88,128]{1,0:T(8,128)S(1)} collective-permute-done((f32[88,128]{1,0:T(8,128)S(1)}, f32[88,128]{1,0:T(8,128)S(1)}, u32[]{:S(2)}, u32[]{:S(2)}) %collective-permute-start.8) | collective-permute-done | bytes 45088 | tf_op jit(solution)/shard_map/ppermute | solution.py:539
  20.2 0.0 collective-permute-done.9.own_ref
  20.2 2.0 %final.1 = (f32[5,256,128]{2,1,0:T(8,128)}, f32[32,64]{1,0:T(8,128)}) custom-call(f32[5,256,128]{2,1,0:T(8,128)S(1)} %get-tuple-element.58.state_ref, f32[5,256,128]{2,1,0:T(8,128)S(1)} %get-tuple-element.59.change_ref, f32[88,128]{1,0:T(8,128)S(1)} %collective-permute-done.8.other_ref, f32[88,128]{1,0:T(8,128)S(1)} %collective-permute-done.9.own_ref, ...), custom_call_target="tpu_custom_call" | custom-call | flops 3276800 | bytes 1048576 | tf_op jit(solution)/shard_map/final/pallas_call | solution.py:632
  (3 shorter events, 0.0 us)
Async XLA Ops:
  1.9 1.4 %collective-permute-start.1 = (f32[6,8,128]{2,1,0:T(8,128)S(1)}, f32[6,8,128]{2,1,0:T(8,128)S(1)}, u32[]{:S(2)}, u32[]{:S(2)}) collective-permute-start(f32[6,8,128]{2,1,0:T(8,128)S(1)} %get-tuple-element.43), channel_id=1, source_target_pairs={{0,8},{8,0},{16,24},{24,16},{1,9},{9,1},{17,25},{25,17},{2,10},{10... | collective-permute-start | bytes 73736 | tf_op jit(solution)/shard_map/ppermute | solution.py:532
  3.2 4.5 %collective-permute-start.2 = (f32[6,8,128]{2,1,0:T(8,128)S(1)}, f32[6,8,128]{2,1,0:T(8,128)S(1)}, u32[]{:S(2)}, u32[]{:S(2)}) collective-permute-start(f32[6,8,128]{2,1,0:T(8,128)S(1)} %get-tuple-element.48), channel_id=1, source_target_pairs={{0,24},{8,16},{16,8},{24,0},{1,25},{9,17},{17,9},{25,1},{2,26},{10... | collective-permute-start | bytes 73736 | tf_op jit(solution)/shard_map/ppermute | solution.py:544
  5.9 7.5 %collective-permute-start = (f32[5,32,128]{2,1,0:T(8,128)S(1)}, f32[5,32,128]{2,1,0:T(8,128)S(1)}, u32[]{:S(2)}, u32[]{:S(2)}) collective-permute-start(f32[5,32,128]{2,1,0:T(8,128)S(1)} %get-tuple-element.38), channel_id=1, source_target_pairs={{0,1},{1,2},{2,3},{3,4},{4,5},{5,6},{6,7},{7,0},{8,9},{9,10},{10,1... | collective-permute-start | bytes 245768 | tf_op jit(solution)/shard_map/ppermute | solution.py:528
  8.1 8.2 %collective-permute-start.4 = (f32[48,128]{1,0:T(8,128)S(1)}, f32[48,128]{1,0:T(8,128)S(1)}, u32[]{:S(2)}, u32[]{:S(2)}) collective-permute-start(f32[48,128]{1,0:T(8,128)S(1)} %get-tuple-element.60), channel_id=1, source_target_pairs={{0,12},{1,13},{2,14},{3,15},{4,8},{5,9},{6,10},{7,11},{8,4},{9,5},... | collective-permute-start | bytes 73736 | tf_op jit(solution)/shard_map/ppermute | solution.py:539
  10.7 5.6 %collective-permute-start.5 = (f32[48,128]{1,0:T(8,128)S(1)}, f32[48,128]{1,0:T(8,128)S(1)}, u32[]{:S(2)}, u32[]{:S(2)}) collective-permute-start(f32[48,128]{1,0:T(8,128)S(1)} %get-tuple-element.61), channel_id=1, source_target_pairs={{0,14},{1,15},{2,12},{3,13},{4,10},{5,11},{6,8},{7,9},{8,6},{9,7},... | collective-permute-start | bytes 73736 | tf_op jit(solution)/shard_map/ppermute | solution.py:539
  12.0 4.3 %collective-permute-start.6 = (f32[48,128]{1,0:T(8,128)S(1)}, f32[48,128]{1,0:T(8,128)S(1)}, u32[]{:S(2)}, u32[]{:S(2)}) collective-permute-start(f32[48,128]{1,0:T(8,128)S(1)} %get-tuple-element.62), channel_id=1, source_target_pairs={{0,10},{1,11},{2,8},{3,9},{4,14},{5,15},{6,12},{7,13},{8,2},{9,3},... | collective-permute-start | bytes 73736 | tf_op jit(solution)/shard_map/ppermute | solution.py:539
  13.5 2.8 %collective-permute-start.7 = (f32[48,128]{1,0:T(8,128)S(1)}, f32[48,128]{1,0:T(8,128)S(1)}, u32[]{:S(2)}, u32[]{:S(2)}) collective-permute-start(f32[48,128]{1,0:T(8,128)S(1)} %get-tuple-element.63), channel_id=1, source_target_pairs={{0,8},{1,9},{2,10},{3,11},{4,12},{5,13},{6,14},{7,15},{8,0},{9,1},... | collective-permute-start | bytes 73736 | tf_op jit(solution)/shard_map/ppermute | solution.py:539
  13.5 4.8 %collective-permute-start.3 = (f32[5,32,128]{2,1,0:T(8,128)S(1)}, f32[5,32,128]{2,1,0:T(8,128)S(1)}, u32[]{:S(2)}, u32[]{:S(2)}) collective-permute-start(f32[5,32,128]{2,1,0:T(8,128)S(1)} %get-tuple-element.57), channel_id=1, source_target_pairs={{0,7},{1,0},{2,1},{3,2},{4,3},{5,4},{6,5},{7,6},{8,15},{9,8},{10,9... | collective-permute-start | bytes 245768 | tf_op jit(solution)/shard_map/ppermute | solution.py:528
  16.3 3.9 %collective-permute-start.8 = (f32[88,128]{1,0:T(8,128)S(1)}, f32[88,128]{1,0:T(8,128)S(1)}, u32[]{:S(2)}, u32[]{:S(2)}) collective-permute-start(f32[88,128]{1,0:T(8,128)S(1)} %get-tuple-element.64), channel_id=1, source_target_pairs={{0,9},{1,8},{2,11},{3,10},{4,13},{5,12},{6,15},{7,14},{8,1},{9,0},... | collective-permute-start | bytes 135176 | tf_op jit(solution)/shard_map/ppermute | solution.py:539
  17.5 2.8 %collective-permute-start.9 = (f32[88,128]{1,0:T(8,128)S(1)}, f32[88,128]{1,0:T(8,128)S(1)}, u32[]{:S(2)}, u32[]{:S(2)}) collective-permute-start(f32[88,128]{1,0:T(8,128)S(1)} %get-tuple-element.65), channel_id=1, source_target_pairs={{0,8},{1,9},{2,10},{3,11},{4,12},{5,13},{6,14},{7,15},{8,0},{9,1},... | collective-permute-start | bytes 135176 | tf_op jit(solution)/shard_map/ppermute | solution.py:539

commit v11 on v10

--- a/solution.py
+++ b/solution.py
@@ -281,12 +281,11 @@
         outs[2][...] = folded(msg, picked)
 
 
-def pack_kernel(sizes, msg, n_far, edge_ref, y_near, y_far, top_ref, x_first, main_ref, main_edges, *rest):
+def pack_kernel(sizes, msg, n_far, edge_ref, y_near, y_far, top_ref, main_ref, main_edges, *rest):
     nx, ny, nz = sizes
     group = msg.group
     (extra_ref, extra_edges), rest = (rest[:2], rest[2:]) if msg.extra else ((None, None), rest)
-    far, x_out, outs, spread = rest[:n_far], rest[n_far], rest[n_far + 1 : -1], rest[-1]
-    x_out[...] = x_first[...]
+    far, outs, spread = rest[:n_far], rest[n_far:-1], rest[-1]
     on = lax.broadcasted_iota(jnp.int32, (nx, nz), 1) % STRIDE == 0
     spread[pl.ds(0, LANES), :] = jnp.zeros((LANES, spread.shape[1]), jnp.float32)
     rows = [[None] * group for _ in range(FIELDS)]
@@ -595,13 +594,13 @@
     far = [around(top, "sect", d) for d in range(2, n_sect - 1)] if n_sect > 4 else []
     x_low = around(x_last, "slab", 1)
     firsts = range(half) if direct else range(1)
-    x_first, *packed = call(
+    packed = call(
         functools.partial(pack_kernel, sizes, geometry, len(far)),
-        [x_edge] + [(half // len(firsts) * geometry.count, LANES)] * len(firsts),
+        [(half // len(firsts) * geometry.count, LANES)] * len(firsts),
         "pack",
         PACK_COST * cells,
         [pltpu.VMEM((spread_rows(geometry), columns), jnp.float32)],
-    )(edge, y_near, y_far, top, x_first, *selected, *far)
+    )(edge, y_near, y_far, top, *selected, *far)
     shapes = [a.shape for a in (x_low, x_first, packed[0])]
     x_low, x_first, first = call(hold_kernel, shapes, "hold", HOLD_COST * cells)(x_low, x_first, packed[0])
     x_high = around(x_first, "slab", -1)

time: 22.4 us -> 22.4 us (level)
  no operation moved by 1% of the time
where the time goes in v11:
time: 22.4 us; the launch traced here: 22.2 us
  starting transfers between devices  12.8 us (57%)
  Pallas kernels  5.74 us (26%)
  waiting for transfers between devices  2.98 us (13%)
  between operations  0.7 us (3%)
    ppermute x6, starting transfers between devices, crossed(): return lax.ppermute(value, ('sect', 'slab'), pairs)  5.38 us
    ppermute x2, starting transfers between devices, around(): lax.ppermute(value, axis, [(i, (i + amount) % count) for i in range(count)])  4.25 us
    ppermute x1, starting transfers between devices, to_other(): lax.ppermute(value, axis, [(i, (i + 2 * (i % 2) - 1) % count) for i in ra...  2.67 us
    ppermute x2, waiting for transfers between devices, around(): lax.ppermute(value, axis, [(i, (i + amount) % count) for i in range(count)])  2.1 us
    pallas_call x1, Pallas kernels, body(): call(functools.partial(final_kernel, sizes, geometry, direct), [(FIELDS,...  1.99 us
    pallas_call x1, Pallas kernels, body(): call(functools.partial(edges_kernel, sizes), [x_edge, x_edge, y_edge, (FI...  1.23 us
    pallas_call x1, Pallas kernels, body(): call(functools.partial(change_kernel, sizes), [(FIELDS, nx * ny, nz)] * 2...  1.09 us
    ppermute x6, waiting for transfers between devices, crossed(): return lax.ppermute(value, ('sect', 'slab'), pairs)  0.75 us
  transfers between devices with their start and end apart: 10, of which 4 were waited for; matrix products, arithmetic and copies ran while one was open for 0% of the time, Pallas kernels for 11%

profile of v11, /device:TPU:0, one launch (start us, length us, event | category | flops | bytes accessed | tf_op | source)
XLA Modules:
  0.0 22.2 jit_solution(10484771492410733025)
XLA Ops:
  0.6 1.2 %edges.1 = (f32[5,32,128]{2,1,0:T(8,128)S(1)}, f32[5,32,128]{2,1,0:T(8,128)S(1)}, f32[6,8,128]{2,1,0:T(8,128)S(1)}, f32[5,8,128]{2,1,0:T(8,128)S(1)}, f32[8,128]...) custom-call(f32[256,128]{1,0:T(8,128)} %bitcast.7, ...), custom_call_target="tpu_custom_call" | custom-call | flops 655360 | bytes 1048576 | tf_op jit(solution)/shard_map/edges/pallas_call | solution.py:566
  1.9 0.5 %collective-permute-start.1 = (f32[6,8,128]{2,1,0:T(8,128)S(1)}, f32[6,8,128]{2,1,0:T(8,128)S(1)}, u32[]{:S(2)}, u32[]{:S(2)}) collective-permute-start(f32[6,8,128]{2,1,0:T(8,128)S(1)} %get-tuple-element.43), channel_id=1, source_target_pairs={{0,8},{8,0},{16,24},{24,16},{1,9},{9,1},{17,25},{25,17},{2,10},{10... | collective-permute-start | bytes 73736 | tf_op jit(solution)/shard_map/ppermute | solution.py:531
  2.4 0.7 %prepare.1 = (f32[320,128]{1,0:T(8,128)S(1)}, f32[2,11,8,128]{3,2,1,0:T(8,128)S(1)}, f32[8,128]{1,0:T(8,128)S(1)}) custom-call(f32[256,128]{1,0:T(8,128)S(1)} %get-tuple-element.34.r_ref, f32[768,128]{1,0:T(8,128)S(1)} %get-tuple-element.35.v_ref, f32[256,128]{1,0:T(8,128)S(1)} %get-tuple-element.36.p_ref, s32[4,1,32]{2,1,0:T(1,128)S(1)} %get-tuple-element.39.owner_ref), custom_call_target="tpu_custom_call" | custom-call | flops 9830400 | bytes 1048576 | tf_op jit(solution)/shard_map/prepare/pallas_call | solution.py:575
  3.1 0.1 collective-permute-done.1.near_ref.y_near
  3.2 2.7 %collective-permute-start.2 = (f32[6,8,128]{2,1,0:T(8,128)S(1)}, f32[6,8,128]{2,1,0:T(8,128)S(1)}, u32[]{:S(2)}, u32[]{:S(2)}) collective-permute-start(f32[6,8,128]{2,1,0:T(8,128)S(1)} %get-tuple-element.48), channel_id=1, source_target_pairs={{0,24},{8,16},{16,8},{24,0},{1,25},{9,17},{17,9},{25,1},{2,26},{10... | collective-permute-start | bytes 73736 | tf_op jit(solution)/shard_map/ppermute | solution.py:543
  5.9 1.5 %collective-permute-start = (f32[5,32,128]{2,1,0:T(8,128)S(1)}, f32[5,32,128]{2,1,0:T(8,128)S(1)}, u32[]{:S(2)}, u32[]{:S(2)}) collective-permute-start(f32[5,32,128]{2,1,0:T(8,128)S(1)} %get-tuple-element.37), channel_id=1, source_target_pairs={{0,1},{1,2},{2,3},{3,4},{4,5},{5,6},{6,7},{7,0},{8,9},{9,10},{10,1... | collective-permute-start | bytes 245768 | tf_op jit(solution)/shard_map/ppermute | solution.py:527
  7.4 0.3 %select.1 = (f32[2,11,8,128]{3,2,1,0:T(8,128)S(1)}, f32[128,128]{1,0:T(8,128)S(1)}, f32[128,128]{1,0:T(8,128)S(1)}, f32[32,128]{1,0:T(8,128)S(1)}, f32[128,128]{1,0:T(8,128)S(1)}) custom-call(f32[320,128]{1,0:T(8,128)S(1)} %get-tuple-element.40.spread, f32[2,11,8,128]{3,2,1,0:T(8,128)S(1)} %get-tuple-element.45.edge_ref, ...), custom_call_target="tpu_custom_call" | custom-call | flops 9830400 | bytes 1048576 | tf_op jit(solution)/shard_map/select/pallas_call | solution.py:588
  7.8 0.0 collective-permute-done.2.y_far
  7.8 0.3 %pack.1 = (f32[48,128]{1,0:T(8,128)S(1)}, f32[48,128]{1,0:T(8,128)S(1)}, f32[48,128]{1,0:T(8,128)S(1)}, f32[48,128]{1,0:T(8,128)S(1)}) custom-call(f32[2,11,8,128]{3,2,1,0:T(8,128)S(1)} %get-tuple-element.47.edge_ref, f32[6,8,128]{2,1,0:T(8,128)S(1)} %collective-permute-done.1.near_ref.y_near, f32[6,8,128]{2,1,0:T(8,128)S(1)} %collective-permute-done.2.y_far, ...), custom_call_target="tpu_custom_call" | custom-call | flops 983040000 | bytes 1048576 | tf_op jit(solution)/shard_map/pack/pallas_call | solution.py:597
  8.1 2.5 %collective-permute-start.4 = (f32[48,128]{1,0:T(8,128)S(1)}, f32[48,128]{1,0:T(8,128)S(1)}, u32[]{:S(2)}, u32[]{:S(2)}) collective-permute-start(f32[48,128]{1,0:T(8,128)S(1)} %get-tuple-element.58), channel_id=1, source_target_pairs={{0,12},{1,13},{2,14},{3,15},{4,8},{5,9},{6,10},{7,11},{8,4},{9,5},... | collective-permute-start | bytes 73736 | tf_op jit(solution)/shard_map/ppermute | solution.py:538
  10.7 1.3 %collective-permute-start.5 = (f32[48,128]{1,0:T(8,128)S(1)}, f32[48,128]{1,0:T(8,128)S(1)}, u32[]{:S(2)}, u32[]{:S(2)}) collective-permute-start(f32[48,128]{1,0:T(8,128)S(1)} %get-tuple-element.59), channel_id=1, source_target_pairs={{0,14},{1,15},{2,12},{3,13},{4,10},{5,11},{6,8},{7,9},{8,6},{9,7},... | collective-permute-start | bytes 73736 | tf_op jit(solution)/shard_map/ppermute | solution.py:538
  12.0 0.2 %collective-permute-start.6 = (f32[48,128]{1,0:T(8,128)S(1)}, f32[48,128]{1,0:T(8,128)S(1)}, u32[]{:S(2)}, u32[]{:S(2)}) collective-permute-start(f32[48,128]{1,0:T(8,128)S(1)} %get-tuple-element.60), channel_id=1, source_target_pairs={{0,10},{1,11},{2,8},{3,9},{4,14},{5,15},{6,12},{7,13},{8,2},{9,3},... | collective-permute-start | bytes 73736 | tf_op jit(solution)/shard_map/ppermute | solution.py:538
  12.2 1.3 %collective-permute-done.refs_0_ = f32[5,32,128]{2,1,0:T(8,128)S(1)} collective-permute-done((f32[5,32,128]{2,1,0:T(8,128)S(1)}, f32[5,32,128]{2,1,0:T(8,128)S(1)}, u32[]{:S(2)}, u32[]{:S(2)}) %collective-permute-start) | collective-permute-done | bytes 81952 | tf_op jit(solution)/shard_map/ppermute | solution.py:527
  13.5 0.1 collective-permute-start.7
  13.5 2.7 %collective-permute-start.3 = (f32[5,32,128]{2,1,0:T(8,128)S(1)}, f32[5,32,128]{2,1,0:T(8,128)S(1)}, u32[]{:S(2)}, u32[]{:S(2)}) collective-permute-start(f32[5,32,128]{2,1,0:T(8,128)S(1)} %get-tuple-element.55), channel_id=1, source_target_pairs={{0,7},{1,0},{2,1},{3,2},{4,3},{5,4},{6,5},{7,6},{8,15},{9,8},{10,9... | collective-permute-start | bytes 245768 | tf_op jit(solution)/shard_map/ppermute | solution.py:527
  16.3 0.0 collective-permute-done.4.refs_0_
  16.3 0.0 collective-permute-done.5.refs_1_
  16.3 0.0 collective-permute-done.6.refs_2_
  16.3 0.0 collective-permute-done.7.refs_3_
  16.3 1.1 %collective-permute-start.8 = (f32[88,128]{1,0:T(8,128)S(1)}, f32[88,128]{1,0:T(8,128)S(1)}, u32[]{:S(2)}, u32[]{:S(2)}) collective-permute-start(f32[88,128]{1,0:T(8,128)S(1)} %get-tuple-element.62), channel_id=1, source_target_pairs={{0,9},{1,8},{2,11},{3,10},{4,13},{5,12},{6,15},{7,14},{8,1},{9,0},... | collective-permute-start | bytes 135176 | tf_op jit(solution)/shard_map/ppermute | solution.py:538
  17.5 0.1 collective-permute-start.9
  17.5 0.8 %collective-permute-done.3.x_high = f32[5,32,128]{2,1,0:T(8,128)S(1)} collective-permute-done((f32[5,32,128]{2,1,0:T(8,128)S(1)}, f32[5,32,128]{2,1,0:T(8,128)S(1)}, u32[]{:S(2)}, u32[]{:S(2)}) %collective-permute-start.3) | collective-permute-done | bytes 81952 | tf_op jit(solution)/shard_map/ppermute | solution.py:527
  18.4 1.1 %change.1 = (f32[5,256,128]{2,1,0:T(8,128)S(1)}, f32[5,256,128]{2,1,0:T(8,128)S(1)}) custom-call(f32[256,128]{1,0:T(8,128)S(1)} %get-tuple-element.34.r_ref, f32[768,128]{1,0:T(8,128)S(1)} %get-tuple-element.35.v_ref, f32[256,128]{1,0:T(8,128)S(1)} %get-tuple-element.36.p_ref, f32[5,32,128]{2,1,0:T(8,128)S(1)} %get-tuple-element.54.x_low, ...), custom_call_target="tpu_custom_call" | custom-call | flops 9830400000 | bytes 1048576 | tf_op jit(solution)/shard_map/change/pallas_call | solution.py:625
  19.5 0.7 %collective-permute-done.8.other_ref = f32[88,128]{1,0:T(8,128)S(1)} collective-permute-done((f32[88,128]{1,0:T(8,128)S(1)}, f32[88,128]{1,0:T(8,128)S(1)}, u32[]{:S(2)}, u32[]{:S(2)}) %collective-permute-start.8) | collective-permute-done | bytes 45088 | tf_op jit(solution)/shard_map/ppermute | solution.py:538
  20.2 0.0 collective-permute-done.9.own_ref
  20.2 2.0 %final.1 = (f32[5,256,128]{2,1,0:T(8,128)}, f32[32,64]{1,0:T(8,128)}) custom-call(f32[5,256,128]{2,1,0:T(8,128)S(1)} %get-tuple-element.56.state_ref, f32[5,256,128]{2,1,0:T(8,128)S(1)} %get-tuple-element.57.change_ref, f32[88,128]{1,0:T(8,128)S(1)} %collective-permute-done.8.other_ref, f32[88,128]{1,0:T(8,128)S(1)} %collective-permute-done.9.own_ref, ...), custom_call_target="tpu_custom_call" | custom-call | flops 3276800 | bytes 1048576 | tf_op jit(solution)/shard_map/final/pallas_call | solution.py:631
  (3 shorter events, 0.0 us)
Async XLA Ops:
  1.9 1.4 %collective-permute-start.1 = (f32[6,8,128]{2,1,0:T(8,128)S(1)}, f32[6,8,128]{2,1,0:T(8,128)S(1)}, u32[]{:S(2)}, u32[]{:S(2)}) collective-permute-start(f32[6,8,128]{2,1,0:T(8,128)S(1)} %get-tuple-element.43), channel_id=1, source_target_pairs={{0,8},{8,0},{16,24},{24,16},{1,9},{9,1},{17,25},{25,17},{2,10},{10... | collective-permute-start | bytes 73736 | tf_op jit(solution)/shard_map/ppermute | solution.py:531
  3.2 4.5 %collective-permute-start.2 = (f32[6,8,128]{2,1,0:T(8,128)S(1)}, f32[6,8,128]{2,1,0:T(8,128)S(1)}, u32[]{:S(2)}, u32[]{:S(2)}) collective-permute-start(f32[6,8,128]{2,1,0:T(8,128)S(1)} %get-tuple-element.48), channel_id=1, source_target_pairs={{0,24},{8,16},{16,8},{24,0},{1,25},{9,17},{17,9},{25,1},{2,26},{10... | collective-permute-start | bytes 73736 | tf_op jit(solution)/shard_map/ppermute | solution.py:543
  5.9 7.5 %collective-permute-start = (f32[5,32,128]{2,1,0:T(8,128)S(1)}, f32[5,32,128]{2,1,0:T(8,128)S(1)}, u32[]{:S(2)}, u32[]{:S(2)}) collective-permute-start(f32[5,32,128]{2,1,0:T(8,128)S(1)} %get-tuple-element.37), channel_id=1, source_target_pairs={{0,1},{1,2},{2,3},{3,4},{4,5},{5,6},{6,7},{7,0},{8,9},{9,10},{10,1... | collective-permute-start | bytes 245768 | tf_op jit(solution)/shard_map/ppermute | solution.py:527
  8.1 8.2 %collective-permute-start.4 = (f32[48,128]{1,0:T(8,128)S(1)}, f32[48,128]{1,0:T(8,128)S(1)}, u32[]{:S(2)}, u32[]{:S(2)}) collective-permute-start(f32[48,128]{1,0:T(8,128)S(1)} %get-tuple-element.58), channel_id=1, source_target_pairs={{0,12},{1,13},{2,14},{3,15},{4,8},{5,9},{6,10},{7,11},{8,4},{9,5},... | collective-permute-start | bytes 73736 | tf_op jit(solution)/shard_map/ppermute | solution.py:538
  10.7 5.6 %collective-permute-start.5 = (f32[48,128]{1,0:T(8,128)S(1)}, f32[48,128]{1,0:T(8,128)S(1)}, u32[]{:S(2)}, u32[]{:S(2)}) collective-permute-start(f32[48,128]{1,0:T(8,128)S(1)} %get-tuple-element.59), channel_id=1, source_target_pairs={{0,14},{1,15},{2,12},{3,13},{4,10},{5,11},{6,8},{7,9},{8,6},{9,7},... | collective-permute-start | bytes 73736 | tf_op jit(solution)/shard_map/ppermute | solution.py:538
  12.0 4.3 %collective-permute-start.6 = (f32[48,128]{1,0:T(8,128)S(1)}, f32[48,128]{1,0:T(8,128)S(1)}, u32[]{:S(2)}, u32[]{:S(2)}) collective-permute-start(f32[48,128]{1,0:T(8,128)S(1)} %get-tuple-element.60), channel_id=1, source_target_pairs={{0,10},{1,11},{2,8},{3,9},{4,14},{5,15},{6,12},{7,13},{8,2},{9,3},... | collective-permute-start | bytes 73736 | tf_op jit(solution)/shard_map/ppermute | solution.py:538
  13.5 2.8 %collective-permute-start.7 = (f32[48,128]{1,0:T(8,128)S(1)}, f32[48,128]{1,0:T(8,128)S(1)}, u32[]{:S(2)}, u32[]{:S(2)}) collective-permute-start(f32[48,128]{1,0:T(8,128)S(1)} %get-tuple-element.61), channel_id=1, source_target_pairs={{0,8},{1,9},{2,10},{3,11},{4,12},{5,13},{6,14},{7,15},{8,0},{9,1},... | collective-permute-start | bytes 73736 | tf_op jit(solution)/shard_map/ppermute | solution.py:538
  13.5 4.8 %collective-permute-start.3 = (f32[5,32,128]{2,1,0:T(8,128)S(1)}, f32[5,32,128]{2,1,0:T(8,128)S(1)}, u32[]{:S(2)}, u32[]{:S(2)}) collective-permute-start(f32[5,32,128]{2,1,0:T(8,128)S(1)} %get-tuple-element.55), channel_id=1, source_target_pairs={{0,7},{1,0},{2,1},{3,2},{4,3},{5,4},{6,5},{7,6},{8,15},{9,8},{10,9... | collective-permute-start | bytes 245768 | tf_op jit(solution)/shard_map/ppermute | solution.py:527
  16.3 3.9 %collective-permute-start.8 = (f32[88,128]{1,0:T(8,128)S(1)}, f32[88,128]{1,0:T(8,128)S(1)}, u32[]{:S(2)}, u32[]{:S(2)}) collective-permute-start(f32[88,128]{1,0:T(8,128)S(1)} %get-tuple-element.62), channel_id=1, source_target_pairs={{0,9},{1,8},{2,11},{3,10},{4,13},{5,12},{6,15},{7,14},{8,1},{9,0},... | collective-permute-start | bytes 135176 | tf_op jit(solution)/shard_map/ppermute | solution.py:538
  17.5 2.8 %collective-permute-start.9 = (f32[88,128]{1,0:T(8,128)S(1)}, f32[88,128]{1,0:T(8,128)S(1)}, u32[]{:S(2)}, u32[]{:S(2)}) collective-permute-start(f32[88,128]{1,0:T(8,128)S(1)} %get-tuple-element.63), channel_id=1, source_target_pairs={{0,8},{1,9},{2,10},{3,11},{4,12},{5,13},{6,14},{7,15},{8,0},{9,1},... | collective-permute-start | bytes 135176 | tf_op jit(solution)/shard_map/ppermute | solution.py:538

commit v12 on v11

--- a/solution.py
+++ b/solution.py
@@ -161,11 +161,11 @@
     top_ref[...] = top
 
 
-def join_kernel(y_far, top_ref, near_ref, edge_ref, out_ref, edge_out):
+def join_kernel(y_far, top_ref, near_ref, target_ref, out_ref, target_out):
     for f in range(FIELDS):
         out_ref[f] = y_far[f]
     out_ref[FIELDS] = jnp.maximum(top_ref[...], near_ref[FIELDS])
-    edge_out[...] = edge_ref[...]
+    target_out[...] = target_ref[...]
 
 
 def spread_rows(msg):
@@ -243,10 +243,9 @@
     return jnp.concatenate([picked[a * every : (a + 1) * every] for a in range(msg.fold)], axis=1)
 
 
-def select_kernel(sizes, msg, direct, spread, edge_ref, target_ref, edge_out, *outs):
+def select_kernel(sizes, msg, direct, spread, target_ref, *outs):
     _, ny, nz = sizes
     group, width, columns = msg.group, spread_rows(msg), ny * (nz // STRIDE)
-    edge_out[...] = edge_ref[...]
     target = target_ref[0:1]
     z_me, y_me = place_of(direct)
     at = lax.broadcasted_iota(jnp.int32, (1, columns), 1) % ny
@@ -579,18 +578,18 @@
         PREPARE_COST * cells,
     )(*gas, owners)
     y_near = to_partner(y_near, "sect", 1)
-    y_far, edge = call(join_kernel, [y_edge, parts], "join", cells)(y_far, top, y_near, edge)
+    y_far, target = call(join_kernel, [y_edge, (ROWS, columns)], "join", cells)(y_far, top, y_near, target)
     y_far = to_other(y_far, "sect")
     selected = [(n_slab * geometry.rows, LANES), (n_slab * geometry.rows, columns)]
     if geometry.extra:
         count = n_slab * geometry.extra_rows
         selected += [(count, LANES), (geometry.fold * count, columns)]
-    edge, *selected = call(
+    selected = call(
         functools.partial(select_kernel, sizes, geometry, direct),
-        [parts, *selected],
+        selected,
         "select",
         SELECT_COST * cells,
-    )(spread, edge, target)
+    )(spread, target)
     far = [around(top, "sect", d) for d in range(2, n_sect - 1)] if n_sect > 4 else []
     x_low = around(x_last, "slab", 1)
     firsts = range(half) if direct else range(1)

time: 22.4 us -> 22 us (0.982)
  Pallas kernels: 5.74 us -> 5.39 us
    pallas_call x1, Pallas kernels: 1.99 us -> 1.66 us  [body(): call(functools.partial(final_kernel, sizes, geometry, direct), [(FIELDS,...]
where the time goes in v12:
time: 22 us; the launch traced here: 21.8 us
  starting transfers between devices  12.8 us (58%)
  Pallas kernels  5.39 us (24%)
  waiting for transfers between devices  2.97 us (14%)
  between operations  0.7 us (3%)
    ppermute x6, starting transfers between devices, crossed(): return lax.ppermute(value, ('sect', 'slab'), pairs)  5.38 us
    ppermute x2, starting transfers between devices, around(): lax.ppermute(value, axis, [(i, (i + amount) % count) for i in range(count)])  4.25 us
    ppermute x1, starting transfers between devices, to_other(): lax.ppermute(value, axis, [(i, (i + 2 * (i % 2) - 1) % count) for i in ra...  2.6 us
    ppermute x2, waiting for transfers between devices, around(): lax.ppermute(value, axis, [(i, (i + amount) % count) for i in range(count)])  2.1 us
    pallas_call x1, Pallas kernels, body(): call(functools.partial(final_kernel, sizes, geometry, direct), [(FIELDS,...  1.66 us
    pallas_call x1, Pallas kernels, body(): call(functools.partial(edges_kernel, sizes), [x_edge, x_edge, y_edge, (FI...  1.23 us
    pallas_call x1, Pallas kernels, body(): call(functools.partial(change_kernel, sizes), [(FIELDS, nx * ny, nz)] * 2...  1.09 us
    ppermute x6, waiting for transfers between devices, crossed(): return lax.ppermute(value, ('sect', 'slab'), pairs)  0.75 us
  transfers between devices with their start and end apart: 10, of which 4 were waited for; matrix products, arithmetic and copies ran while one was open for 0% of the time, Pallas kernels for 11%

profile of v12, /device:TPU:0, one launch (start us, length us, event | category | flops | bytes accessed | tf_op | source)
XLA Modules:
  0.0 21.8 jit_solution(9701622922459449128)
XLA Ops:
  0.6 1.2 %edges.1 = (f32[5,32,128]{2,1,0:T(8,128)S(1)}, f32[5,32,128]{2,1,0:T(8,128)S(1)}, f32[6,8,128]{2,1,0:T(8,128)S(1)}, f32[5,8,128]{2,1,0:T(8,128)S(1)}, f32[8,128]...) custom-call(f32[256,128]{1,0:T(8,128)} %bitcast.7, ...), custom_call_target="tpu_custom_call" | custom-call | flops 655360 | bytes 1048576 | tf_op jit(solution)/shard_map/edges/pallas_call | solution.py:565
  1.9 0.5 %collective-permute-start.1 = (f32[6,8,128]{2,1,0:T(8,128)S(1)}, f32[6,8,128]{2,1,0:T(8,128)S(1)}, u32[]{:S(2)}, u32[]{:S(2)}) collective-permute-start(f32[6,8,128]{2,1,0:T(8,128)S(1)} %get-tuple-element.40), channel_id=1, source_target_pairs={{0,8},{8,0},{16,24},{24,16},{1,9},{9,1},{17,25},{25,17},{2,10},{10... | collective-permute-start | bytes 73736 | tf_op jit(solution)/shard_map/ppermute | solution.py:530
  2.4 0.7 %prepare.1 = (f32[320,128]{1,0:T(8,128)S(1)}, f32[2,11,8,128]{3,2,1,0:T(8,128)S(1)}, f32[8,128]{1,0:T(8,128)S(1)}) custom-call(f32[256,128]{1,0:T(8,128)S(1)} %get-tuple-element.33.r_ref, f32[768,128]{1,0:T(8,128)S(1)} %get-tuple-element.34.v_ref, f32[256,128]{1,0:T(8,128)S(1)} %get-tuple-element.35.p_ref, s32[4,1,32]{2,1,0:T(1,128)S(1)} %get-tuple-element.38.owner_ref), custom_call_target="tpu_custom_call" | custom-call | flops 9830400 | bytes 1048576 | tf_op jit(solution)/shard_map/prepare/pallas_call | solution.py:574
  3.1 0.1 collective-permute-done.1.near_ref.y_near
  3.2 2.6 %collective-permute-start.2 = (f32[6,8,128]{2,1,0:T(8,128)S(1)}, f32[6,8,128]{2,1,0:T(8,128)S(1)}, u32[]{:S(2)}, u32[]{:S(2)}) collective-permute-start(f32[6,8,128]{2,1,0:T(8,128)S(1)} %get-tuple-element.44), channel_id=1, source_target_pairs={{0,24},{8,16},{16,8},{24,0},{1,25},{9,17},{17,9},{25,1},{2,26},{10... | collective-permute-start | bytes 73736 | tf_op jit(solution)/shard_map/ppermute | solution.py:542
  5.8 1.5 %collective-permute-start = (f32[5,32,128]{2,1,0:T(8,128)S(1)}, f32[5,32,128]{2,1,0:T(8,128)S(1)}, u32[]{:S(2)}, u32[]{:S(2)}) collective-permute-start(f32[5,32,128]{2,1,0:T(8,128)S(1)} %get-tuple-element.36), channel_id=1, source_target_pairs={{0,1},{1,2},{2,3},{3,4},{4,5},{5,6},{6,7},{7,0},{8,9},{9,10},{10,1... | collective-permute-start | bytes 245768 | tf_op jit(solution)/shard_map/ppermute | solution.py:526
  7.4 0.3 %select.1 = (f32[128,128]{1,0:T(8,128)S(1)}, f32[128,128]{1,0:T(8,128)S(1)}, f32[32,128]{1,0:T(8,128)S(1)}, f32[128,128]{1,0:T(8,128)S(1)}) custom-call(f32[320,128]{1,0:T(8,128)S(1)} %get-tuple-element.45.spread, f32[8,128]{1,0:T(8,128)S(1)} %get-tuple-element.46.target_ref), custom_call_target="tpu_custom_call" | custom-call | flops 9830400 | bytes 1048576 | tf_op jit(solution)/shard_map/select/pallas_call | solution.py:587
  7.7 0.0 collective-permute-done.2.y_far
  7.7 0.3 %pack.1 = (f32[48,128]{1,0:T(8,128)S(1)}, f32[48,128]{1,0:T(8,128)S(1)}, f32[48,128]{1,0:T(8,128)S(1)}, f32[48,128]{1,0:T(8,128)S(1)}) custom-call(f32[2,11,8,128]{3,2,1,0:T(8,128)S(1)} %get-tuple-element.39.edge_ref, f32[6,8,128]{2,1,0:T(8,128)S(1)} %collective-permute-done.1.near_ref.y_near, f32[6,8,128]{2,1,0:T(8,128)S(1)} %collective-permute-done.2.y_far, ...), custom_call_target="tpu_custom_call" | custom-call | flops 983040000 | bytes 1048576 | tf_op jit(solution)/shard_map/pack/pallas_call | solution.py:596
  8.0 2.6 %collective-permute-start.4 = (f32[48,128]{1,0:T(8,128)S(1)}, f32[48,128]{1,0:T(8,128)S(1)}, u32[]{:S(2)}, u32[]{:S(2)}) collective-permute-start(f32[48,128]{1,0:T(8,128)S(1)} %get-tuple-element.56), channel_id=1, source_target_pairs={{0,12},{1,13},{2,14},{3,15},{4,8},{5,9},{6,10},{7,11},{8,4},{9,5},... | collective-permute-start | bytes 73736 | tf_op jit(solution)/shard_map/ppermute | solution.py:537
  10.6 1.3 %collective-permute-start.5 = (f32[48,128]{1,0:T(8,128)S(1)}, f32[48,128]{1,0:T(8,128)S(1)}, u32[]{:S(2)}, u32[]{:S(2)}) collective-permute-start(f32[48,128]{1,0:T(8,128)S(1)} %get-tuple-element.57), channel_id=1, source_target_pairs={{0,14},{1,15},{2,12},{3,13},{4,10},{5,11},{6,8},{7,9},{8,6},{9,7},... | collective-permute-start | bytes 73736 | tf_op jit(solution)/shard_map/ppermute | solution.py:537
  11.9 0.2 %collective-permute-start.6 = (f32[48,128]{1,0:T(8,128)S(1)}, f32[48,128]{1,0:T(8,128)S(1)}, u32[]{:S(2)}, u32[]{:S(2)}) collective-permute-start(f32[48,128]{1,0:T(8,128)S(1)} %get-tuple-element.58), channel_id=1, source_target_pairs={{0,10},{1,11},{2,8},{3,9},{4,14},{5,15},{6,12},{7,13},{8,2},{9,3},... | collective-permute-start | bytes 73736 | tf_op jit(solution)/shard_map/ppermute | solution.py:537
  12.1 1.3 %collective-permute-done.refs_0_ = f32[5,32,128]{2,1,0:T(8,128)S(1)} collective-permute-done((f32[5,32,128]{2,1,0:T(8,128)S(1)}, f32[5,32,128]{2,1,0:T(8,128)S(1)}, u32[]{:S(2)}, u32[]{:S(2)}) %collective-permute-start) | collective-permute-done | bytes 81952 | tf_op jit(solution)/shard_map/ppermute | solution.py:526
  13.4 0.1 collective-permute-start.7
  13.5 2.7 %collective-permute-start.3 = (f32[5,32,128]{2,1,0:T(8,128)S(1)}, f32[5,32,128]{2,1,0:T(8,128)S(1)}, u32[]{:S(2)}, u32[]{:S(2)}) collective-permute-start(f32[5,32,128]{2,1,0:T(8,128)S(1)} %get-tuple-element.53), channel_id=1, source_target_pairs={{0,7},{1,0},{2,1},{3,2},{4,3},{5,4},{6,5},{7,6},{8,15},{9,8},{10,9... | collective-permute-start | bytes 245768 | tf_op jit(solution)/shard_map/ppermute | solution.py:526
  16.2 0.0 collective-permute-done.4.refs_0_
  16.2 0.0 collective-permute-done.5.refs_1_
  16.2 0.0 collective-permute-done.6.refs_2_
  16.2 0.0 collective-permute-done.7.refs_3_
  16.2 1.1 %collective-permute-start.8 = (f32[88,128]{1,0:T(8,128)S(1)}, f32[88,128]{1,0:T(8,128)S(1)}, u32[]{:S(2)}, u32[]{:S(2)}) collective-permute-start(f32[88,128]{1,0:T(8,128)S(1)} %get-tuple-element.60), channel_id=1, source_target_pairs={{0,9},{1,8},{2,11},{3,10},{4,13},{5,12},{6,15},{7,14},{8,1},{9,0},... | collective-permute-start | bytes 135176 | tf_op jit(solution)/shard_map/ppermute | solution.py:537
  17.4 0.1 collective-permute-start.9
  17.5 0.8 %collective-permute-done.3.x_high = f32[5,32,128]{2,1,0:T(8,128)S(1)} collective-permute-done((f32[5,32,128]{2,1,0:T(8,128)S(1)}, f32[5,32,128]{2,1,0:T(8,128)S(1)}, u32[]{:S(2)}, u32[]{:S(2)}) %collective-permute-start.3) | collective-permute-done | bytes 81952 | tf_op jit(solution)/shard_map/ppermute | solution.py:526
  18.3 1.1 %change.1 = (f32[5,256,128]{2,1,0:T(8,128)S(1)}, f32[5,256,128]{2,1,0:T(8,128)S(1)}) custom-call(f32[256,128]{1,0:T(8,128)S(1)} %get-tuple-element.33.r_ref, f32[768,128]{1,0:T(8,128)S(1)} %get-tuple-element.34.v_ref, f32[256,128]{1,0:T(8,128)S(1)} %get-tuple-element.35.p_ref, f32[5,32,128]{2,1,0:T(8,128)S(1)} %get-tuple-element.52.x_low, ...), custom_call_target="tpu_custom_call" | custom-call | flops 9830400000 | bytes 1048576 | tf_op jit(solution)/shard_map/change/pallas_call | solution.py:624
  19.4 0.7 %collective-permute-done.8.other_ref = f32[88,128]{1,0:T(8,128)S(1)} collective-permute-done((f32[88,128]{1,0:T(8,128)S(1)}, f32[88,128]{1,0:T(8,128)S(1)}, u32[]{:S(2)}, u32[]{:S(2)}) %collective-permute-start.8) | collective-permute-done | bytes 45088 | tf_op jit(solution)/shard_map/ppermute | solution.py:537
  20.2 0.0 collective-permute-done.9.own_ref
  20.2 1.7 %final.1 = (f32[5,256,128]{2,1,0:T(8,128)}, f32[32,64]{1,0:T(8,128)}) custom-call(f32[5,256,128]{2,1,0:T(8,128)S(1)} %get-tuple-element.54.state_ref, f32[5,256,128]{2,1,0:T(8,128)S(1)} %get-tuple-element.55.change_ref, f32[88,128]{1,0:T(8,128)S(1)} %collective-permute-done.8.other_ref, f32[88,128]{1,0:T(8,128)S(1)} %collective-permute-done.9.own_ref, ...), custom_call_target="tpu_custom_call" | custom-call | flops 3276800 | bytes 1048576 | tf_op jit(solution)/shard_map/final/pallas_call | solution.py:630
  (3 shorter events, 0.0 us)
Async XLA Ops:
  1.9 1.4 %collective-permute-start.1 = (f32[6,8,128]{2,1,0:T(8,128)S(1)}, f32[6,8,128]{2,1,0:T(8,128)S(1)}, u32[]{:S(2)}, u32[]{:S(2)}) collective-permute-start(f32[6,8,128]{2,1,0:T(8,128)S(1)} %get-tuple-element.40), channel_id=1, source_target_pairs={{0,8},{8,0},{16,24},{24,16},{1,9},{9,1},{17,25},{25,17},{2,10},{10... | collective-permute-start | bytes 73736 | tf_op jit(solution)/shard_map/ppermute | solution.py:530
  3.2 4.4 %collective-permute-start.2 = (f32[6,8,128]{2,1,0:T(8,128)S(1)}, f32[6,8,128]{2,1,0:T(8,128)S(1)}, u32[]{:S(2)}, u32[]{:S(2)}) collective-permute-start(f32[6,8,128]{2,1,0:T(8,128)S(1)} %get-tuple-element.44), channel_id=1, source_target_pairs={{0,24},{8,16},{16,8},{24,0},{1,25},{9,17},{17,9},{25,1},{2,26},{10... | collective-permute-start | bytes 73736 | tf_op jit(solution)/shard_map/ppermute | solution.py:542
  5.8 7.5 %collective-permute-start = (f32[5,32,128]{2,1,0:T(8,128)S(1)}, f32[5,32,128]{2,1,0:T(8,128)S(1)}, u32[]{:S(2)}, u32[]{:S(2)}) collective-permute-start(f32[5,32,128]{2,1,0:T(8,128)S(1)} %get-tuple-element.36), channel_id=1, source_target_pairs={{0,1},{1,2},{2,3},{3,4},{4,5},{5,6},{6,7},{7,0},{8,9},{9,10},{10,1... | collective-permute-start | bytes 245768 | tf_op jit(solution)/shard_map/ppermute | solution.py:526
  8.0 8.2 %collective-permute-start.4 = (f32[48,128]{1,0:T(8,128)S(1)}, f32[48,128]{1,0:T(8,128)S(1)}, u32[]{:S(2)}, u32[]{:S(2)}) collective-permute-start(f32[48,128]{1,0:T(8,128)S(1)} %get-tuple-element.56), channel_id=1, source_target_pairs={{0,12},{1,13},{2,14},{3,15},{4,8},{5,9},{6,10},{7,11},{8,4},{9,5},... | collective-permute-start | bytes 73736 | tf_op jit(solution)/shard_map/ppermute | solution.py:537
  10.6 5.6 %collective-permute-start.5 = (f32[48,128]{1,0:T(8,128)S(1)}, f32[48,128]{1,0:T(8,128)S(1)}, u32[]{:S(2)}, u32[]{:S(2)}) collective-permute-start(f32[48,128]{1,0:T(8,128)S(1)} %get-tuple-element.57), channel_id=1, source_target_pairs={{0,14},{1,15},{2,12},{3,13},{4,10},{5,11},{6,8},{7,9},{8,6},{9,7},... | collective-permute-start | bytes 73736 | tf_op jit(solution)/shard_map/ppermute | solution.py:537
  11.9 4.3 %collective-permute-start.6 = (f32[48,128]{1,0:T(8,128)S(1)}, f32[48,128]{1,0:T(8,128)S(1)}, u32[]{:S(2)}, u32[]{:S(2)}) collective-permute-start(f32[48,128]{1,0:T(8,128)S(1)} %get-tuple-element.58), channel_id=1, source_target_pairs={{0,10},{1,11},{2,8},{3,9},{4,14},{5,15},{6,12},{7,13},{8,2},{9,3},... | collective-permute-start | bytes 73736 | tf_op jit(solution)/shard_map/ppermute | solution.py:537
  13.4 2.8 %collective-permute-start.7 = (f32[48,128]{1,0:T(8,128)S(1)}, f32[48,128]{1,0:T(8,128)S(1)}, u32[]{:S(2)}, u32[]{:S(2)}) collective-permute-start(f32[48,128]{1,0:T(8,128)S(1)} %get-tuple-element.59), channel_id=1, source_target_pairs={{0,8},{1,9},{2,10},{3,11},{4,12},{5,13},{6,14},{7,15},{8,0},{9,1},... | collective-permute-start | bytes 73736 | tf_op jit(solution)/shard_map/ppermute | solution.py:537
  13.5 4.8 %collective-permute-start.3 = (f32[5,32,128]{2,1,0:T(8,128)S(1)}, f32[5,32,128]{2,1,0:T(8,128)S(1)}, u32[]{:S(2)}, u32[]{:S(2)}) collective-permute-start(f32[5,32,128]{2,1,0:T(8,128)S(1)} %get-tuple-element.53), channel_id=1, source_target_pairs={{0,7},{1,0},{2,1},{3,2},{4,3},{5,4},{6,5},{7,6},{8,15},{9,8},{10,9... | collective-permute-start | bytes 245768 | tf_op jit(solution)/shard_map/ppermute | solution.py:526
  16.2 3.9 %collective-permute-start.8 = (f32[88,128]{1,0:T(8,128)S(1)}, f32[88,128]{1,0:T(8,128)S(1)}, u32[]{:S(2)}, u32[]{:S(2)}) collective-permute-start(f32[88,128]{1,0:T(8,128)S(1)} %get-tuple-element.60), channel_id=1, source_target_pairs={{0,9},{1,8},{2,11},{3,10},{4,13},{5,12},{6,15},{7,14},{8,1},{9,0},... | collective-permute-start | bytes 135176 | tf_op jit(solution)/shard_map/ppermute | solution.py:537
  17.4 2.8 %collective-permute-start.9 = (f32[88,128]{1,0:T(8,128)S(1)}, f32[88,128]{1,0:T(8,128)S(1)}, u32[]{:S(2)}, u32[]{:S(2)}) collective-permute-start(f32[88,128]{1,0:T(8,128)S(1)} %get-tuple-element.61), channel_id=1, source_target_pairs={{0,8},{1,9},{2,10},{3,11},{4,12},{5,13},{6,14},{7,15},{8,0},{9,1},... | collective-permute-start | bytes 135176 | tf_op jit(solution)/shard_map/ppermute | solution.py:537
